TPU v7x, 32 devices: a whole 2x2x4 slice. The times are simulated.
32 devices in a mesh: dp: 16 (over z, x, core), tensor: 2 (over y).
Axes of the slice: x: 2, y: 2, z: 4, core: 2. Of those that a mesh axis runs over, the one named last changes fastest.
Arguments:
- tokens: bfloat16 [16384, 896], P(('dp', 'tensor')), may hold values from -6 to 6
- cotangent: bfloat16 [16384, 896], P(('dp', 'tensor')), may hold values from -6 to 6
- seq_lengths: int32 [64], replicated, may hold values from 1 to 682, as said below
- seq_place: int32 [64], replicated, may hold values from 0 to 63, as said below
- norm1_gain: float32 [896], replicated, may hold values from 0.5 to 1.5
- qkv_weight: bfloat16 [896, 1152], P(None, 'tensor'), may hold values from -0.25 to 0.25
- qkv_bias: float32 [1152], P('tensor'), may hold values from -3 to 3
- out_weight: bfloat16 [896, 896], P('tensor'), may hold values from -0.75 to 0.75
- norm2_gain: float32 [896], replicated, may hold values from 0.5 to 1.5
- gate_weight: bfloat16 [896, 4864], P(None, 'tensor'), may hold values from -0.1875 to 0.1875
- up_weight: bfloat16 [896, 4864], P(None, 'tensor'), may hold values from -0.1875 to 0.1875
- down_weight: bfloat16 [4864, 896], P('tensor'), may hold values from -0.125 to 0.125
Outputs:
- block_out: bfloat16 [16384, 896], P(('dp', 'tensor'))
- tokens_grad: float32 [16384, 896], P(('dp', 'tensor'))
- norm1_gain_grad: float32 [896], P('dp')
- qkv_weight_grad: float32 [896, 1152], P('dp', 'tensor')
- qkv_bias_grad: float32 [1152], P('tensor')
- out_weight_grad: float32 [896, 896], P('tensor', 'dp')
- norm2_gain_grad: float32 [896], P('dp')
- gate_weight_grad: float32 [896, 4864], P('dp', 'tensor')
- up_weight_grad: float32 [896, 4864], P('dp', 'tensor')
- down_weight_grad: float32 [4864, 896], P('tensor', 'dp')
Inputs may be any that keep to these rules, and one draw needn't show every extreme that they name: `seq_lengths`: the lengths of the 4 sequences of one data index add up to at most 1024; some sequence has exactly 682 tokens. A permutation: sequence s lies on data index seq_place[s] // 4 with rank seq_place[s] % 4 there, so each data index holds 4 sequences.
All inputs are finite; a program needn't handle non-finite values.
Results may differ from a plain program's by a relative error of at most 0.014.
The roundings to bfloat16 on the way count: a program that leaves them out, or rounds other values in their place, can miss the bound.
Values may be sent and summed in bfloat16 or wider, within the bound.
A program may use at most 192 MiB of HBM per device.

v0:
```python
import jax
import jax.numpy as jnp
from jax import lax
from jax.sharding import PartitionSpec as P

QUERY_HEADS = 14
KEY_VALUE_HEADS = 2
HEAD_WIDTH = 64
SEQ_DEV = 4
QB = 512


norm_eps = 1e-06
rope_base = 1000000.0
masked_score = -1e30


def seq_layout(lengths, placed, group_id, number_of_slots):
    target = group_id * SEQ_DEV + jnp.arange(SEQ_DEV, dtype=jnp.int32)
    owned = placed[None, :] == target[:, None]
    counted = jnp.sum(jnp.where(owned, lengths[None, :], 0), axis=1)
    seq_ends = jnp.cumsum(counted)
    seq_starts = seq_ends - counted
    slot_ids = jnp.arange(number_of_slots, dtype=jnp.int32)
    inside = (slot_ids[:, None] >= seq_starts[None, :]) & (slot_ids[:, None] < seq_ends[None, :])
    ranks = jnp.arange(SEQ_DEV, dtype=jnp.int32)
    segment = jnp.sum(jnp.where(inside, ranks[None, :], 0), axis=1) + jnp.where(
        jnp.any(inside, axis=1), 0, SEQ_DEV
    )
    position = slot_ids - jnp.sum(jnp.where(inside, seq_starts[None, :], 0), axis=1)
    return (segment, position)


def rope_tables(position):
    half_dim = HEAD_WIDTH // 2
    inverse = jnp.power(rope_base, -2.0 * jnp.arange(half_dim, dtype=jnp.float32) / HEAD_WIDTH)
    angles = position.astype(jnp.float32)[:, None] * inverse[None, :]
    return (jnp.cos(angles), jnp.sin(angles))


def rotate(vectors, cosine, sine_table):
    half_dim = vectors.shape[-1] // 2
    first_half = vectors[..., :half_dim]
    second_half = vectors[..., half_dim:]
    return jnp.concatenate(
        [
            first_half * cosine - second_half * sine_table,
            second_half * cosine + first_half * sine_table,
        ],
        axis=-1,
    )


def rotate_back(vectors, cosine, sine_table):
    half_dim = vectors.shape[-1] // 2
    first_half = vectors[..., :half_dim]
    second_half = vectors[..., half_dim:]
    return jnp.concatenate(
        [
            first_half * cosine + second_half * sine_table,
            second_half * cosine - first_half * sine_table,
        ],
        axis=-1,
    )


def allowed_keys(segment, row_start, row_end):
    query_ids = jnp.arange(row_start, row_end, dtype=jnp.int32)
    key_ids = jnp.arange(0, row_end, dtype=jnp.int32)
    query_seg = segment[row_start:row_end]
    same = query_seg[:, None] == segment[None, :row_end]
    causal = key_ids[None, :] <= query_ids[:, None]
    real_row = (query_seg[:, None] < SEQ_DEV) | (key_ids[None, :] == query_ids[:, None])
    return same & causal & real_row


def rms_forward(token_rows, gain):
    rms_scale = lax.rsqrt(jnp.mean(token_rows * token_rows, axis=-1, keepdims=True) + norm_eps)
    return (rms_scale, token_rows * rms_scale * gain)


def rms_backward(token_rows, rms_scale, gain, grad_rows):
    weighted = gain * grad_rows
    inner = jnp.mean(weighted * token_rows, axis=-1, keepdims=True)
    row_grad = rms_scale * weighted - token_rows * (rms_scale * rms_scale * rms_scale) * inner
    gain_grad = jnp.sum(grad_rows * token_rows * rms_scale, axis=0)
    return (row_grad, gain_grad)


def contract_rows(left, right):
    return lax.dot_general(
        left, right, (((0,), (0,)), ((), ())), preferred_element_type=jnp.float32
    )


def times_transpose(left, right):
    return lax.dot_general(
        left, right, (((1,), (1,)), ((), ())), preferred_element_type=jnp.float32
    )


def shards(
    tokens,
    cotangent,
    seq_lengths,
    seq_place,
    norm1_gain,
    qkv_weight,
    qkv_bias,
    out_weight,
    norm2_gain,
    gate_weight,
    up_weight,
    down_weight,
):
    local_rows = tokens.shape[0]
    group_rows = local_rows * lax.axis_size("tensor")
    segment, position = seq_layout(seq_lengths, seq_place, lax.axis_index("dp"), group_rows)
    query_columns = out_weight.shape[0]
    key_columns = (qkv_weight.shape[1] - query_columns) // 2
    kv_local = key_columns // HEAD_WIDTH
    heads_per_group = QUERY_HEADS // KEY_VALUE_HEADS
    score_scale = HEAD_WIDTH ** (-0.5)
    block_count = group_rows // QB
    token_vals = tokens.astype(jnp.float32)
    rms_one, normed_one = rms_forward(token_vals, norm1_gain)
    normed_one = lax.all_gather(normed_one.astype(jnp.bfloat16), "tensor", axis=0, tiled=True)
    projected = jnp.dot(normed_one, qkv_weight, preferred_element_type=jnp.float32) + qkv_bias
    query_rows = projected[:, :query_columns].reshape(
        group_rows, kv_local, heads_per_group, HEAD_WIDTH
    )
    key_matrix = projected[:, query_columns : query_columns + key_columns].reshape(
        group_rows, kv_local, HEAD_WIDTH
    )
    value_matrix = (
        projected[:, query_columns + key_columns :]
        .reshape(group_rows, kv_local, HEAD_WIDTH)
        .astype(jnp.bfloat16)
    )
    cosine, sine_table = rope_tables(position)
    queries_r = rotate(query_rows, cosine[:, None, None, :], sine_table[:, None, None, :]).astype(
        jnp.bfloat16
    )
    keys_r = rotate(key_matrix, cosine[:, None, :], sine_table[:, None, :]).astype(jnp.bfloat16)
    key_masks = []
    log_totals = []
    contexts = []
    for block_id in range(block_count):
        row_start = block_id * QB
        row_end = row_start + QB
        key_mask = allowed_keys(segment, row_start, row_end)
        scores = (
            jnp.einsum(
                "qjgd,kjd->jgqk",
                queries_r[row_start:row_end],
                keys_r[:row_end],
                preferred_element_type=jnp.float32,
            )
            * score_scale
        )
        scores = jnp.where(key_mask[None, None], scores, masked_score)
        row_max = jnp.max(scores, axis=-1, keepdims=True)
        expo = jnp.exp(scores - row_max)
        row_total = jnp.sum(expo, axis=-1, keepdims=True)
        attn_probs = (expo / row_total).astype(jnp.bfloat16)
        key_masks.append(key_mask)
        log_totals.append(row_max + jnp.log(row_total))
        contexts.append(
            jnp.einsum(
                "jgqk,kjd->qjgd",
                attn_probs,
                value_matrix[:row_end],
                preferred_element_type=jnp.float32,
            )
        )
    context = (
        jnp.concatenate(contexts, axis=0).reshape(group_rows, query_columns).astype(jnp.bfloat16)
    )
    hidden_one = token_vals + lax.psum_scatter(
        jnp.dot(context, out_weight, preferred_element_type=jnp.float32),
        "tensor",
        scatter_dimension=0,
        tiled=True,
    )
    rms_two, normed_two = rms_forward(hidden_one, norm2_gain)
    normed_two = lax.all_gather(normed_two.astype(jnp.bfloat16), "tensor", axis=0, tiled=True)
    gate_pre = jnp.dot(normed_two, gate_weight, preferred_element_type=jnp.float32)
    up_pre = jnp.dot(normed_two, up_weight, preferred_element_type=jnp.float32)
    activated = jax.nn.silu(gate_pre)
    mixed = (activated * up_pre).astype(jnp.bfloat16)
    block_result = (
        hidden_one
        + lax.psum_scatter(
            jnp.dot(mixed, down_weight, preferred_element_type=jnp.float32).astype(jnp.bfloat16),
            "tensor",
            scatter_dimension=0,
            tiled=True,
        ).astype(jnp.float32)
    ).astype(jnp.bfloat16)
    cot_group = lax.all_gather(cotangent, "tensor", axis=0, tiled=True)
    down_grad = contract_rows(mixed, cot_group)
    d_mixed = times_transpose(cot_group, down_weight)
    sigmoid_gate = jax.nn.sigmoid(gate_pre)
    d_gate = (d_mixed * up_pre * sigmoid_gate * (1.0 + gate_pre * (1.0 - sigmoid_gate))).astype(
        jnp.bfloat16
    )
    d_up = (d_mixed * activated).astype(jnp.bfloat16)
    gate_grad = contract_rows(normed_two, d_gate)
    up_grad = contract_rows(normed_two, d_up)
    gate_part = times_transpose(d_gate, gate_weight)
    d_normed_two = lax.psum_scatter(
        gate_part + times_transpose(d_up, up_weight), "tensor", scatter_dimension=0, tiled=True
    )
    d_hidden_norm, gain_two_grad = rms_backward(hidden_one, rms_two, norm2_gain, d_normed_two)
    d_hidden = cotangent.astype(jnp.float32) + d_hidden_norm
    d_resid = lax.all_gather(d_hidden.astype(jnp.bfloat16), "tensor", axis=0, tiled=True)
    out_grad = contract_rows(context, d_resid)
    d_context = (
        times_transpose(d_resid, out_weight)
        .astype(jnp.bfloat16)
        .reshape(group_rows, kv_local, heads_per_group, HEAD_WIDTH)
    )
    d_query_blocks = []
    d_keys = jnp.zeros((group_rows, kv_local, HEAD_WIDTH), jnp.float32)
    d_values = jnp.zeros((group_rows, kv_local, HEAD_WIDTH), jnp.float32)
    for block_id in range(block_count):
        row_start = block_id * QB
        row_end = row_start + QB
        scores = (
            jnp.einsum(
                "qjgd,kjd->jgqk",
                queries_r[row_start:row_end],
                keys_r[:row_end],
                preferred_element_type=jnp.float32,
            )
            * score_scale
        )
        scores = jnp.where(key_masks[block_id][None, None], scores, masked_score)
        probs_full = jnp.exp(scores - log_totals[block_id])
        attn_probs = probs_full.astype(jnp.bfloat16)
        d_block = d_context[row_start:row_end]
        d_probs = jnp.einsum(
            "qjgd,kjd->jgqk", d_block, value_matrix[:row_end], preferred_element_type=jnp.float32
        )
        inner = jnp.sum(probs_full * d_probs, axis=-1, keepdims=True)
        d_scores = (probs_full * (d_probs - inner)).astype(jnp.bfloat16)
        d_query_blocks.append(
            jnp.einsum(
                "jgqk,kjd->qjgd", d_scores, keys_r[:row_end], preferred_element_type=jnp.float32
            )
            * score_scale
        )
        d_keys = d_keys.at[:row_end].add(
            jnp.einsum(
                "jgqk,qjgd->kjd",
                d_scores,
                queries_r[row_start:row_end],
                preferred_element_type=jnp.float32,
            )
            * score_scale
        )
        d_values = d_values.at[:row_end].add(
            jnp.einsum("jgqk,qjgd->kjd", attn_probs, d_block, preferred_element_type=jnp.float32)
        )
    d_queries = rotate_back(
        jnp.concatenate(d_query_blocks, axis=0),
        cosine[:, None, None, :],
        sine_table[:, None, None, :],
    )
    d_keys = rotate_back(d_keys, cosine[:, None, :], sine_table[:, None, :])
    d_proj = jnp.concatenate(
        [
            d_queries.reshape(group_rows, query_columns),
            d_keys.reshape(group_rows, key_columns),
            d_values.reshape(group_rows, key_columns),
        ],
        axis=1,
    ).astype(jnp.bfloat16)
    qkv_grad = contract_rows(normed_one, d_proj)
    bias_grad = jnp.sum(d_proj, axis=0, dtype=jnp.float32)
    d_normed_one = lax.psum_scatter(
        times_transpose(d_proj, qkv_weight).astype(jnp.bfloat16),
        "tensor",
        scatter_dimension=0,
        tiled=True,
    ).astype(jnp.float32)
    d_token_norm, gain_one_grad = rms_backward(token_vals, rms_one, norm1_gain, d_normed_one)
    tokens_grad = d_hidden + d_token_norm
    qkv_grad, out_grad, gate_grad, up_grad, down_grad, gain_one_grad, gain_two_grad = (
        lax.psum_scatter(qkv_grad, "dp", scatter_dimension=0, tiled=True),
        lax.psum_scatter(out_grad, "dp", scatter_dimension=1, tiled=True),
        lax.psum_scatter(gate_grad, "dp", scatter_dimension=0, tiled=True),
        lax.psum_scatter(up_grad, "dp", scatter_dimension=0, tiled=True),
        lax.psum_scatter(down_grad, "dp", scatter_dimension=1, tiled=True),
        lax.psum_scatter(gain_one_grad, "dp", scatter_dimension=0, tiled=True),
        lax.psum_scatter(gain_two_grad, "dp", scatter_dimension=0, tiled=True),
    )
    bias_grad = lax.psum(bias_grad, "dp")
    gain_one_grad, gain_two_grad = lax.psum((gain_one_grad, gain_two_grad), "tensor")
    return (
        block_result,
        tokens_grad,
        gain_one_grad,
        qkv_grad,
        bias_grad,
        out_grad,
        gain_two_grad,
        gate_grad,
        up_grad,
        down_grad,
    )


def solution(mesh):
    in_specs = (
        P(("dp", "tensor"), None),
        P(("dp", "tensor"), None),
        P(),
        P(),
        P(),
        P(None, "tensor"),
        P("tensor"),
        P("tensor", None),
        P(),
        P(None, "tensor"),
        P(None, "tensor"),
        P("tensor", None),
    )
    out_specs = (
        P(("dp", "tensor"), None),
        P(("dp", "tensor"), None),
        P("dp"),
        P("dp", "tensor"),
        P("tensor"),
        P("tensor", "dp"),
        P("dp"),
        P("dp", "tensor"),
        P("dp", "tensor"),
        P("tensor", "dp"),
    )
    return jax.shard_map(shards, mesh=mesh, in_specs=in_specs, out_specs=out_specs, check_vma=False)
```

profile of v0, /device:TPU:0, one launch (start us, length us, event | category | flops | bytes accessed | tf_op | source)
XLA Modules:
  0.0 909.8 jit_solution(15089683599481920513)
XLA Ops:
  7.3 1.5 fusion.31
  8.8 0.6 multiply_multiply_fusion
  9.4 0.6 copy-done.18
  10.0 2.4 fusion.33
  13.4 0.5 multiply_cosine_fusion
  13.9 0.7 fusion.27
  14.7 30.7 %all-gather.5.cloned.1.call-done = bf16[1024,896]{1,0:T(8,128)(2,1)} async-done(((bf16[512,896]{1,0:T(8,128)(2,1)}), bf16[1024,896]{1,0:T(8,128)(2,1)}) %all-gather.5.cloned.1.call-update) | async-done | bytes 1835024 | tf_op jit(solution)/shard_map/all_gather | solution.py:127
  45.4 2.9 fusion.116
  48.6 0.6 fusion.88
  49.5 1.3 fusion.117
  50.8 1.0 fusion.16
  51.8 1.9 copy-done.1
  53.7 1.4 fusion.49
  55.1 6.7 fusion.115
  61.8 7.2 fusion.3
  69.0 6.7 fusion.46
  75.8 0.9 copy-done.10
  76.7 3.1 fusion.118
  79.9 49.2 %reduce-scatter.18.cloned.1.call-done = f32[512,896]{1,0:T(8,128)} async-done(((f32[1024,896]{1,0:T(8,128)}), f32[512,896]{1,0:T(8,128)}) %reduce-scatter.18.cloned.1.call-update) | async-done | bytes 1835024 | tf_op jit(solution)/shard_map/reduce_scatter | solution.py:179
  129.2 2.0 multiply_reduce_fusion.2
  131.2 1.1 multiply_convert_fusion.3
  132.4 0.5 all-gather.9.cloned.1.call-update
  133.0 29.7 %all-gather.7.cloned.1.call-done = bf16[1024,896]{1,0:T(8,128)(2,1)} async-done(((bf16[512,896]{1,0:T(8,128)(2,1)}), bf16[1024,896]{1,0:T(8,128)(2,1)}) %all-gather.7.cloned.1.call-update) | async-done | bytes 1835024 | tf_op jit(solution)/shard_map/all_gather | solution.py:186
  162.7 10.7 %fusion.120 = f32[1024,2432]{1,0:T(8,128)} fusion(bf16[1024,896]{1,0:T(8,128)(2,1)} %all-gather.7.cloned.1.call-done, bf16[896,2432]{1,0:T(8,128)(2,1)} %param.34), kind=kOutput, calls=%fused_computation.181 | convolution fusion | flops 4462739456 | bytes 16154624 | tf_op jit(solution)/shard_map/dot_general | solution.py:188
  173.5 10.1 %fusion.119 = f32[1024,2432]{1,0:T(8,128)} fusion(bf16[1024,896]{1,0:T(8,128)(2,1)S(1)} %copy-done.26, bf16[896,2432]{1,0:T(8,128)(2,1)} %param.33), kind=kOutput, calls=%fused_computation.180 | convolution fusion | flops 4462739456 | bytes 16154624 | tf_op jit(solution)/shard_map/dot_general | solution.py:187
  183.5 10.9 %all-gather.9.cloned.1.call-done = bf16[1024,896]{1,0:T(8,128)(2,1)} async-done(((bf16[512,896]{1,0:T(8,128)(2,1)}), bf16[1024,896]{1,0:T(8,128)(2,1)}) %all-gather.9.cloned.1.call-update) | async-done | bytes 1835024 | tf_op jit(solution)/shard_map/all_gather | solution.py:200
  194.4 17.5 %multiply_convert_fusion = (bf16[1024,2432]{1,0:T(8,128)(2,1)}, bf16[1024,2432]{1,0:T(8,128)(2,1)}, bf16[1024,2432]{1,0:T(8,128)(2,1)}) fusion(f32[1024,2432]{1,0:T(8,128)} %fusion.119, f32[1024,2432]{1,0:T(8,128)} %fusion.120, bf16[1024,896]{1,0:T(8,128)(2,1)} %all-gather.9.cloned.1.call-done, bf16[2432,896]{1,0:T(8,128)(2,1)} %param.35), kind=kOutput, calls=%fused_computation.11 | convolution fusion | flops 4500094976 | bytes 41058304 | tf_op jit(solution)/shard_map/dot_general | solution.py:97
  211.9 8.9 fusion.121
  220.8 9.6 %convolution_add_fusion = f32[1024,896]{1,0:T(8,128)} fusion(f32[1024,896]{1,0:T(8,128)S(1)} %fusion.121, bf16[1024,2432]{1,0:T(8,128)(2,1)S(1)} %copy-done.30, bf16[896,2432]{1,0:T(8,128)(2,1)} %param.34), kind=kOutput, calls=%fused_computation.70 | convolution fusion | flops 4463656960 | bytes 16678912 | tf_op jit(solution)/shard_map/dot_general | solution.py:97
  230.5 10.0 %convolution_convert_fusion.1 = bf16[1024,896]{1,0:T(8,128)(2,1)} fusion(bf16[1024,2432]{1,0:T(8,128)(2,1)} %get-tuple-element.91, bf16[2432,896]{1,0:T(8,128)(2,1)} %param.35), kind=kOutput, calls=%fused_computation.72 | convolution fusion | flops 4463656960 | bytes 11173888 | tf_op jit(solution)/shard_map/dot_general | solution.py:194
  240.5 39.1 %reduce-scatter.22.cloned.1.call-done = f32[512,896]{1,0:T(8,128)} async-done(((f32[1024,896]{1,0:T(8,128)}), f32[512,896]{1,0:T(8,128)}) %reduce-scatter.22.cloned.1.call-update) | async-done | bytes 1835024 | tf_op jit(solution)/shard_map/reduce_scatter | solution.py:211
  279.7 2.0 multiply_reduce_fusion
  281.7 29.7 %reduce-scatter.20.cloned.1.call-done = bf16[512,896]{1,0:T(8,128)(2,1)} async-done(((bf16[1024,896]{1,0:T(8,128)(2,1)}), bf16[512,896]{1,0:T(8,128)(2,1)}) %reduce-scatter.20.cloned.1.call-update) | async-done | bytes 917520 | tf_op jit(solution)/shard_map/reduce_scatter | solution.py:193
  311.3 4.5 fusion.112
  315.9 30.2 %all-gather.11.cloned.1.call-done = bf16[1024,896]{1,0:T(8,128)(2,1)} async-done(((bf16[512,896]{1,0:T(8,128)(2,1)}), bf16[1024,896]{1,0:T(8,128)(2,1)}) %all-gather.11.cloned.1.call-update) | async-done | bytes 1835024 | tf_op jit(solution)/shard_map/all_gather | solution.py:216
  346.2 3.0 convolution_convert_fusion.2
  349.2 0.8 fusion.113
  350.0 4.6 fusion.67
  354.6 5.2 fusion.10
  359.9 9.4 %fusion.21 = bf16[7,512,512]{1,2,0:T(8,128)(2,1)} fusion(f32[512,512,7]{1,0,2:T(8,128)} %get-tuple-element.122, f32[1,7,512,512]{2,3,1,0:T(8,128)} %copy-done.1, f32[7,512]{1,0:T(8,128)S(1)} %get-tuple-element.121, f32[7,512]{1,0:T(8,128)S(1)} %log_add_fusion.1), kind=kLoop, calls=%fused_computation.41 | loop fusion | flops 7340032 | bytes 18378752 | tf_op jit(solution)/shard_map/reshape.154
  369.3 3.4 fusion.71
  372.7 2.8 fusion.39
  375.5 7.6 fusion
  383.2 2.4 fusion.64
  385.5 7.1 fusion.9
  392.7 1.4 fusion.38
  394.1 2.3 fusion.57
  396.5 0.6 fusion.92
  397.4 3.0 convolution_convert_fusion
  400.5 4.0 fusion.122
  404.6 4.5 fusion.111
  409.4 11.3 %fusion.125 = f32[2432,896]{0,1:T(8,128)} fusion(bf16[1024,2432]{1,0:T(8,128)(2,1)} %get-tuple-element.91, bf16[1024,896]{1,0:T(8,128)(2,1)} %all-gather.9.cloned.1.call-done), kind=kOutput, calls=%fused_computation.186 | convolution fusion | flops 4462739456 | bytes 15532032 | tf_op jit(solution)/shard_map/dot_general | solution.py:91
  420.8 11.3 %fusion.124 = f32[896,2432]{1,0:T(8,128)} fusion(bf16[1024,896]{1,0:T(8,128)(2,1)} %all-gather.7.cloned.1.call-done, bf16[1024,2432]{1,0:T(8,128)(2,1)} %get-tuple-element.89), kind=kOutput, calls=%fused_computation.185 | convolution fusion | flops 4462739456 | bytes 15532032 | tf_op jit(solution)/shard_map/dot_general | solution.py:91
  432.5 11.4 %fusion.123 = f32[896,2432]{1,0:T(8,128)} fusion(bf16[1024,896]{1,0:T(8,128)(2,1)} %all-gather.7.cloned.1.call-done, bf16[1024,2432]{1,0:T(8,128)(2,1)} %get-tuple-element.90), kind=kOutput, calls=%fused_computation.184 | convolution fusion | flops 4462739456 | bytes 15532032 | tf_op jit(solution)/shard_map/dot_general | solution.py:91
  443.9 0.6 copy-done.29
  444.5 0.6 dynamic-slice.26
  446.0 2.0 fusion.37
  448.1 61.5 %all-reduce.8 = (f32[896]{0:T(1024)S(1)}, f32[576]{0:T(1024)}, f32[896]{0:T(1024)S(1)}) all-reduce(f32[896]{0:T(1024)S(1)} %get-tuple-element.76, f32[576]{0:T(1024)S(1)} %convert_reduce_fusion, f32[896]{0:T(1024)S(1)} %get-tuple-element.74), channel_id=6, replica_groups=mesh['dp'=16,'tensor'=2] {'dp'}, use_global_device_ids=true, to_apply=%region_20.21.clone | all-reduce | flops 2368 | bytes 18944
  509.7 5.4 all-reduce.9
  515.1 3.5 fusion.30
  518.7 42.7 %reduce-scatter.28.cloned.1.call-done = f32[56,576]{1,0:T(8,128)} async-done(((f32[896,576]{1,0:T(8,128)}), f32[56,576]{1,0:T(8,128)}) %reduce-scatter.28.cloned.1.call-update) | async-done | bytes 129040
  561.3 113.9 %reduce-scatter.34.cloned.1.call-done = f32[2432,56]{0,1:T(8,128)} async-done(((f32[2432,896]{0,1:T(8,128)}), f32[2432,56]{0,1:T(8,128)}) %reduce-scatter.34.cloned.1.call-update) | async-done | bytes 544784
  675.2 113.8 %reduce-scatter.32.cloned.1.call-done = f32[56,2432]{1,0:T(8,128)} async-done(((f32[896,2432]{1,0:T(8,128)}), f32[56,2432]{1,0:T(8,128)}) %reduce-scatter.32.cloned.1.call-update) | async-done | bytes 544784
  789.0 114.0 %reduce-scatter.30.cloned.1.call-done = f32[56,2432]{1,0:T(8,128)} async-done(((f32[896,2432]{1,0:T(8,128)}), f32[56,2432]{1,0:T(8,128)}) %reduce-scatter.30.cloned.1.call-update) | async-done | bytes 544784
  (126 shorter events, 3.6 us)
Async XLA Ops:
  7.2 38.2 %copy-start = (bf16[896,576]{0,1:T(8,128)(2,1)S(1)}, bf16[896,576]{0,1:T(8,128)(2,1)}, u32[]{:S(2)}) copy-start(bf16[896,576]{0,1:T(8,128)(2,1)} %param.29) | copy-start | bytes 3096580
  7.2 5.3 copy-start.25
  7.2 5.3 copy-start.24
  7.2 38.2 %copy-start.28 = (f32[576]{0:T(1024)S(1)}, f32[576]{0:T(1024)}, u32[]{:S(2)}) copy-start(f32[576]{0:T(1024)} %param.30) | copy-start | bytes 6916
  7.2 38.2 %all-gather.5.cloned.1.call-start = ((), (), s32[]{:S(2)}) async-start(), calls=%async_computation.9 | async-start | bytes 2752512 | tf_op jit(solution)/shard_map/all_gather | solution.py:127
  9.4 0.6 copy-start.18
  12.4 116.8 %reduce-scatter.18.cloned.1.call-start = ((), (), s32[]{:S(2)}) async-start(), calls=%async_computation.10 | async-start | bytes 5505024 | tf_op jit(solution)/shard_map/reduce_scatter | solution.py:179
  12.4 36.1 %copy-start.22 = (f32[32]{0:T(128)}, f32[32]{0:T(128)S(1)}, u32[]{:S(2)}) copy-start(f32[32]{0:T(128)S(1)} %multiply_power_fusion) | copy-start | bytes 388
  13.1 35.5 %copy-start.14 = (f32[1024]{0:T(1024)}, f32[1024]{0:T(1024)S(1)}, u32[]{:S(2)}) copy-start(f32[1024]{0:T(1024)S(1)} %get-tuple-element.123) | copy-start | bytes 12292
  13.9 35.2 %copy-start.6 = (f32[1024,32]{0,1:T(8,128)}, f32[1024,32]{0,1:T(8,128)S(1)}, u32[]{:S(2)}) copy-start(f32[1024,32]{0,1:T(8,128)S(1)} %get-tuple-element.103) | copy-start | bytes 393220
  13.9 35.2 %copy-start.8 = (f32[1024,32]{0,1:T(8,128)}, f32[1024,32]{0,1:T(8,128)S(1)}, u32[]{:S(2)}) copy-start(f32[1024,32]{0,1:T(8,128)S(1)} %get-tuple-element.104) | copy-start | bytes 393220
  48.3 20.6 %copy-start.20 = (bf16[1024,576]{0,1:T(8,128)(2,1)}, bf16[1024,576]{0,1:T(8,128)(2,1)S(1)}, u32[]{:S(2)}) copy-start(bf16[1024,576]{0,1:T(8,128)(2,1)S(1)} %get-tuple-element.115) | copy-start | bytes 3538948
  49.5 5.6 copy-start.3
  50.8 2.9 copy-start.1
  69.0 7.8 copy-start.27
  75.8 1.0 copy-start.10
  79.9 51.4 %copy-start.17 = (f32[896]{0:T(1024)S(1)}, f32[896]{0:T(1024)}, u32[]{:S(2)}) copy-start(f32[896]{0:T(1024)} %param.32) | copy-start | bytes 10756
  79.9 82.8 %all-gather.7.cloned.1.call-start = ((), (), s32[]{:S(2)}) async-start(), calls=%async_computation.11 | async-start | bytes 2752512 | tf_op jit(solution)/shard_map/all_gather | solution.py:186
  132.4 62.0 %all-gather.9.cloned.1.call-start = ((), (), s32[]{:S(2)}) async-start(), calls=%async_computation.13 | async-start | bytes 2752512 | tf_op jit(solution)/shard_map/all_gather | solution.py:200
  133.0 146.7 %reduce-scatter.22.cloned.1.call-start = ((), (), s32[]{:S(2)}) async-start(), calls=%async_computation.14 | async-start | bytes 5505024 | tf_op jit(solution)/shard_map/reduce_scatter | solution.py:211
  162.7 10.7 %copy-start.26 = (bf16[1024,896]{1,0:T(8,128)(2,1)S(1)}, bf16[1024,896]{1,0:T(8,128)(2,1)}, u32[]{:S(2)}) copy-start(bf16[1024,896]{1,0:T(8,128)(2,1)} %all-gather.7.cloned.1.call-done) | copy-start | bytes 5505028
  211.9 8.9 copy-start.30
  230.4 80.9 %reduce-scatter.20.cloned.1.call-start = ((), (), s32[]{:S(2)}) async-start(), calls=%async_computation.12 | async-start | bytes 2752512 | tf_op jit(solution)/shard_map/reduce_scatter | solution.py:193
  240.5 105.7 %all-gather.11.cloned.1.call-start = ((), (), s32[]{:S(2)}) async-start(), calls=%async_computation.15 | async-start | bytes 2752512 | tf_op jit(solution)/shard_map/all_gather | solution.py:216
  315.8 130.2 %reduce-scatter.24.cloned.1.call-start = ((), (), s32[]{:S(2)}) async-start(), calls=%async_computation.16 | async-start | bytes 2752512 | tf_op jit(solution)/shard_map/reduce_scatter | solution.py:281
  346.1 8.5 slice-start.4
  349.1 5.5 slice-start.5
  359.9 9.4 %copy-start.4 = (bf16[1024,1,7,32]{0,3,2,1:T(8,128)(2,1)S(1)}, bf16[1024,1,7,32]{0,3,2,1:T(8,128)(2,1)}, u32[]{:S(2)}) copy-start(bf16[1024,1,7,32]{0,3,2,1:T(8,128)(2,1)} %copy-done.3) | copy-start | bytes 1376260
  359.9 15.6 %slice-start = ((s8[14680064]{0:T(1024)(128)(4,1)}), s8[4194304]{0:T(1024)(128)(4,1)S(1)}, s32[]{:S(2)}) async-start(s8[14680064]{0:T(1024)(128)(4,1)} %bitcast.214), calls=%async_computation.22 | async-start | bytes 8388608
  359.9 15.6 %slice-start.1 = ((s8[14680064]{0:T(1024)(128)(4,1)}), s8[4194304]{0:T(1024)(128)(4,1)S(1)}, s32[]{:S(2)}) async-start(s8[14680064]{0:T(1024)(128)(4,1)} %bitcast.214), calls=%async_computation.23 | async-start | bytes 8388608
  359.9 15.6 %slice-start.2 = ((s8[14680064]{0:T(1024)(128)(4,1)}), s8[2097152]{0:T(1024)(128)(4,1)S(1)}, s32[]{:S(2)}) async-start(s8[14680064]{0:T(1024)(128)(4,1)} %bitcast.214), calls=%async_computation.24 | async-start | bytes 4194304
  369.3 6.2 slice-start.3
  369.3 6.2 copy-start.5
  385.5 11.9 %copy-start.12 = (bf16[1024,64]{0,1:T(8,128)(2,1)}, bf16[1024,64]{0,1:T(8,128)(2,1)S(1)}, u32[]{:S(2)}) copy-start(bf16[1024,64]{0,1:T(8,128)(2,1)S(1)} %fusion.64) | copy-start | bytes 393220
  394.1 2.4 copy-start.15
  394.1 2.4 copy-start.23
  394.1 2.9 copy-start.7
  394.1 2.9 copy-start.9
  397.4 3.1 copy-start.11
  400.5 4.1 copy-start.13
  400.5 118.2 %reduce-scatter.26.cloned.1.call-start = ((), (), s32[]{:S(2)}) async-start(), calls=%async_computation.17 | async-start | bytes 1949696 | tf_op jit(solution)/shard_map/reduce_scatter | solution.py:291
  404.5 156.8 %reduce-scatter.28.cloned.1.call-start = ((), (), s32[]{:S(2)}) async-start(), calls=%async_computation.18 | async-start | bytes 2437120
  409.1 266.1 %reduce-scatter.34.cloned.1.call-start = ((), (), s32[]{:S(2)}) async-start(), calls=%async_computation.21 | async-start | bytes 9261056
  420.8 368.3 %reduce-scatter.32.cloned.1.call-start = ((), (), s32[]{:S(2)}) async-start(), calls=%async_computation.20 | async-start | bytes 9261056
  432.2 470.8 %reduce-scatter.30.cloned.1.call-start = ((), (), s32[]{:S(2)}) async-start(), calls=%async_computation.19 | async-start | bytes 9261056
  443.9 0.7 copy-start.29
  443.9 2.2 copy-start.2
  443.9 2.2 copy-start.16
  443.9 2.2 copy-start.19
  443.9 71.3 %copy-start.21 = (f32[512]{0:T(512)S(1)}, f32[512]{0:T(512)}, u32[]{:S(2)}) copy-start(f32[512]{0:T(512)} %get-tuple-element.109) | copy-start | bytes 6148
Sparse Core Ops, SparseCore 0:
  12.5 32.8 all-gather.4
  80.0 49.0 reduce-scatter.17
  132.5 30.1 all-gather.6
  164.2 30.1 all-gather.8
  230.5 49.0 reduce-scatter.21
  282.3 28.9 reduce-scatter.19
  315.9 30.1 all-gather.10
  400.6 28.9 reduce-scatter.23
  433.8 60.7 reduce-scatter.25
  498.8 62.4 reduce-scatter.27
  565.9 109.2 reduce-scatter.33
  679.7 109.3 reduce-scatter.31
  793.6 109.3 reduce-scatter.29
where the time goes:
time: 916 us; the launch traced here: 910 us
  waiting for transfers between devices  605 us (66%)
  matrix products  167 us (18%)
  blocking collectives  66.9 us (7%)
  other arithmetic  48.6 us (5%)
  between operations  15.5 us (2%)
    unnamed x17, waiting for transfers between devices  385 us
    unnamed x1, blocking collectives  61.5 us
    reduce_scatter x1, waiting for transfers between devices, shards(): lax.psum_scatter(jnp.dot(context, out_weight, preferred_element_type=jnp....  49.2 us
    dot_general x5, matrix products, contract_rows(): lax.dot_general(left, right, (((0,), (0,)), ((), ())), preferred_element_...  42.6 us
    dot_general x5, matrix products, times_transpose(): lax.dot_general(left, right, (((1,), (1,)), ((), ())), preferred_element_...  41.9 us
    reduce_scatter x1, waiting for transfers between devices, shards(): lax.psum_scatter(gate_part + times_transpose(d_up, up_weight), 'tensor',...  39.1 us
    all_gather x1, waiting for transfers between devices, shards(): lax.all_gather(normed_one.astype(jnp.bfloat16), 'tensor', axis=0, tiled=T...  30.7 us
    all_gather x1, waiting for transfers between devices, shards(): lax.all_gather(d_hidden.astype(jnp.bfloat16), 'tensor', axis=0, tiled=True)  30.2 us
  transfers between devices with their start and end apart: 13, of which 11 were waited for; matrix products, arithmetic and copies ran while one was open for 9% of the time, Pallas kernels for 0%

commit v1 on v0

--- a/solution.py
+++ b/solution.py
@@ -97,6 +97,48 @@
     return lax.dot_general(
         left, right, (((1,), (1,)), ((), ())), preferred_element_type=jnp.float32
     )
+
+
+def pair_swap(block):
+    return lax.ppermute(block, "tensor", [(0, 1), (1, 0)])
+
+
+def gather_pair(own):
+    other = pair_swap(own)
+    first = lax.axis_index("tensor") == 0
+    return jnp.concatenate(
+        [jnp.where(first, own, other), jnp.where(first, other, own)], axis=0
+    )
+
+
+def half_rows(array, which):
+    rows = array.shape[0] // 2
+    return lax.dynamic_slice_in_dim(array, which * rows, rows, axis=0)
+
+
+def sum_pair(partial_of):
+    me = lax.axis_index("tensor")
+    sent = pair_swap(partial_of(1 - me).astype(jnp.bfloat16))
+    return partial_of(me) + sent.astype(jnp.float32)
+
+
+def dp_sum_rows(partial):
+    count = lax.axis_size("dp")
+    me = lax.axis_index("dp")
+    rows = partial.shape[0] // count
+    current = partial.reshape(count, rows, partial.shape[1])
+    step = 1
+    while step < count:
+        bit = (me // step) % 2
+        pairs = current.reshape(current.shape[0] // 2, 2, rows, partial.shape[1])
+        sent = lax.dynamic_index_in_dim(pairs, 1 - bit, axis=1, keepdims=False)
+        kept = lax.dynamic_index_in_dim(pairs, bit, axis=1, keepdims=False)
+        got = lax.ppermute(sent, "dp", [(i, i ^ step) for i in range(count)])
+        current = kept.astype(jnp.float32) + got.astype(jnp.float32)
+        step *= 2
+        if step < count:
+            current = current.astype(jnp.bfloat16)
+    return current[0]
 
 
 def shards(
@@ -124,7 +166,10 @@
     block_count = group_rows // QB
     token_vals = tokens.astype(jnp.float32)
     rms_one, normed_one = rms_forward(token_vals, norm1_gain)
-    normed_one = lax.all_gather(normed_one.astype(jnp.bfloat16), "tensor", axis=0, tiled=True)
+    normed_one = gather_pair(normed_one.astype(jnp.bfloat16))
+    cot_sent, _ = lax.optimization_barrier((cotangent, normed_one))
+    cot_group = gather_pair(cot_sent)
+    d_mixed = lax.optimization_barrier(times_transpose(cot_group, down_weight))
     projected = jnp.dot(normed_one, qkv_weight, preferred_element_type=jnp.float32) + qkv_bias
     query_rows = projected[:, :query_columns].reshape(
         group_rows, kv_local, heads_per_group, HEAD_WIDTH
@@ -176,45 +221,37 @@
     context = (
         jnp.concatenate(contexts, axis=0).reshape(group_rows, query_columns).astype(jnp.bfloat16)
     )
-    hidden_one = token_vals + lax.psum_scatter(
-        jnp.dot(context, out_weight, preferred_element_type=jnp.float32),
-        "tensor",
-        scatter_dimension=0,
-        tiled=True,
+    hidden_one = token_vals + sum_pair(
+        lambda t: jnp.dot(half_rows(context, t), out_weight, preferred_element_type=jnp.float32)
     )
     rms_two, normed_two = rms_forward(hidden_one, norm2_gain)
-    normed_two = lax.all_gather(normed_two.astype(jnp.bfloat16), "tensor", axis=0, tiled=True)
+    normed_two = gather_pair(normed_two.astype(jnp.bfloat16))
     gate_pre = jnp.dot(normed_two, gate_weight, preferred_element_type=jnp.float32)
     up_pre = jnp.dot(normed_two, up_weight, preferred_element_type=jnp.float32)
     activated = jax.nn.silu(gate_pre)
     mixed = (activated * up_pre).astype(jnp.bfloat16)
     block_result = (
         hidden_one
-        + lax.psum_scatter(
-            jnp.dot(mixed, down_weight, preferred_element_type=jnp.float32).astype(jnp.bfloat16),
-            "tensor",
-            scatter_dimension=0,
-            tiled=True,
-        ).astype(jnp.float32)
+        + sum_pair(
+            lambda t: jnp.dot(half_rows(mixed, t), down_weight, preferred_element_type=jnp.float32)
+        )
     ).astype(jnp.bfloat16)
-    cot_group = lax.all_gather(cotangent, "tensor", axis=0, tiled=True)
-    down_grad = contract_rows(mixed, cot_group)
-    d_mixed = times_transpose(cot_group, down_weight)
+    down_grad = contract_rows(cot_group, mixed).astype(jnp.bfloat16)
     sigmoid_gate = jax.nn.sigmoid(gate_pre)
     d_gate = (d_mixed * up_pre * sigmoid_gate * (1.0 + gate_pre * (1.0 - sigmoid_gate))).astype(
         jnp.bfloat16
     )
     d_up = (d_mixed * activated).astype(jnp.bfloat16)
-    gate_grad = contract_rows(normed_two, d_gate)
-    up_grad = contract_rows(normed_two, d_up)
-    gate_part = times_transpose(d_gate, gate_weight)
-    d_normed_two = lax.psum_scatter(
-        gate_part + times_transpose(d_up, up_weight), "tensor", scatter_dimension=0, tiled=True
+    gate_grad = contract_rows(normed_two, d_gate).astype(jnp.bfloat16)
+    up_grad = contract_rows(normed_two, d_up).astype(jnp.bfloat16)
+    d_normed_two = sum_pair(
+        lambda t: times_transpose(half_rows(d_gate, t), gate_weight)
+        + times_transpose(half_rows(d_up, t), up_weight)
     )
     d_hidden_norm, gain_two_grad = rms_backward(hidden_one, rms_two, norm2_gain, d_normed_two)
     d_hidden = cotangent.astype(jnp.float32) + d_hidden_norm
-    d_resid = lax.all_gather(d_hidden.astype(jnp.bfloat16), "tensor", axis=0, tiled=True)
-    out_grad = contract_rows(context, d_resid)
+    d_resid = gather_pair(d_hidden.astype(jnp.bfloat16))
+    out_grad = contract_rows(d_resid, context).astype(jnp.bfloat16)
     d_context = (
         times_transpose(d_resid, out_weight)
         .astype(jnp.bfloat16)
@@ -276,27 +313,34 @@
         ],
         axis=1,
     ).astype(jnp.bfloat16)
-    qkv_grad = contract_rows(normed_one, d_proj)
+    qkv_grad = contract_rows(normed_one, d_proj).astype(jnp.bfloat16)
     bias_grad = jnp.sum(d_proj, axis=0, dtype=jnp.float32)
-    d_normed_one = lax.psum_scatter(
-        times_transpose(d_proj, qkv_weight).astype(jnp.bfloat16),
-        "tensor",
-        scatter_dimension=0,
-        tiled=True,
-    ).astype(jnp.float32)
+    d_normed_one = sum_pair(lambda t: times_transpose(half_rows(d_proj, t), qkv_weight))
     d_token_norm, gain_one_grad = rms_backward(token_vals, rms_one, norm1_gain, d_normed_one)
     tokens_grad = d_hidden + d_token_norm
-    qkv_grad, out_grad, gate_grad, up_grad, down_grad, gain_one_grad, gain_two_grad = (
-        lax.psum_scatter(qkv_grad, "dp", scatter_dimension=0, tiled=True),
-        lax.psum_scatter(out_grad, "dp", scatter_dimension=1, tiled=True),
-        lax.psum_scatter(gate_grad, "dp", scatter_dimension=0, tiled=True),
-        lax.psum_scatter(up_grad, "dp", scatter_dimension=0, tiled=True),
-        lax.psum_scatter(down_grad, "dp", scatter_dimension=1, tiled=True),
-        lax.psum_scatter(gain_one_grad, "dp", scatter_dimension=0, tiled=True),
-        lax.psum_scatter(gain_two_grad, "dp", scatter_dimension=0, tiled=True),
-    )
-    bias_grad = lax.psum(bias_grad, "dp")
-    gain_one_grad, gain_two_grad = lax.psum((gain_one_grad, gain_two_grad), "tensor")
+    down_grad = dp_sum_rows(down_grad).T
+    gate_grad = dp_sum_rows(gate_grad)
+    up_grad = dp_sum_rows(up_grad)
+    small = dp_sum_rows(jnp.concatenate([qkv_grad, out_grad], axis=1))
+    qkv_grad = small[:, : qkv_weight.shape[1]]
+    out_grad = small[:, qkv_weight.shape[1] :].T
+    me = lax.axis_index("tensor")
+    width = norm1_gain.shape[0]
+    bias_columns = bias_grad.shape[0]
+    placed_bias = lax.dynamic_update_slice_in_dim(
+        jnp.zeros((bias_columns * lax.axis_size("tensor"),), jnp.float32),
+        bias_grad,
+        me * bias_columns,
+        axis=0,
+    )
+    sums = lax.psum(
+        jnp.concatenate([gain_one_grad, gain_two_grad, placed_bias]), ("dp", "tensor")
+    )
+    share = width // lax.axis_size("dp")
+    gain_at = lax.axis_index("dp") * share
+    gain_one_grad = lax.dynamic_slice_in_dim(sums, gain_at, share)
+    gain_two_grad = lax.dynamic_slice_in_dim(sums, width + gain_at, share)
+    bias_grad = lax.dynamic_slice_in_dim(sums, 2 * width + me * bias_columns, bias_columns)
     return (
         block_result,
         tokens_grad,

time: 916 us -> 520 us (0.57)
  waiting for transfers between devices: 605 us -> 160 us
  starting transfers between devices: 1 us -> 25.7 us
  blocking collectives: 66.9 us -> 90.1 us
  matrix products: 167 us -> 151 us
  other arithmetic: 48.6 us -> 64.5 us
  local copies, waits for them, and re-layouts: 5.97 us -> 19.8 us
  between operations: 15.5 us -> 2.11 us
    unnamed x17 -> x0, waiting for transfers between devices: 385 us -> none
    ppermute x0 -> x24, waiting for transfers between devices: none -> 160 us  [the longest x8 103 us: pair_swap(): return lax.ppermute(block, 'tensor', [(0, 1), (1, 0)])]
    reduce_scatter x5 -> x0, waiting for transfers between devices: 118 us -> none  [the longest x1 49.2 us: shards(): lax.psum_scatter(jnp.dot(context, out_weight, preferred_element_type=jnp....]
    all_gather x4 -> x0, waiting for transfers between devices: 102 us -> none  [the longest x1 30.7 us: shards(): lax.all_gather(normed_one.astype(jnp.bfloat16), 'tensor', axis=0, tiled=T...]
    psum x1, blocking collectives: 5.42 us -> 90.1 us  [shards(): lax.psum(jnp.concatenate([gain_one_grad, gain_two_grad, placed_bias]), ('...]
    unnamed x1 -> x0, blocking collectives: 61.5 us -> none
    ppermute x0 -> x24, starting transfers between devices: none -> 25.7 us  [the longest x16 14.9 us: dp_sum_rows(): got = lax.ppermute(sent, 'dp', [(i, i ^ step) for i in range(count)])]
    dot_general x5, matrix products: 42.6 us -> 24.1 us  [contract_rows(): lax.dot_general(left, right, (((0,), (0,)), ((), ())), preferred_element_...]
  transfers between devices with their start and end apart: 13 -> 24, of which waited for: 11 -> 14; matrix products, arithmetic and copies ran while one was open for 9% -> 25% of each run, Pallas kernels for 0% -> 0%
where the time goes in v1:
time: 520 us; the launch traced here: 513 us
  waiting for transfers between devices  160 us (31%)
  matrix products  151 us (29%)
  blocking collectives  90.1 us (17%)
  other arithmetic  64.5 us (12%)
  starting transfers between devices  25.7 us (5%)
  local copies, waits for them, and re-layouts  19.8 us (4%)
    ppermute x8, waiting for transfers between devices, pair_swap(): return lax.ppermute(block, 'tensor', [(0, 1), (1, 0)])  103 us
    psum x1, blocking collectives, shards(): lax.psum(jnp.concatenate([gain_one_grad, gain_two_grad, placed_bias]), ('...  90.1 us
    ppermute x16, waiting for transfers between devices, dp_sum_rows(): got = lax.ppermute(sent, 'dp', [(i, i ^ step) for i in range(count)])  57.2 us
    dot_general x8, matrix products, times_transpose(): lax.dot_general(left, right, (((1,), (1,)), ((), ())), preferred_element_...  39.5 us
    dot_general x5, matrix products, contract_rows(): lax.dot_general(left, right, (((0,), (0,)), ((), ())), preferred_element_...  24.1 us
    another operation x7, other arithmetic  20.5 us
    dot_general x1, matrix products, shards(): jnp.dot(normed_two, gate_weight, preferred_element_type=jnp.float32)  17.4 us
    ppermute x16, starting transfers between devices, dp_sum_rows(): got = lax.ppermute(sent, 'dp', [(i, i ^ step) for i in range(count)])  14.9 us
  transfers between devices with their start and end apart: 24, of which 14 were waited for; matrix products, arithmetic and copies ran while one was open for 25% of the time, Pallas kernels for 0%

profile of v1, /device:TPU:0, one launch (start us, length us, event | category | flops | bytes accessed | tf_op | source)
XLA Modules:
  0.0 513.1 jit_solution(15785122156757741251)
XLA Ops:
  2.9 2.4 fusion.48
  5.2 3.0 collective-permute-start
  10.5 18.4 %collective-permute-done = bf16[512,896]{1,0:T(8,128)(2,1)} collective-permute-done((bf16[512,896]{1,0:T(8,128)(2,1)}, bf16[512,896]{1,0:T(8,128)(2,1)}, u32[]{:S(2)}, u32[]{:S(2)}) %collective-permute-start) | collective-permute-done | bytes 917536 | tf_op jit(solution)/shard_map/ppermute | solution.py:103
  28.9 1.7 broadcast_select_fusion.7
  35.6 2.0 copy-done.1
  38.9 6.8 %fusion.172 = (f32[7,512]{1,0:T(8,128)S(1)}, f32[1,7,512,1024]{2,3,1,0:T(8,128)}) fusion(bf16[1024,1,7,32]{0,3,2,1:T(8,128)(2,1)S(1)} %get-tuple-element.92, bf16[1024,1,7,32]{0,3,2,1:T(8,128)(2,1)S(1)} %get-tuple-element.91, bf16[1024,32]{0,1:T(8,128)(2,1)S(1)} %bitcast.344, bf16[1024,32]{0,1:T(8,128)(2,1)S(1)} %bitcast.342, pred[512,1024]{0,1:T(8,128)(4,1)S(1)} %fusion.44), kind=kOutput, calls=%fused_computation.276 | convolution fusion | flops 481948160 | bytes 16267264 | tf_op jit(solution)/shard_map/qjgd,kjd->jgqk/dot_general | solution.py:198
  45.7 7.2 %fusion.3 = f32[7,512]{1,0:T(8,128)S(1)} fusion(f32[1,7,512,1024]{2,3,1,0:T(8,128)} %get-tuple-element.120, f32[7,512]{1,0:T(8,128)S(1)} %get-tuple-element.119), kind=kLoop, calls=%fused_computation.9 | loop fusion | flops 7336448 | bytes 14708736 | tf_op jit(solution)/shard_map/reduce_sum | solution.py:209
  52.9 6.7 %fusion.71 = bf16[512,1,7,64]{0,3,2,1:T(8,128)(2,1)S(1)} fusion(f32[7,512]{1,0:T(8,128)S(1)} %fusion.3, f32[1,7,512,1024]{2,3,1,0:T(8,128)} %get-tuple-element.120, f32[7,512]{1,0:T(8,128)S(1)} %get-tuple-element.119, bf16[1024,576]{0,1:T(8,128)(2,1)S(1)} %get-tuple-element.121), kind=kOutput, calls=%fused_computation.121 | convolution fusion | flops 481001472 | bytes 15302656 | tf_op jit(solution)/shard_map/jgqk,kjd->qjgd/dot_general | solution.py:214
  61.4 1.8 collective-permute-start.1
  63.5 21.4 %collective-permute-done.1 = bf16[512,896]{1,0:T(8,128)(2,1)} collective-permute-done((bf16[512,896]{1,0:T(8,128)(2,1)S(1)}, bf16[512,896]{1,0:T(8,128)(2,1)}, u32[]{:S(2)}, u32[]{:S(2)}) %collective-permute-start.1) | collective-permute-done | bytes 917536 | tf_op jit(solution)/shard_map/ppermute | solution.py:103
  84.8 2.7 multiply_reduce_fusion.2
  88.8 1.7 collective-permute-start.2
  90.5 14.0 %collective-permute-done.4 = bf16[512,896]{1,0:T(8,128)(2,1)} collective-permute-done((bf16[512,896]{1,0:T(8,128)(2,1)}, bf16[512,896]{1,0:T(8,128)(2,1)}, u32[]{:S(2)}, u32[]{:S(2)}) %collective-permute-start.4) | collective-permute-done | bytes 917536 | tf_op jit(solution)/shard_map/ppermute | solution.py:103
  104.5 17.9 %collective-permute-done.2 = bf16[512,896]{1,0:T(8,128)(2,1)} collective-permute-done((bf16[512,896]{1,0:T(8,128)(2,1)}, bf16[512,896]{1,0:T(8,128)(2,1)}, u32[]{:S(2)}, u32[]{:S(2)}) %collective-permute-start.2) | collective-permute-done | bytes 917536 | tf_op jit(solution)/shard_map/ppermute | solution.py:103
  122.4 2.4 broadcast_select_fusion.3
  124.9 8.9 %fusion.77 = f32[1024,2432]{1,0:T(8,128)} fusion(bf16[2432,896]{1,0:T(8,128)(2,1)S(1)} %bitcast.354, bf16[512,896]{1,0:T(8,128)(2,1)S(1)} %get-tuple-element.96, bf16[512,896]{1,0:T(8,128)(2,1)S(1)} %get-tuple-element.95), kind=kOutput, calls=%fused_computation.123 | convolution fusion | flops 4466409472 | bytes 16154624 | tf_op jit(solution)/shard_map/dot_general | solution.py:97
  133.8 9.0 %fusion.164 = f32[1024,2432]{1,0:T(8,128)} fusion(bf16[896,2432]{1,0:T(8,128)(2,1)S(1)} %bitcast.350, bf16[512,896]{1,0:T(8,128)(2,1)S(1)} %get-tuple-element.133, bf16[512,896]{1,0:T(8,128)(2,1)S(1)} %get-tuple-element.134), kind=kOutput, calls=%fused_computation.270 | convolution fusion | flops 4466409472 | bytes 16154624 | tf_op jit(solution)/shard_map/dot_general | solution.py:230
  142.8 17.4 %multiply_convert_fusion.1 = (bf16[1024,2432]{1,0:T(8,128)(2,1)}, bf16[1024,2432]{1,0:T(8,128)(2,1)}, bf16[1024,2432]{1,0:T(8,128)(2,1)}) fusion(f32[1024,2432]{1,0:T(8,128)} %fusion.77, f32[1024,2432]{1,0:T(8,128)} %fusion.164, bf16[896,2432]{1,0:T(8,128)(2,1)} %param.33, bf16[512,896]{1,0:T(8,128)(2,1)S(1)} %get-tuple-element.133, ...), kind=kOutput, calls=%fused_computation.12 | convolution fusion | flops 4503764992 | bytes 41058304 | tf_op jit(solution)/shard_map/dot_general | solution.py:229
  160.2 7.2 %fusion.28 = f32[512,896]{1,0:T(8,128)} fusion(bf16[896,2432]{1,0:T(8,128)(2,1)} %param.34, bf16[1024,2432]{1,0:T(8,128)(2,1)} %get-tuple-element.87, s32[]{:T(128)S(6)} %select_n.223), kind=kOutput, calls=%fused_computation.54 | convolution fusion | flops 2231369728 | bytes 8683524 | tf_op jit(solution)/shard_map/dot_general | solution.py:97
  167.4 6.5 %fusion.32 = f32[512,896]{1,0:T(8,128)} fusion(bf16[896,2432]{1,0:T(8,128)(2,1)} %param.34, bf16[1024,2432]{1,0:T(8,128)(2,1)S(1)} %copy-done.52, s32[]{:T(128)S(6)} %select_n.222), kind=kOutput, calls=%fused_computation.58 | convolution fusion | flops 2231369728 | bytes 8683524 | tf_op jit(solution)/shard_map/dot_general | solution.py:97
  173.9 7.5 %convolution_convert_fusion.1 = bf16[896,2432]{1,0:T(8,128)(2,1)S(1)} fusion(bf16[1024,2432]{1,0:T(8,128)(2,1)} %get-tuple-element.87, bf16[512,896]{1,0:T(8,128)(2,1)S(1)} %get-tuple-element.133, bf16[512,896]{1,0:T(8,128)(2,1)S(1)} %copy-done.30), kind=kOutput, calls=%fused_computation.34 | convolution fusion | flops 4468588544 | bytes 11173888 | tf_op jit(solution)/shard_map/dot_general | solution.py:91
  181.5 6.1 %fusion.60 = bf16[512,896]{1,0:T(8,128)(2,1)S(1)} fusion(bf16[2432,896]{1,0:T(8,128)(2,1)S(1)} %bitcast.356, bf16[1024,2432]{1,0:T(8,128)(2,1)} %get-tuple-element.88, s32[]{:T(128)S(6)} %select_n.223), kind=kOutput, calls=%fused_computation.110 | convolution fusion | flops 2231828480 | bytes 7766020 | tf_op jit(solution)/shard_map/dot_general | solution.py:236
  189.1 5.5 %convolution_convert_fusion.2 = bf16[896,2432]{1,0:T(8,128)(2,1)S(1)} fusion(bf16[1024,2432]{1,0:T(8,128)(2,1)S(1)} %bitcast.358, bf16[512,896]{1,0:T(8,128)(2,1)S(1)} %get-tuple-element.133, bf16[512,896]{1,0:T(8,128)(2,1)S(1)} %copy-done.30), kind=kOutput, calls=%fused_computation.35 | convolution fusion | flops 4468588544 | bytes 11173888 | tf_op jit(solution)/shard_map/dot_general | solution.py:91
  194.6 5.7 %add_convert_fusion = bf16[512,896]{1,0:T(8,128)(2,1)S(1)} fusion(f32[512,896]{1,0:T(8,128)} %fusion.28, bf16[896,2432]{1,0:T(8,128)(2,1)S(1)} %bitcast.352, bf16[1024,2432]{1,0:T(8,128)(2,1)S(1)} %bitcast.358, s32[]{:T(128)S(6)} %select_n.223), kind=kOutput, calls=%fused_computation.104 | convolution fusion | flops 2232287232 | bytes 9601028 | tf_op jit(solution)/shard_map/dot_general | solution.py:97
  201.0 1.6 dynamic-slice_bitcast_fusion.2
  204.2 7.5 %convolution_convert_fusion = bf16[896,2432]{1,0:T(8,128)(2,1)S(1)} fusion(bf16[1024,2432]{1,0:T(8,128)(2,1)} %get-tuple-element.88, bf16[512,896]{1,0:T(8,128)(2,1)S(1)} %get-tuple-element.96, bf16[512,896]{1,0:T(8,128)(2,1)S(1)} %get-tuple-element.95), kind=kOutput, calls=%fused_computation.33 | convolution fusion | flops 4468588544 | bytes 11173888 | tf_op jit(solution)/shard_map/dot_general | solution.py:91
  211.7 16.2 %collective-permute-done.5 = bf16[512,896]{1,0:T(8,128)(2,1)S(1)} collective-permute-done((bf16[512,896]{1,0:T(8,128)(2,1)S(1)}, bf16[512,896]{1,0:T(8,128)(2,1)S(1)}, u32[]{:S(2)}, u32[]{:S(2)}) %collective-permute-start.5) | collective-permute-done | bytes 917536 | tf_op jit(solution)/shard_map/ppermute | solution.py:103
  227.9 3.2 multiply_reduce_fusion
  231.2 3.0 fusion.168
  237.3 5.5 %add_convert_fusion.1 = bf16[512,896]{1,0:T(8,128)(2,1)} fusion(f32[512,896]{1,0:T(8,128)S(1)} %get-tuple-element.126, bf16[512,896]{1,0:T(8,128)(2,1)S(1)} %collective-permute-done.3, bf16[2432,896]{1,0:T(8,128)(2,1)S(1)} %bitcast.356, bf16[1024,2432]{1,0:T(8,128)(2,1)} %get-tuple-element.88, s32[]{:T(128)S(6)} %select_n.222), kind=kOutput, calls=%fused_computation.105 | convolution fusion | flops 2233204736 | bytes 10518532 | tf_op jit(solution)/shard_map/dot_general | solution.py:236
  242.9 11.0 %collective-permute-done.6 = bf16[512,896]{1,0:T(8,128)(2,1)S(1)} collective-permute-done((bf16[512,896]{1,0:T(8,128)(2,1)S(1)}, bf16[512,896]{1,0:T(8,128)(2,1)S(1)}, u32[]{:S(2)}, u32[]{:S(2)}) %collective-permute-start.6) | collective-permute-done | bytes 917536 | tf_op jit(solution)/shard_map/ppermute | solution.py:103
  254.1 2.2 convolution_convert_fusion.7
  258.4 5.4 %fusion.10 = (f32[7,512]{1,0:T(8,128)S(1)}, f32[512,512,7]{1,0,2:T(8,128)}) fusion(f32[1,7,512,512]{2,3,1,0:T(8,128)S(1)} %bitcast.302, f32[7,512]{1,0:T(8,128)S(1)} %log_add_fusion.1, bf16[512,7,64]{0,2,1:T(8,128)(2,1)S(1)} %bitcast.332, bf16[1024,576]{0,1:T(8,128)(2,1)} %copy-done.43), kind=kOutput, calls=%fused_computation.22 | convolution fusion | flops 240382464 | bytes 15233024 | tf_op jit(solution)/shard_map/qjgd,kjd->jgqk/dot_general | solution.py:279
  263.7 9.3 %fusion.24 = bf16[7,512,512]{1,2,0:T(8,128)(2,1)} fusion(f32[512,512,7]{1,0,2:T(8,128)} %get-tuple-element.131, f32[1,7,512,512]{2,3,1,0:T(8,128)} %copy-done.1, f32[7,512]{1,0:T(8,128)S(1)} %get-tuple-element.130, f32[7,512]{1,0:T(8,128)S(1)} %log_add_fusion.1), kind=kLoop, calls=%fused_computation.50 | loop fusion | flops 7340032 | bytes 18378752 | tf_op jit(solution)/shard_map/reshape.166
  273.1 3.4 fusion.97
  276.5 3.8 fusion.64
  280.3 7.5 %fusion = (f32[7,512]{1,0:T(8,128)S(1)}, f32[1024,512,7]{1,0,2:T(8,128)}) fusion(f32[1,7,512,1024]{2,3,1,0:T(8,128)S(1)} %bitcast.300, f32[7,512]{1,0:T(8,128)S(1)} %log_add_fusion, bf16[512,7,64]{0,2,1:T(8,128)(2,1)S(1)} %bitcast.330, bf16[1024,576]{0,1:T(8,128)(2,1)} %copy-done.43), kind=kOutput, calls=%fused_computation.3 | convolution fusion | flops 480768512 | bytes 29978624 | tf_op jit(solution)/shard_map/qjgd,kjd->jgqk/dot_general | solution.py:279
  287.9 7.5 %fusion.9 = bf16[7,512,1024]{1,2,0:T(8,128)(2,1)S(1)} fusion(f32[1024,512,7]{1,0,2:T(8,128)} %get-tuple-element.129, f32[1,7,512,1024]{2,3,1,0:T(8,128)S(1)} %bitcast.300, f32[7,512]{1,0:T(8,128)S(1)} %get-tuple-element.128, f32[7,512]{1,0:T(8,128)S(1)} %log_add_fusion), kind=kLoop, calls=%fused_computation.18 | loop fusion | flops 14680064 | bytes 36728832 | tf_op jit(solution)/shard_map/reshape.175
  295.4 2.3 fusion.63
  297.7 2.3 fusion.83
  300.7 2.1 add_convert_fusion.2
  304.2 2.4 fusion.90
  310.0 2.5 copy.63
  312.5 3.1 convolution_convert_fusion.6
  317.8 2.9 fusion.18
  320.9 1.6 collective-permute-start.21
  322.5 2.1 fusion.19
  327.3 2.1 fusion.20
  331.1 3.7 collective-permute-done.7
  334.8 3.7 fusion.54
  338.5 90.1 %psum.7 = f32[2944]{0:T(1024)S(1)} all-reduce(f32[2944]{0:T(1024)S(1)} %pad_maximum_fusion.15), channel_id=1, replica_groups=mesh['dp'=16,'tensor'=2] {'dp','tensor'}, use_global_device_ids=true, to_apply=%region_18.19 | all-reduce | flops 2944 | bytes 23552 | tf_op jit(solution)/shard_map/psum | solution.py:336
  428.6 2.0 fusion.55
  430.7 2.3 collective-permute-start.9
  434.3 3.2 fusion.51
  437.4 4.7 collective-permute-done.9
  442.9 1.7 fusion.40
  449.9 2.3 collective-permute-done.10
  452.5 2.1 collective-permute-start.14
  454.6 20.1 %collective-permute-done.11 = bf16[1,56,1024]{2,1,0:T(8,128)(2,1)S(1)} collective-permute-done((bf16[1,56,1024]{2,1,0:T(8,128)(2,1)S(1)}, bf16[1,56,1024]{2,1,0:T(8,128)(2,1)S(1)}, u32[]{:S(2)}, u32[]{:S(2)}) %collective-permute-start.11) | collective-permute-done | bytes 114720 | tf_op jit(solution)/shard_map/ppermute | solution.py:136
  476.3 3.4 collective-permute-start.23
  479.8 4.9 collective-permute-done.18
  485.0 9.2 %collective-permute-done.14 = bf16[2,56,2432]{2,1,0:T(8,128)(2,1)S(1)} collective-permute-done((bf16[2,56,2432]{2,1,0:T(8,128)(2,1)S(1)}, bf16[2,56,2432]{2,1,0:T(8,128)(2,1)S(1)}, u32[]{:S(2)}, u32[]{:S(2)}) %collective-permute-start.14) | collective-permute-done | bytes 544800 | tf_op jit(solution)/shard_map/ppermute | solution.py:136
  495.3 13.7 %collective-permute-done.19 = bf16[1,56,2432]{2,1,0:T(8,128)(2,1)S(1)} collective-permute-done((bf16[1,56,2432]{2,1,0:T(8,128)(2,1)S(1)}, bf16[1,56,2432]{2,1,0:T(8,128)(2,1)S(1)}, u32[]{:S(2)}, u32[]{:S(2)}) %collective-permute-start.19) | collective-permute-done | bytes 272416 | tf_op jit(solution)/shard_map/ppermute | solution.py:136
  509.9 2.2 collective-permute-done.15
  (264 shorter events, 47.0 us)
Async XLA Ops:
  0.6 30.0 %copy-start = (bf16[896,576]{0,1:T(8,128)(2,1)S(1)}, bf16[896,576]{0,1:T(8,128)(2,1)}, u32[]{:S(2)}) copy-start(bf16[896,576]{0,1:T(8,128)(2,1)} %param.29) | copy-start | bytes 3096580
  0.7 28.2 %copy-start.2 = (bf16[512,896]{1,0:T(8,128)(2,1)S(1)}, bf16[512,896]{1,0:T(8,128)(2,1)}, u32[]{:S(2)}) copy-start(bf16[512,896]{1,0:T(8,128)(2,1)} %param.24) | copy-start | bytes 2752516
  0.7 28.2 %copy-start.41 = (f32[896]{0:T(1024)S(1)}, f32[896]{0:T(1024)}, u32[]{:S(2)}) copy-start(f32[896]{0:T(1024)} %param.28) | copy-start | bytes 10756
  0.7 7.6 %copy-start.50 = (s32[64]{0:T(128)S(1)}, s32[64]{0:T(128)}, u32[]{:S(2)}) copy-start(s32[64]{0:T(128)} %param.27) | copy-start | bytes 772
  0.7 7.6 %copy-start.49 = (s32[64]{0:T(128)S(1)}, s32[64]{0:T(128)}, u32[]{:S(2)}) copy-start(s32[64]{0:T(128)} %param.26) | copy-start | bytes 772
  2.9 27.7 %copy-start.44 = (f32[512]{0:T(512)}, f32[512]{0:T(512)S(1)}, u32[]{:S(2)}) copy-start(f32[512]{0:T(512)S(1)} %get-tuple-element.116) | copy-start | bytes 6148
  5.2 23.6 %collective-permute-start = (bf16[512,896]{1,0:T(8,128)(2,1)}, bf16[512,896]{1,0:T(8,128)(2,1)}, u32[]{:S(2)}, u32[]{:S(2)}) collective-permute-start(bf16[512,896]{1,0:T(8,128)(2,1)} %fusion.48), channel_id=1, source_target_pairs={{0,1},{1,0},{2,3},{3,2},{4,5},{5,4},{6,7},{7,6},{8,9},{9,8},{10,11... | collective-permute-start | bytes 2752520 | tf_op jit(solution)/shard_map/ppermute | solution.py:103
  8.2 24.1 %copy-start.47 = (f32[32]{0:T(128)}, f32[32]{0:T(128)S(1)}, u32[]{:S(2)}) copy-start(f32[32]{0:T(128)S(1)} %multiply_power_fusion) | copy-start | bytes 388
  8.9 23.5 %copy-start.38 = (f32[1024]{0:T(1024)}, f32[1024]{0:T(1024)S(1)}, u32[]{:S(2)}) copy-start(f32[1024]{0:T(1024)S(1)} %subtract_convert_fusion.2) | copy-start | bytes 12292
  9.2 21.5 %copy-start.51 = (f32[576]{0:T(1024)S(1)}, f32[576]{0:T(1024)}, u32[]{:S(2)}) copy-start(f32[576]{0:T(1024)} %param.30) | copy-start | bytes 6916
  9.7 23.2 %copy-start.23 = (f32[1024,32]{0,1:T(8,128)}, f32[1024,32]{0,1:T(8,128)S(1)}, u32[]{:S(2)}) copy-start(f32[1024,32]{0,1:T(8,128)S(1)} %get-tuple-element.109) | copy-start | bytes 393220
  9.7 23.2 %copy-start.25 = (f32[1024,32]{0,1:T(8,128)}, f32[1024,32]{0,1:T(8,128)S(1)}, u32[]{:S(2)}) copy-start(f32[1024,32]{0,1:T(8,128)S(1)} %get-tuple-element.110) | copy-start | bytes 393220
  32.1 20.8 %copy-start.43 = (bf16[1024,576]{0,1:T(8,128)(2,1)}, bf16[1024,576]{0,1:T(8,128)(2,1)S(1)}, u32[]{:S(2)}) copy-start(bf16[1024,576]{0,1:T(8,128)(2,1)S(1)} %get-tuple-element.121) | copy-start | bytes 3538948
  52.9 7.8 %copy-start.35 = (bf16[448,896]{1,0:T(8,128)(2,1)S(1)}, bf16[448,896]{1,0:T(8,128)(2,1)}, u32[]{:S(2)}) copy-start(bf16[448,896]{1,0:T(8,128)(2,1)} %param.31) | copy-start | bytes 2408452
  61.4 23.5 %collective-permute-start.1 = (bf16[512,896]{1,0:T(8,128)(2,1)S(1)}, bf16[512,896]{1,0:T(8,128)(2,1)}, u32[]{:S(2)}, u32[]{:S(2)}) collective-permute-start(bf16[512,896]{1,0:T(8,128)(2,1)S(1)} %convolution_convert_fusion.5), channel_id=1, source_target_pairs={{0,1},{1,0},{2,3},{3,2},{4,5},{5,4},{6,7},{7,6},{8,9},{9,8},{10,11... | collective-permute-start | bytes 2752520 | tf_op jit(solution)/shard_map/ppermute | solution.py:103
  63.2 41.3 %collective-permute-start.4 = (bf16[512,896]{1,0:T(8,128)(2,1)}, bf16[512,896]{1,0:T(8,128)(2,1)}, u32[]{:S(2)}, u32[]{:S(2)}) collective-permute-start(bf16[512,896]{1,0:T(8,128)(2,1)} %param.25), channel_id=1, source_target_pairs={{0,1},{1,0},{2,3},{3,2},{4,5},{5,4},{6,7},{7,6},{8,9},{9,8},{10,11... | collective-permute-start | bytes 2752520 | tf_op jit(solution)/shard_map/ppermute | solution.py:103
  63.5 24.1 %copy-start.40 = (f32[896]{0:T(1024)S(1)}, f32[896]{0:T(1024)}, u32[]{:S(2)}) copy-start(f32[896]{0:T(1024)} %param.32) | copy-start | bytes 10756
  88.8 33.7 %collective-permute-start.2 = (bf16[512,896]{1,0:T(8,128)(2,1)}, bf16[512,896]{1,0:T(8,128)(2,1)}, u32[]{:S(2)}, u32[]{:S(2)}) collective-permute-start(bf16[512,896]{1,0:T(8,128)(2,1)} %multiply_convert_fusion.3), channel_id=1, source_target_pairs={{0,1},{1,0},{2,3},{3,2},{4,5},{5,4},{6,7},{7,6},{8,9},{9,8},{10,11... | collective-permute-start | bytes 2752520 | tf_op jit(solution)/shard_map/ppermute | solution.py:103
  90.5 34.4 %slice-start.16 = ((s8[4358144]{0:T(1024)(128)(4,1)}), s8[4194304]{0:T(1024)(128)(4,1)S(1)}, s32[]{:S(2)}) async-start(s8[4358144]{0:T(1024)(128)(4,1)} %bitcast.353), calls=%async_computation.16 | async-start | bytes 8388608
  90.5 34.4 %slice-start.17 = ((s8[4358144]{0:T(1024)(128)(4,1)}), s8[163840]{0:T(1024)(128)(4,1)S(1)}, s32[]{:S(2)}) async-start(s8[4358144]{0:T(1024)(128)(4,1)} %bitcast.353), calls=%async_computation.17 | async-start | bytes 327680
  122.4 11.4 %slice-start.12 = ((s8[4358144]{0:T(1024)(128)(4,1)}), s8[4194304]{0:T(1024)(128)(4,1)S(1)}, s32[]{:S(2)}) async-start(s8[4358144]{0:T(1024)(128)(4,1)} %bitcast.349), calls=%async_computation.12 | async-start | bytes 8388608
  124.9 8.9 %copy-start.29 = (bf16[512,896]{1,0:T(8,128)(2,1)}, bf16[512,896]{1,0:T(8,128)(2,1)S(1)}, u32[]{:S(2)}) copy-start(bf16[512,896]{1,0:T(8,128)(2,1)S(1)} %get-tuple-element.134) | copy-start | bytes 2752516
  124.9 8.9 %slice-start.13 = ((s8[4358144]{0:T(1024)(128)(4,1)}), s8[163840]{0:T(1024)(128)(4,1)S(1)}, s32[]{:S(2)}) async-start(s8[4358144]{0:T(1024)(128)(4,1)} %bitcast.349), calls=%async_computation.13 | async-start | bytes 327680
  160.2 7.2 %copy-start.52 = (bf16[1024,2432]{1,0:T(8,128)(2,1)S(1)}, bf16[1024,2432]{1,0:T(8,128)(2,1)}, u32[]{:S(2)}) copy-start(bf16[1024,2432]{1,0:T(8,128)(2,1)} %get-tuple-element.87) | copy-start | bytes 14942212
  167.4 14.0 %slice-start.18 = ((s8[4358144]{0:T(1024)(128)(4,1)}), s8[4194304]{0:T(1024)(128)(4,1)S(1)}, s32[]{:S(2)}) async-start(s8[4358144]{0:T(1024)(128)(4,1)} %bitcast.355), calls=%async_computation.18 | async-start | bytes 8388608
  167.4 21.6 %slice-start.20 = ((s8[4980736]{0:T(1024)(128)(4,1)}), s8[4194304]{0:T(1024)(128)(4,1)S(1)}, s32[]{:S(2)}) async-start(s8[4980736]{0:T(1024)(128)(4,1)} %bitcast.357), calls=%async_computation.20 | async-start | bytes 8388608
  173.9 7.5 %slice-start.19 = ((s8[4358144]{0:T(1024)(128)(4,1)}), s8[163840]{0:T(1024)(128)(4,1)S(1)}, s32[]{:S(2)}) async-start(s8[4358144]{0:T(1024)(128)(4,1)} %bitcast.355), calls=%async_computation.19 | async-start | bytes 327680
  173.9 15.2 %slice-start.21 = ((s8[4980736]{0:T(1024)(128)(4,1)}), s8[786432]{0:T(1024)(128)(4,1)S(1)}, s32[]{:S(2)}) async-start(s8[4980736]{0:T(1024)(128)(4,1)} %bitcast.357), calls=%async_computation.21 | async-start | bytes 1572864
  181.4 21.2 %copy-start.15 = (bf16[896,2432]{1,0:T(8,128)(2,1)}, bf16[896,2432]{1,0:T(8,128)(2,1)S(1)}, u32[]{:S(2)}) copy-start(bf16[896,2432]{1,0:T(8,128)(2,1)S(1)} %convolution_convert_fusion.1) | copy-start | bytes 13074436
  181.4 13.1 %slice-start.14 = ((s8[4358144]{0:T(1024)(128)(4,1)}), s8[4194304]{0:T(1024)(128)(4,1)S(1)}, s32[]{:S(2)}) async-start(s8[4358144]{0:T(1024)(128)(4,1)} %bitcast.351), calls=%async_computation.14 | async-start | bytes 8388608
  187.6 49.8 %collective-permute-start.3 = (bf16[512,896]{1,0:T(8,128)(2,1)S(1)}, bf16[512,896]{1,0:T(8,128)(2,1)S(1)}, u32[]{:S(2)}, u32[]{:S(2)}) collective-permute-start(bf16[512,896]{1,0:T(8,128)(2,1)S(1)} %fusion.60), channel_id=1, source_target_pairs={{0,1},{1,0},{2,3},{3,2},{4,5},{5,4},{6,7},{7,6},{8,9},{9,8},{10,11... | collective-permute-start | bytes 2752520 | tf_op jit(solution)/shard_map/ppermute | solution.py:103
  200.3 27.6 %collective-permute-start.5 = (bf16[512,896]{1,0:T(8,128)(2,1)S(1)}, bf16[512,896]{1,0:T(8,128)(2,1)S(1)}, u32[]{:S(2)}, u32[]{:S(2)}) collective-permute-start(bf16[512,896]{1,0:T(8,128)(2,1)S(1)} %add_convert_fusion), channel_id=1, source_target_pairs={{0,1},{1,0},{2,3},{3,2},{4,5},{5,4},{6,7},{7,6},{8,9},{9,8},{10,11... | collective-permute-start | bytes 2752520 | tf_op jit(solution)/shard_map/ppermute | solution.py:103
  204.2 23.8 %copy-start.53 = (f32[512,896]{1,0:T(8,128)S(1)}, f32[512,896]{1,0:T(8,128)}, u32[]{:S(2)}) copy-start(f32[512,896]{1,0:T(8,128)} %fusion.32) | copy-start | bytes 5505028
  211.7 23.6 %copy-start.16 = (bf16[896,2432]{1,0:T(8,128)(2,1)}, bf16[896,2432]{1,0:T(8,128)(2,1)S(1)}, u32[]{:S(2)}) copy-start(bf16[896,2432]{1,0:T(8,128)(2,1)S(1)} %convolution_convert_fusion) | copy-start | bytes 13074436
  234.2 19.7 %collective-permute-start.6 = (bf16[512,896]{1,0:T(8,128)(2,1)S(1)}, bf16[512,896]{1,0:T(8,128)(2,1)S(1)}, u32[]{:S(2)}, u32[]{:S(2)}) collective-permute-start(bf16[512,896]{1,0:T(8,128)(2,1)S(1)} %get-tuple-element.84), channel_id=1, source_target_pairs={{0,1},{1,0},{2,3},{3,2},{4,5},{5,4},{6,7},{7,6},{8,9},{9,8},{10,11... | collective-permute-start | bytes 2752520 | tf_op jit(solution)/shard_map/ppermute | solution.py:103
  236.8 81.0 %collective-permute-start.20 = (bf16[8,56,2432]{2,1,0:T(8,128)(2,1)}, bf16[8,56,2432]{2,1,0:T(8,128)(2,1)}, u32[]{:S(2)}, u32[]{:S(2)}) collective-permute-start(bf16[8,56,2432]{2,1,0:T(8,128)(2,1)} %dynamic-slice_bitcast_fusion), channel_id=1, source_target_pairs={{0,2},{2,0},{4,6},{6,4},{8,10},{10,8},{12,14},{14,12},{16,18},{18,... | collective-permute-start | bytes 6537224 | tf_op jit(solution)/shard_map/ppermute | solution.py:136
  236.8 85.6 %collective-permute-start.16 = (bf16[8,56,2432]{2,1,0:T(8,128)(2,1)}, bf16[8,56,2432]{2,1,0:T(8,128)(2,1)}, u32[]{:S(2)}, u32[]{:S(2)}) collective-permute-start(bf16[8,56,2432]{2,1,0:T(8,128)(2,1)} %dynamic-slice_bitcast_fusion.1), channel_id=1, source_target_pairs={{0,2},{2,0},{4,6},{6,4},{8,10},{10,8},{12,14},{14,12},{16,18},{18,... | collective-permute-start | bytes 6537224 | tf_op jit(solution)/shard_map/ppermute | solution.py:136
  237.3 89.9 %collective-permute-start.12 = (bf16[8,56,2432]{2,1,0:T(8,128)(2,1)}, bf16[8,56,2432]{2,1,0:T(8,128)(2,1)}, u32[]{:S(2)}, u32[]{:S(2)}) collective-permute-start(bf16[8,56,2432]{2,1,0:T(8,128)(2,1)} %dynamic-slice_bitcast_fusion.2), channel_id=1, source_target_pairs={{0,2},{2,0},{4,6},{6,4},{8,10},{10,8},{12,14},{14,12},{16,18},{18,... | collective-permute-start | bytes 6537224 | tf_op jit(solution)/shard_map/ppermute | solution.py:136
  242.9 11.2 %copy-start.21 = (bf16[1024,1,7,64]{0,3,2,1:T(8,128)(2,1)S(1)}, bf16[1024,1,7,64]{0,3,2,1:T(8,128)(2,1)}, u32[]{:S(2)}) copy-start(bf16[1024,1,7,64]{0,3,2,1:T(8,128)(2,1)} %copy-done.20) | copy-start | bytes 2752516
  263.7 9.3 %copy-start.13 = (bf16[1024,1,7,32]{0,3,2,1:T(8,128)(2,1)S(1)}, bf16[1024,1,7,32]{0,3,2,1:T(8,128)(2,1)}, u32[]{:S(2)}) copy-start(bf16[1024,1,7,32]{0,3,2,1:T(8,128)(2,1)} %copy-done.12) | copy-start | bytes 1376260
  263.7 16.6 %slice-start = ((s8[14680064]{0:T(1024)(128)(4,1)}), s8[4194304]{0:T(1024)(128)(4,1)S(1)}, s32[]{:S(2)}) async-start(s8[14680064]{0:T(1024)(128)(4,1)} %bitcast.299), calls=%async_computation | async-start | bytes 8388608
  263.7 16.6 %slice-start.1 = ((s8[14680064]{0:T(1024)(128)(4,1)}), s8[4194304]{0:T(1024)(128)(4,1)S(1)}, s32[]{:S(2)}) async-start(s8[14680064]{0:T(1024)(128)(4,1)} %bitcast.299), calls=%async_computation.1 | async-start | bytes 8388608
  263.7 16.6 %slice-start.2 = ((s8[14680064]{0:T(1024)(128)(4,1)}), s8[2097152]{0:T(1024)(128)(4,1)S(1)}, s32[]{:S(2)}) async-start(s8[14680064]{0:T(1024)(128)(4,1)} %bitcast.299), calls=%async_computation.2 | async-start | bytes 4194304
  273.0 7.2 %slice-start.3 = ((s8[14680064]{0:T(1024)(128)(4,1)}), s8[4194304]{0:T(1024)(128)(4,1)S(1)}, s32[]{:S(2)}) async-start(s8[14680064]{0:T(1024)(128)(4,1)} %bitcast.299), calls=%async_computation.3 | async-start | bytes 8388608
  295.4 7.5 %slice-start.6 = ((s8[7340032]{0:T(1024)(128)(4,1)}), s8[4194304]{0:T(1024)(128)(4,1)S(1)}, s32[]{:S(2)}) async-start(s8[7340032]{0:T(1024)(128)(4,1)} %bitcast.303), calls=%async_computation.6 | async-start | bytes 8388608
  312.5 9.9 %slice-start.10 = ((s8[4358144]{0:T(1024)(128)(4,1)}), s8[163840]{0:T(1024)(128)(4,1)S(1)}, s32[]{:S(2)}) async-start(s8[4358144]{0:T(1024)(128)(4,1)} %bitcast.319), calls=%async_computation.10 | async-start | bytes 327680
  315.7 19.1 %collective-permute-start.7 = (bf16[512,896]{1,0:T(8,128)(2,1)}, bf16[512,896]{1,0:T(8,128)(2,1)}, u32[]{:S(2)}, u32[]{:S(2)}) collective-permute-start(bf16[512,896]{1,0:T(8,128)(2,1)} %convolution_convert_fusion.6), channel_id=1, source_target_pairs={{0,1},{1,0},{2,3},{3,2},{4,5},{5,4},{6,7},{7,6},{8,9},{9,8},{10,11... | collective-permute-start | bytes 2752520 | tf_op jit(solution)/shard_map/ppermute | solution.py:103
  317.4 111.2 %collective-permute-start.8 = (bf16[8,56,1024]{2,1,0:T(8,128)(2,1)}, bf16[8,56,1024]{2,1,0:T(8,128)(2,1)}, u32[]{:S(2)}, u32[]{:S(2)}) collective-permute-start(bf16[8,56,1024]{2,1,0:T(8,128)(2,1)} %dynamic-slice_bitcast_fusion.6), channel_id=1, source_target_pairs={{0,2},{2,0},{4,6},{6,4},{8,10},{10,8},{12,14},{14,12},{16,18},{18,... | collective-permute-start | bytes 2752520 | tf_op jit(solution)/shard_map/ppermute | solution.py:136
  317.8 9.4 %slice-start.8 = ((s8[4358144]{0:T(1024)(128)(4,1)}), s8[4194304]{0:T(1024)(128)(4,1)S(1)}, s32[]{:S(2)}) async-start(s8[4358144]{0:T(1024)(128)(4,1)} %bitcast.315), calls=%async_computation.8 | async-start | bytes 8388608
  320.9 122.0 %collective-permute-start.21 = (bf16[4,56,2432]{2,1,0:T(8,128)(2,1)S(1)}, bf16[4,56,2432]{2,1,0:T(8,128)(2,1)}, u32[]{:S(2)}, u32[]{:S(2)}) collective-permute-start(bf16[4,56,2432]{2,1,0:T(8,128)(2,1)S(1)} %dynamic-slice_bitcast_fusion.3), channel_id=1, source_target_pairs={{0,4},{2,6},{4,0},{6,2},{8,12},{10,14},{12,8},{14,10},{16,20},{18,... | collective-permute-start | bytes 3268616 | tf_op jit(solution)/shard_map/ppermute | solution.py:136
  325.8 120.4 %collective-permute-start.17 = (bf16[4,56,2432]{2,1,0:T(8,128)(2,1)}, bf16[4,56,2432]{2,1,0:T(8,128)(2,1)}, u32[]{:S(2)}, u32[]{:S(2)}) collective-permute-start(bf16[4,56,2432]{2,1,0:T(8,128)(2,1)} %dynamic-slice_bitcast_fusion.4), channel_id=1, source_target_pairs={{0,4},{2,6},{4,0},{6,2},{8,12},{10,14},{12,8},{14,10},{16,20},{18,... | collective-permute-start | bytes 3268616 | tf_op jit(solution)/shard_map/ppermute | solution.py:136
  329.4 9.1 %copy-start.4 = (bf16[8,56,2432]{2,1,0:T(8,128)(2,1)}, bf16[8,56,2432]{2,1,0:T(8,128)(2,1)S(1)}, u32[]{:S(2)}) copy-start(bf16[8,56,2432]{2,1,0:T(8,128)(2,1)S(1)} %fusion.20) | copy-start | bytes 6537220
  330.5 117.9 %collective-permute-start.13 = (bf16[4,56,2432]{2,1,0:T(8,128)(2,1)}, bf16[4,56,2432]{2,1,0:T(8,128)(2,1)}, u32[]{:S(2)}, u32[]{:S(2)}) collective-permute-start(bf16[4,56,2432]{2,1,0:T(8,128)(2,1)} %dynamic-slice_bitcast_fusion.5), channel_id=1, source_target_pairs={{0,4},{2,6},{4,0},{6,2},{8,12},{10,14},{12,8},{14,10},{16,20},{18,... | collective-permute-start | bytes 3268616 | tf_op jit(solution)/shard_map/ppermute | solution.py:136
  338.5 95.7 %copy-start.46 = (f32[512]{0:T(512)S(1)}, f32[512]{0:T(512)}, u32[]{:S(2)}) copy-start(f32[512]{0:T(512)} %get-tuple-element.115) | copy-start | bytes 6148
  430.7 11.5 %collective-permute-start.9 = (bf16[4,56,1024]{2,1,0:T(8,128)(2,1)S(1)}, bf16[4,56,1024]{2,1,0:T(8,128)(2,1)S(1)}, u32[]{:S(2)}, u32[]{:S(2)}) collective-permute-start(bf16[4,56,1024]{2,1,0:T(8,128)(2,1)S(1)} %dynamic-slice_bitcast_fusion.10), channel_id=1, source_target_pairs={{0,4},{2,6},{4,0},{6,2},{8,12},{10,14},{12,8},{14,10},{16,20},{18,... | collective-permute-start | bytes 1376264 | tf_op jit(solution)/shard_map/ppermute | solution.py:136
  434.3 8.7 %copy-start.7 = (bf16[8,56,2432]{2,1,0:T(8,128)(2,1)S(1)}, bf16[8,56,2432]{2,1,0:T(8,128)(2,1)}, u32[]{:S(2)}) copy-start(bf16[8,56,2432]{2,1,0:T(8,128)(2,1)} %copy-done.6) | copy-start | bytes 6537220
  442.4 9.8 %collective-permute-start.10 = (bf16[2,56,1024]{2,1,0:T(8,128)(2,1)S(1)}, bf16[2,56,1024]{2,1,0:T(8,128)(2,1)S(1)}, u32[]{:S(2)}, u32[]{:S(2)}) collective-permute-start(bf16[2,56,1024]{2,1,0:T(8,128)(2,1)S(1)} %dynamic-slice_bitcast_fusion.11), channel_id=1, source_target_pairs={{0,8},{2,10},{4,12},{6,14},{8,0},{10,2},{12,4},{14,6},{16,24},{18,... | collective-permute-start | bytes 688136 | tf_op jit(solution)/shard_map/ppermute | solution.py:136
  444.6 31.5 %collective-permute-start.22 = (bf16[2,56,2432]{2,1,0:T(8,128)(2,1)S(1)}, bf16[2,56,2432]{2,1,0:T(8,128)(2,1)S(1)}, u32[]{:S(2)}, u32[]{:S(2)}) collective-permute-start(bf16[2,56,2432]{2,1,0:T(8,128)(2,1)S(1)} %dynamic-slice_bitcast_fusion.7), channel_id=1, source_target_pairs={{0,8},{2,10},{4,12},{6,14},{8,0},{10,2},{12,4},{14,6},{16,24},{18,... | collective-permute-start | bytes 1634312 | tf_op jit(solution)/shard_map/ppermute | solution.py:136
  447.7 37.0 %collective-permute-start.18 = (bf16[2,56,2432]{2,1,0:T(8,128)(2,1)S(1)}, bf16[2,56,2432]{2,1,0:T(8,128)(2,1)S(1)}, u32[]{:S(2)}, u32[]{:S(2)}) collective-permute-start(bf16[2,56,2432]{2,1,0:T(8,128)(2,1)S(1)} %dynamic-slice_bitcast_fusion.8), channel_id=1, source_target_pairs={{0,8},{2,10},{4,12},{6,14},{8,0},{10,2},{12,4},{14,6},{16,24},{18,... | collective-permute-start | bytes 1634312 | tf_op jit(solution)/shard_map/ppermute | solution.py:136
  452.3 22.4 %collective-permute-start.11 = (bf16[1,56,1024]{2,1,0:T(8,128)(2,1)S(1)}, bf16[1,56,1024]{2,1,0:T(8,128)(2,1)S(1)}, u32[]{:S(2)}, u32[]{:S(2)}) collective-permute-start(bf16[1,56,1024]{2,1,0:T(8,128)(2,1)S(1)} %constant_dynamic-slice_fusion.3), channel_id=1, source_target_pairs={{0,16},{2,18},{4,20},{6,22},{8,24},{10,26},{12,28},{14,30},{16,0},... | collective-permute-start | bytes 344072 | tf_op jit(solution)/shard_map/ppermute | solution.py:136
  452.5 41.7 %collective-permute-start.14 = (bf16[2,56,2432]{2,1,0:T(8,128)(2,1)S(1)}, bf16[2,56,2432]{2,1,0:T(8,128)(2,1)S(1)}, u32[]{:S(2)}, u32[]{:S(2)}) collective-permute-start(bf16[2,56,2432]{2,1,0:T(8,128)(2,1)S(1)} %dynamic-slice_bitcast_fusion.9), channel_id=1, source_target_pairs={{0,8},{2,10},{4,12},{6,14},{8,0},{10,2},{12,4},{14,6},{16,24},{18,... | collective-permute-start | bytes 1634312 | tf_op jit(solution)/shard_map/ppermute | solution.py:136
  476.3 18.1 %collective-permute-start.23 = (bf16[1,56,2432]{2,1,0:T(8,128)(2,1)S(1)}, bf16[1,56,2432]{2,1,0:T(8,128)(2,1)S(1)}, u32[]{:S(2)}, u32[]{:S(2)}) collective-permute-start(bf16[1,56,2432]{2,1,0:T(8,128)(2,1)S(1)} %constant_dynamic-slice_fusion), channel_id=1, source_target_pairs={{0,16},{2,18},{4,20},{6,22},{8,24},{10,26},{12,28},{14,30},{16,0},... | collective-permute-start | bytes 817160 | tf_op jit(solution)/shard_map/ppermute | solution.py:136
  484.9 24.1 %collective-permute-start.19 = (bf16[1,56,2432]{2,1,0:T(8,128)(2,1)S(1)}, bf16[1,56,2432]{2,1,0:T(8,128)(2,1)S(1)}, u32[]{:S(2)}, u32[]{:S(2)}) collective-permute-start(bf16[1,56,2432]{2,1,0:T(8,128)(2,1)S(1)} %constant_dynamic-slice_fusion.1), channel_id=1, source_target_pairs={{0,16},{2,18},{4,20},{6,22},{8,24},{10,26},{12,28},{14,30},{16,0},... | collective-permute-start | bytes 817160 | tf_op jit(solution)/shard_map/ppermute | solution.py:136
  494.4 17.7 %collective-permute-start.15 = (bf16[1,56,2432]{2,1,0:T(8,128)(2,1)S(1)}, bf16[1,56,2432]{2,1,0:T(8,128)(2,1)S(1)}, u32[]{:S(2)}, u32[]{:S(2)}) collective-permute-start(bf16[1,56,2432]{2,1,0:T(8,128)(2,1)S(1)} %constant_dynamic-slice_fusion.2), channel_id=1, source_target_pairs={{0,16},{2,18},{4,20},{6,22},{8,24},{10,26},{12,28},{14,30},{16,0},... | collective-permute-start | bytes 817160 | tf_op jit(solution)/shard_map/ppermute | solution.py:136
  (36 other events, 136.1 us)

commit v2 on v1

--- a/solution.py
+++ b/solution.py
@@ -122,23 +122,48 @@
     return partial_of(me) + sent.astype(jnp.float32)
 
 
-def dp_sum_rows(partial):
+def dp_bits(last_first):
     count = lax.axis_size("dp")
-    me = lax.axis_index("dp")
-    rows = partial.shape[0] // count
-    current = partial.reshape(count, rows, partial.shape[1])
+    bits = []
     step = 1
     while step < count:
-        bit = (me // step) % 2
-        pairs = current.reshape(current.shape[0] // 2, 2, rows, partial.shape[1])
-        sent = lax.dynamic_index_in_dim(pairs, 1 - bit, axis=1, keepdims=False)
-        kept = lax.dynamic_index_in_dim(pairs, bit, axis=1, keepdims=False)
-        got = lax.ppermute(sent, "dp", [(i, i ^ step) for i in range(count)])
-        current = kept.astype(jnp.float32) + got.astype(jnp.float32)
+        bits.append(step)
         step *= 2
-        if step < count:
-            current = current.astype(jnp.bfloat16)
+    if last_first:
+        bits = bits[:1] + bits[2:] + bits[1:2]
+    return bits
+
+
+def dp_blocks(partial):
+    count = lax.axis_size("dp")
+    return partial.reshape(count, partial.shape[0] // count, partial.shape[1])
+
+
+def dp_stage(current, bits, at):
+    count = lax.axis_size("dp")
+    step = bits[at]
+    low = 2 ** sum(1 for later in bits[at + 1 :] if later < step)
+    blocks, rows, columns = current.shape
+    bit = (lax.axis_index("dp") // step) % 2
+    pairs = current.reshape(blocks // (2 * low), 2, low, rows, columns)
+    sent = lax.dynamic_index_in_dim(pairs, 1 - bit, axis=1, keepdims=False)
+    kept = lax.dynamic_index_in_dim(pairs, bit, axis=1, keepdims=False)
+    sent = sent.reshape(blocks // 2, rows, columns)
+    kept = kept.reshape(blocks // 2, rows, columns)
+    got = lax.ppermute(sent, "dp", [(i, i ^ step) for i in range(count)])
+    total = kept.astype(jnp.float32) + got.astype(jnp.float32)
+    return total if at == len(bits) - 1 else total.astype(jnp.bfloat16)
+
+
+def dp_rest(current, bits, at):
+    while at < len(bits):
+        current = dp_stage(current, bits, at)
+        at += 1
     return current[0]
+
+
+def after(value, *earlier):
+    return lax.optimization_barrier((value,) + earlier)
 
 
 def shards(
@@ -169,7 +194,6 @@
     normed_one = gather_pair(normed_one.astype(jnp.bfloat16))
     cot_sent, _ = lax.optimization_barrier((cotangent, normed_one))
     cot_group = gather_pair(cot_sent)
-    d_mixed = lax.optimization_barrier(times_transpose(cot_group, down_weight))
     projected = jnp.dot(normed_one, qkv_weight, preferred_element_type=jnp.float32) + qkv_bias
     query_rows = projected[:, :query_columns].reshape(
         group_rows, kv_local, heads_per_group, HEAD_WIDTH
@@ -221,36 +245,61 @@
     context = (
         jnp.concatenate(contexts, axis=0).reshape(group_rows, query_columns).astype(jnp.bfloat16)
     )
+    context, cot_group = after(context, cot_group)
     hidden_one = token_vals + sum_pair(
         lambda t: jnp.dot(half_rows(context, t), out_weight, preferred_element_type=jnp.float32)
     )
     rms_two, normed_two = rms_forward(hidden_one, norm2_gain)
-    normed_two = gather_pair(normed_two.astype(jnp.bfloat16))
+    d_mixed = times_transpose(cot_group, down_weight)
+    normed_two, d_mixed = after(gather_pair(normed_two.astype(jnp.bfloat16)), d_mixed)
     gate_pre = jnp.dot(normed_two, gate_weight, preferred_element_type=jnp.float32)
     up_pre = jnp.dot(normed_two, up_weight, preferred_element_type=jnp.float32)
     activated = jax.nn.silu(gate_pre)
     mixed = (activated * up_pre).astype(jnp.bfloat16)
-    block_result = (
-        hidden_one
-        + sum_pair(
-            lambda t: jnp.dot(half_rows(mixed, t), down_weight, preferred_element_type=jnp.float32)
-        )
-    ).astype(jnp.bfloat16)
-    down_grad = contract_rows(cot_group, mixed).astype(jnp.bfloat16)
     sigmoid_gate = jax.nn.sigmoid(gate_pre)
     d_gate = (d_mixed * up_pre * sigmoid_gate * (1.0 + gate_pre * (1.0 - sigmoid_gate))).astype(
         jnp.bfloat16
     )
     d_up = (d_mixed * activated).astype(jnp.bfloat16)
+    me = lax.axis_index("tensor")
+    other_part = (
+        times_transpose(half_rows(d_gate, 1 - me), gate_weight)
+        + times_transpose(half_rows(d_up, 1 - me), up_weight)
+    ).astype(jnp.bfloat16)
+    d_normed_sent = pair_swap(other_part)
+    mixed, d_gate, d_up, other_part = after(mixed, d_gate, d_up, other_part)
+    own_part = times_transpose(half_rows(d_gate, me), gate_weight) + times_transpose(
+        half_rows(d_up, me), up_weight
+    )
+    down_grad = contract_rows(cot_group, mixed).astype(jnp.bfloat16)
     gate_grad = contract_rows(normed_two, d_gate).astype(jnp.bfloat16)
-    up_grad = contract_rows(normed_two, d_up).astype(jnp.bfloat16)
-    d_normed_two = sum_pair(
-        lambda t: times_transpose(half_rows(d_gate, t), gate_weight)
-        + times_transpose(half_rows(d_up, t), up_weight)
-    )
+    own_part, d_normed_sent, down_grad, gate_grad = after(
+        own_part, d_normed_sent, down_grad, gate_grad
+    )
+    d_normed_two = own_part + d_normed_sent.astype(jnp.float32)
+    bits_x = dp_bits(False)
+    bits_z = dp_bits(True)
+    down_sum = dp_stage(dp_blocks(down_grad), bits_x, 0)
+    gate_sum = dp_stage(dp_blocks(gate_grad), bits_z, 0)
     d_hidden_norm, gain_two_grad = rms_backward(hidden_one, rms_two, norm2_gain, d_normed_two)
     d_hidden = cotangent.astype(jnp.float32) + d_hidden_norm
-    d_resid = gather_pair(d_hidden.astype(jnp.bfloat16))
+    d_resid_own = d_hidden.astype(jnp.bfloat16)
+    d_up, mixed, d_resid_own = after(d_up, mixed, d_resid_own)
+    d_resid = gather_pair(d_resid_own)
+    up_grad = contract_rows(normed_two, d_up).astype(jnp.bfloat16)
+    block_sent = jnp.dot(
+        half_rows(mixed, 1 - me), down_weight, preferred_element_type=jnp.float32
+    ).astype(jnp.bfloat16)
+    block_own = jnp.dot(half_rows(mixed, me), down_weight, preferred_element_type=jnp.float32)
+    d_resid, up_grad, block_sent, block_own, down_sum, gate_sum = after(
+        d_resid, up_grad, block_sent, block_own, down_sum, gate_sum
+    )
+    up_sum = dp_stage(dp_blocks(up_grad), bits_x, 0)
+    down_sum = dp_stage(down_sum, bits_x, 1)
+    gate_sum = dp_stage(gate_sum, bits_z, 1)
+    block_result = (hidden_one + (block_own + pair_swap(block_sent).astype(jnp.float32))).astype(
+        jnp.bfloat16
+    )
     out_grad = contract_rows(d_resid, context).astype(jnp.bfloat16)
     d_context = (
         times_transpose(d_resid, out_weight)
@@ -287,6 +336,13 @@
             )
             * score_scale
         )
+        if block_id == 0:
+            d_scores, d_context, up_sum, down_sum, gate_sum, block_result = after(
+                d_scores, d_context, up_sum, down_sum, gate_sum, block_result
+            )
+            up_sum = dp_stage(up_sum, bits_x, 1)
+            down_sum = dp_stage(down_sum, bits_x, 2)
+            gate_sum = dp_stage(gate_sum, bits_z, 2)
         d_keys = d_keys.at[:row_end].add(
             jnp.einsum(
                 "jgqk,qjgd->kjd",
@@ -313,34 +369,40 @@
         ],
         axis=1,
     ).astype(jnp.bfloat16)
+    d_proj, up_sum, down_sum, gate_sum = after(d_proj, up_sum, down_sum, gate_sum)
     qkv_grad = contract_rows(normed_one, d_proj).astype(jnp.bfloat16)
     bias_grad = jnp.sum(d_proj, axis=0, dtype=jnp.float32)
     d_normed_one = sum_pair(lambda t: times_transpose(half_rows(d_proj, t), qkv_weight))
     d_token_norm, gain_one_grad = rms_backward(token_vals, rms_one, norm1_gain, d_normed_one)
     tokens_grad = d_hidden + d_token_norm
-    down_grad = dp_sum_rows(down_grad).T
-    gate_grad = dp_sum_rows(gate_grad)
-    up_grad = dp_sum_rows(up_grad)
-    small = dp_sum_rows(jnp.concatenate([qkv_grad, out_grad], axis=1))
-    qkv_grad = small[:, : qkv_weight.shape[1]]
-    out_grad = small[:, qkv_weight.shape[1] :].T
-    me = lax.axis_index("tensor")
+    up_grad = dp_rest(up_sum, bits_x, 2)
+    down_grad = dp_rest(down_sum, bits_x, 3).T
+    gate_grad = dp_rest(gate_sum, bits_z, 3)
     width = norm1_gain.shape[0]
+    count = lax.axis_size("dp")
+    share = width // count
     bias_columns = bias_grad.shape[0]
-    placed_bias = lax.dynamic_update_slice_in_dim(
-        jnp.zeros((bias_columns * lax.axis_size("tensor"),), jnp.float32),
-        bias_grad,
-        me * bias_columns,
-        axis=0,
-    )
-    sums = lax.psum(
-        jnp.concatenate([gain_one_grad, gain_two_grad, placed_bias]), ("dp", "tensor")
-    )
-    share = width // lax.axis_size("dp")
+    values = jnp.concatenate([gain_one_grad, gain_two_grad, bias_grad]).astype(jnp.bfloat16)
+    lanes = -(-values.shape[0] // (share * 128)) * 128
+    values = jnp.pad(values, (0, share * lanes - values.shape[0])).reshape(1, share, lanes)
+    values = jnp.broadcast_to(values, (count, share, lanes))
+    small = jnp.concatenate([dp_blocks(qkv_grad), dp_blocks(out_grad), values], axis=2)
+    small = dp_rest(small, bits_x, 0)
+    columns = qkv_weight.shape[1]
+    qkv_grad = small[:, :columns]
+    out_grad = small[:, columns : columns + query_columns].T
+    sums = small[:, columns + query_columns :].reshape(-1)
     gain_at = lax.axis_index("dp") * share
-    gain_one_grad = lax.dynamic_slice_in_dim(sums, gain_at, share)
-    gain_two_grad = lax.dynamic_slice_in_dim(sums, width + gain_at, share)
-    bias_grad = lax.dynamic_slice_in_dim(sums, 2 * width + me * bias_columns, bias_columns)
+    gain_mine = jnp.concatenate(
+        [
+            lax.dynamic_slice_in_dim(sums, gain_at, share),
+            lax.dynamic_slice_in_dim(sums, width + gain_at, share),
+        ]
+    )
+    gain_mine = gain_mine + pair_swap(gain_mine)
+    gain_one_grad = gain_mine[:share]
+    gain_two_grad = gain_mine[share:]
+    bias_grad = sums[2 * width : 2 * width + bias_columns]
     return (
         block_result,
         tokens_grad,

time: 520 us -> 395 us (0.76)
  blocking collectives: 90.1 us -> 0 us
  waiting for transfers between devices: 160 us -> 123 us
  local copies, waits for them, and re-layouts: 19.8 us -> 32.9 us
  matrix products: 151 us -> 140 us
    psum x1 -> x0, blocking collectives: 90.1 us -> none  [shards(): lax.psum(jnp.concatenate([gain_one_grad, gain_two_grad, placed_bias]), ('...]
    ppermute x16, waiting for transfers between devices: 57.2 us -> 37.5 us  [dp_stage(): got = lax.ppermute(sent, 'dp', [(i, i ^ step) for i in range(count)])]
    ppermute x8 -> x9, waiting for transfers between devices: 103 us -> 85.2 us  [pair_swap(): return lax.ppermute(block, 'tensor', [(0, 1), (1, 0)])]
    convert_element_type x14 -> x16, other arithmetic: 18.6 us -> 31.4 us  [the longest x12 17 us: dp_stage(): return total if at == len(bits) - 1 else total.astype(jnp.bfloat16)]
    another operation x7 -> x6, other arithmetic: 20.5 us -> 8.99 us
    reshape x0 -> x12, local copies, waits for them, and re-layouts: none -> 11.1 us  [the longest x11 11.1 us: dp_stage(): sent = sent.reshape(blocks // 2, rows, columns)]
    squeeze x16 -> x0, local copies, waits for them, and re-layouts: 8.35 us -> none  [dp_sum_rows(): sent = lax.dynamic_index_in_dim(pairs, 1 - bit, axis=1, keepdims=False)]
    dot_general x8, matrix products: 39.5 us -> 32.7 us  [times_transpose(): lax.dot_general(left, right, (((1,), (1,)), ((), ())), preferred_element_...]
  transfers between devices with their start and end apart: 24 -> 25, of which waited for: 14 -> 14; matrix products, arithmetic and copies ran while one was open for 25% -> 28% of each run, Pallas kernels for 0% -> 0%
where the time goes in v2:
time: 395 us; the launch traced here: 388 us
  matrix products  140 us (35%)
  waiting for transfers between devices  123 us (31%)
  other arithmetic  67.7 us (17%)
  local copies, waits for them, and re-layouts  32.9 us (8%)
  starting transfers between devices  22.1 us (6%)
    ppermute x9, waiting for transfers between devices, pair_swap(): return lax.ppermute(block, 'tensor', [(0, 1), (1, 0)])  85.2 us
    ppermute x16, waiting for transfers between devices, dp_stage(): got = lax.ppermute(sent, 'dp', [(i, i ^ step) for i in range(count)])  37.5 us
    dot_general x8, matrix products, times_transpose(): lax.dot_general(left, right, (((1,), (1,)), ((), ())), preferred_element_...  32.7 us
    dot_general x5, matrix products, contract_rows(): lax.dot_general(left, right, (((0,), (0,)), ((), ())), preferred_element_...  25.1 us
    dot_general x1, matrix products, shards(): jnp.dot(normed_two, gate_weight, preferred_element_type=jnp.float32)  18.9 us
    convert_element_type x12, other arithmetic, dp_stage(): return total if at == len(bits) - 1 else total.astype(jnp.bfloat16)  17 us
    ppermute x16, starting transfers between devices, dp_stage(): got = lax.ppermute(sent, 'dp', [(i, i ^ step) for i in range(count)])  13 us
    dot_general x2, matrix products, shards(): jnp.einsum('qjgd,kjd->jgqk', d_block, value_matrix[:row_end], preferred_e...  13 us
  transfers between devices with their start and end apart: 25, of which 14 were waited for; matrix products, arithmetic and copies ran while one was open for 28% of the time, Pallas kernels for 0%

profile of v2, /device:TPU:0, one launch (start us, length us, event | category | flops | bytes accessed | tf_op | source)
XLA Modules:
  0.0 388.0 jit_solution(14610240141878345106)
XLA Ops:
  2.9 2.4 fusion.52
  5.3 3.0 collective-permute-start
  10.5 19.2 %collective-permute-done = bf16[512,896]{1,0:T(8,128)(2,1)} collective-permute-done((bf16[512,896]{1,0:T(8,128)(2,1)}, bf16[512,896]{1,0:T(8,128)(2,1)}, u32[]{:S(2)}, u32[]{:S(2)}) %collective-permute-start) | collective-permute-done | bytes 917536 | tf_op jit(solution)/shard_map/ppermute | solution.py:103
  29.7 18.8 %collective-permute-done.1 = bf16[512,896]{1,0:T(8,128)(2,1)} collective-permute-done((bf16[512,896]{1,0:T(8,128)(2,1)S(1)}, bf16[512,896]{1,0:T(8,128)(2,1)}, u32[]{:S(2)}, u32[]{:S(2)}) %collective-permute-start.1) | collective-permute-done | bytes 917536 | tf_op jit(solution)/shard_map/ppermute | solution.py:103
  48.6 2.1 broadcast_select_fusion.5
  55.7 1.9 copy-done.1
  59.0 7.0 %fusion.189 = (f32[7,512]{1,0:T(8,128)S(1)}, f32[1,7,512,1024]{2,3,1,0:T(8,128)}) fusion(bf16[1024,1,7,32]{0,3,2,1:T(8,128)(2,1)S(1)} %get-tuple-element.152, bf16[1024,1,7,32]{0,3,2,1:T(8,128)(2,1)S(1)} %get-tuple-element.151, bf16[1024,32]{0,1:T(8,128)(2,1)S(1)} %bitcast.362, bf16[1024,32]{0,1:T(8,128)(2,1)S(1)} %bitcast.360, ...), kind=kOutput, calls=%fused_computation.284 | convolution fusion | flops 481948160 | bytes 16267264 | tf_op jit(solution)/shard_map/qjgd,kjd->jgqk/dot_general | solution.py:222
  66.1 7.2 %fusion.3 = f32[7,512]{1,0:T(8,128)S(1)} fusion(f32[1,7,512,1024]{2,3,1,0:T(8,128)} %get-tuple-element.180, f32[7,512]{1,0:T(8,128)S(1)} %get-tuple-element.179), kind=kLoop, calls=%fused_computation.9 | loop fusion | flops 7336448 | bytes 14708736 | tf_op jit(solution)/shard_map/reduce_sum | solution.py:233
  73.2 6.6 %fusion.80 = bf16[512,1,7,64]{0,3,2,1:T(8,128)(2,1)S(1)} fusion(f32[7,512]{1,0:T(8,128)S(1)} %fusion.3, f32[1,7,512,1024]{2,3,1,0:T(8,128)} %get-tuple-element.180, f32[7,512]{1,0:T(8,128)S(1)} %get-tuple-element.179, bf16[1024,576]{0,1:T(8,128)(2,1)S(1)} %get-tuple-element.181), kind=kOutput, calls=%fused_computation.123 | convolution fusion | flops 481001472 | bytes 15302656 | tf_op jit(solution)/shard_map/jgqk,kjd->qjgd/dot_general | solution.py:238
  83.0 1.8 collective-permute-start.2
  84.9 19.9 %collective-permute-done.2 = bf16[512,896]{1,0:T(8,128)(2,1)} collective-permute-done((bf16[512,896]{1,0:T(8,128)(2,1)S(1)}, bf16[512,896]{1,0:T(8,128)(2,1)}, u32[]{:S(2)}, u32[]{:S(2)}) %collective-permute-start.2) | collective-permute-done | bytes 917536 | tf_op jit(solution)/shard_map/ppermute | solution.py:103
  104.8 2.7 multiply_reduce_fusion.2
  109.3 10.2 %fusion.192 = f32[1024,2432]{1,0:T(8,128)} fusion(bf16[1024,896]{1,0:T(8,128)(2,1)S(1)} %copy-done.26, bf16[2432,896]{1,0:T(8,128)(2,1)} %param.35), kind=kOutput, calls=%fused_computation.287 | convolution fusion | flops 4462739456 | bytes 16154624 | tf_op jit(solution)/shard_map/dot_general | solution.py:97
  119.5 9.0 %collective-permute-done.3 = bf16[512,896]{1,0:T(8,128)(2,1)S(1)} collective-permute-done((bf16[512,896]{1,0:T(8,128)(2,1)S(1)}, bf16[512,896]{1,0:T(8,128)(2,1)S(1)}, u32[]{:S(2)}, u32[]{:S(2)}) %collective-permute-start.3) | collective-permute-done | bytes 917536 | tf_op jit(solution)/shard_map/ppermute | solution.py:103
  129.1 7.9 %fusion.193 = f32[1024,2432]{1,0:T(8,128)} fusion(bf16[1024,896]{1,0:T(8,128)(2,1)S(1)} %pad_maximum_fusion.2, bf16[896,2432]{1,0:T(8,128)(2,1)S(1)} %bitcast.368), kind=kOutput, calls=%fused_computation.288 | convolution fusion | flops 4462739456 | bytes 16154624 | tf_op jit(solution)/shard_map/dot_general | solution.py:256
  137.0 18.9 %multiply_convert_fusion = (bf16[1024,2432]{1,0:T(8,128)(2,1)}, bf16[1024,2432]{1,0:T(8,128)(2,1)}, bf16[1024,2432]{1,0:T(8,128)(2,1)}) fusion(f32[1024,2432]{1,0:T(8,128)} %fusion.192, f32[1024,2432]{1,0:T(8,128)} %fusion.193, bf16[1024,896]{1,0:T(8,128)(2,1)S(1)} %pad_maximum_fusion.2, bf16[896,2432]{1,0:T(8,128)(2,1)} %param.33), kind=kOutput, calls=%fused_computation.11 | convolution fusion | flops 4500094976 | bytes 41058304 | tf_op jit(solution)/shard_map/dot_general | solution.py:255
  156.0 6.0 %fusion.39 = f32[512,896]{1,0:T(8,128)S(1)} fusion(bf16[896,2432]{1,0:T(8,128)(2,1)} %param.34, bf16[1024,2432]{1,0:T(8,128)(2,1)} %get-tuple-element.116, s32[]{:T(128)S(6)} %select_n.221), kind=kOutput, calls=%fused_computation.65 | convolution fusion | flops 2231369728 | bytes 8683524 | tf_op jit(solution)/shard_map/dot_general | solution.py:97
  162.0 5.2 %add_convert_fusion.1 = bf16[512,896]{1,0:T(8,128)(2,1)S(1)} fusion(f32[512,896]{1,0:T(8,128)S(1)} %fusion.39, bf16[896,2432]{1,0:T(8,128)(2,1)} %param.33, bf16[1024,2432]{1,0:T(8,128)(2,1)S(1)} %copy-done.61, s32[]{:T(128)S(6)} %select_n.221), kind=kOutput, calls=%fused_computation.106 | convolution fusion | flops 2232287232 | bytes 9601028 | tf_op jit(solution)/shard_map/dot_general | solution.py:97
  168.4 2.8 fusion.35
  171.3 5.3 %convolution_convert_fusion.1 = bf16[896,2432]{1,0:T(8,128)(2,1)S(1)} fusion(bf16[1024,896]{1,0:T(8,128)(2,1)S(1)} %pad_maximum_fusion.2, bf16[1024,2432]{1,0:T(8,128)(2,1)S(1)} %copy-done.61), kind=kOutput, calls=%fused_computation.34 | convolution fusion | flops 4464918528 | bytes 11173888 | tf_op jit(solution)/shard_map/dot_general | solution.py:91
  176.6 2.8 fusion.61
  179.5 5.5 %convolution_convert_fusion.2 = bf16[896,2432]{1,0:T(8,128)(2,1)S(1)} fusion(bf16[1024,896]{1,0:T(8,128)(2,1)S(1)} %copy-done.26, bf16[1024,2432]{1,0:T(8,128)(2,1)S(1)} %bitcast.378), kind=kOutput, calls=%fused_computation.35 | convolution fusion | flops 4464918528 | bytes 11173888 | tf_op jit(solution)/shard_map/dot_general | solution.py:91
  185.0 2.0 collective-permute-done.4
  188.2 2.0 fusion.185
  190.2 3.7 fusion.64
  195.6 4.1 %fusion.31 = f32[512,896]{1,0:T(8,128)} fusion(bf16[2432,896]{1,0:T(8,128)(2,1)S(1)} %bitcast.374, bf16[1024,2432]{1,0:T(8,128)(2,1)S(1)} %bitcast.380, s32[]{:T(128)S(6)} %select_n.220), kind=kOutput, calls=%fused_computation.57 | convolution fusion | flops 2231369728 | bytes 8683524 | tf_op jit(solution)/shard_map/dot_general | solution.py:293
  199.7 10.0 %convolution_convert_fusion = bf16[896,2432]{1,0:T(8,128)(2,1)} fusion(bf16[1024,896]{1,0:T(8,128)(2,1)S(1)} %pad_maximum_fusion.2, bf16[1024,2432]{1,0:T(8,128)(2,1)} %get-tuple-element.116), kind=kOutput, calls=%fused_computation.33 | convolution fusion | flops 4464918528 | bytes 11173888 | tf_op jit(solution)/shard_map/dot_general | solution.py:91
  209.6 3.0 collective-permute-done.5
  213.0 1.9 fusion.20
  214.9 2.0 fusion.19
  216.9 2.0 convolution_convert_fusion.7
  221.0 1.9 fusion.104
  222.9 5.2 %fusion.10 = (f32[7,512]{1,0:T(8,128)S(1)}, f32[512,512,7]{1,0,2:T(8,128)}) fusion(f32[1,7,512,512]{2,3,1,0:T(8,128)S(1)} %bitcast.327, f32[7,512]{1,0:T(8,128)S(1)} %log_add_fusion.1, bf16[512,7,64]{0,2,1:T(8,128)(2,1)S(1)} %bitcast.350, bf16[1024,576]{0,1:T(8,128)(2,1)} %copy-done.51), kind=kOutput, calls=%fused_computation.22 | convolution fusion | flops 240382464 | bytes 15233024 | tf_op jit(solution)/shard_map/qjgd,kjd->jgqk/dot_general | solution.py:328
  228.2 2.2 copy.67
  230.8 2.3 dynamic-slice_bitcast_fusion.4
  234.7 3.2 dynamic-slice_bitcast_fusion
  241.1 9.4 %fusion.12 = bf16[1,7,512,512]{2,3,1,0:T(8,128)(2,1)} fusion(f32[512,512,7]{1,0,2:T(8,128)} %get-tuple-element.188, f32[1,7,512,512]{2,3,1,0:T(8,128)} %copy-done.1, f32[7,512]{1,0:T(8,128)S(1)} %get-tuple-element.187, f32[7,512]{1,0:T(8,128)S(1)} %log_add_fusion.1), kind=kLoop, calls=%fused_computation.24 | loop fusion | flops 7340032 | bytes 18378752 | tf_op jit(solution)/shard_map/convert_element_type | solution.py:332
  250.5 3.9 fusion.70
  254.4 2.8 add_convert_fusion
  258.8 3.4 collective-permute-done.10
  263.8 2.9 fusion.18
  266.7 7.7 %fusion = (f32[7,512]{1,0:T(8,128)S(1)}, f32[1024,512,7]{1,0,2:T(8,128)}) fusion(f32[1,7,512,1024]{2,3,1,0:T(8,128)S(1)} %bitcast.325, f32[7,512]{1,0:T(8,128)S(1)} %log_add_fusion, bf16[1024,1,7,64]{0,3,2,1:T(8,128)(2,1)S(1)} %bitcast.353, bf16[1024,576]{0,1:T(8,128)(2,1)} %copy-done.51), kind=kOutput, calls=%fused_computation.3 | convolution fusion | flops 480768512 | bytes 29980672 | tf_op jit(solution)/shard_map/qjgd,kjd->jgqk/dot_general | solution.py:328
  274.5 3.0 fusion.98
  280.4 2.6 collective-permute-start.14
  285.4 7.1 %fusion.9 = bf16[7,512,1024]{1,2,0:T(8,128)(2,1)S(1)} fusion(f32[1024,512,7]{1,0,2:T(8,128)} %get-tuple-element.190, f32[1,7,512,1024]{2,3,1,0:T(8,128)S(1)} %bitcast.325, f32[7,512]{1,0:T(8,128)S(1)} %get-tuple-element.189, f32[7,512]{1,0:T(8,128)S(1)} %log_add_fusion), kind=kLoop, calls=%fused_computation.18 | loop fusion | flops 14680064 | bytes 36728832 | tf_op jit(solution)/shard_map/reshape.221
  294.0 2.3 fusion.91
  297.9 8.4 %collective-permute-done.13 = bf16[2,56,2432]{2,1,0:T(8,128)(2,1)S(1)} collective-permute-done((bf16[2,56,2432]{2,1,0:T(8,128)(2,1)}, bf16[2,56,2432]{2,1,0:T(8,128)(2,1)S(1)}, u32[]{:S(2)}, u32[]{:S(2)}) %collective-permute-start.13) | collective-permute-done | bytes 544800 | tf_op jit(solution)/shard_map/ppermute | solution.py:153
  307.2 2.1 fusion.114
  309.3 2.5 fusion.43
  311.9 2.3 convolution_convert_fusion.3
  314.2 1.9 convolution_convert_fusion.6
  316.4 2.5 copy.66
  318.8 1.7 constant_dynamic-slice_fusion
  323.3 1.9 dynamic-slice_bitcast_fusion.6
  326.6 12.3 %collective-permute-done.15 = bf16[512,896]{1,0:T(8,128)(2,1)S(1)} collective-permute-done((bf16[512,896]{1,0:T(8,128)(2,1)}, bf16[512,896]{1,0:T(8,128)(2,1)S(1)}, u32[]{:S(2)}, u32[]{:S(2)}) %collective-permute-start.15) | collective-permute-done | bytes 917536 | tf_op jit(solution)/shard_map/ppermute | solution.py:103
  338.9 2.5 fusion.58
  341.6 5.0 %concatenate.104 = bf16[8,2,1,56,1152]{4,3,1,0,2:T(8,128)(2,1)} concatenate(bf16[8,2,1,56,576]{4,3,1,0,2:T(8,128)(2,1)} %bitcast.334, bf16[8,2,1,56,448]{4,3,1,0,2:T(8,128)(2,1)} %bitcast.351, bf16[8,2,1,56,128]{4,3,1,0,2:T(8,128)(2,1)S(1)} %broadcast_in_dim.83), dimensions={4} | concatenate | bytes 4128768 | tf_op jit(solution)/shard_map/concatenate | solution.py:389
  348.1 1.8 add_bitcast_fusion
  349.9 1.8 add_bitcast_fusion.2
  354.3 11.9 %collective-permute-done.17 = bf16[4,56,1152]{2,1,0:T(8,128)(2,1)S(1)} collective-permute-done((bf16[4,56,1152]{2,1,0:T(8,128)(2,1)S(1)}, bf16[4,56,1152]{2,1,0:T(8,128)(2,1)S(1)}, u32[]{:S(2)}, u32[]{:S(2)}) %collective-permute-start.17) | collective-permute-done | bytes 516128 | tf_op jit(solution)/shard_map/ppermute | solution.py:153
  366.5 3.4 collective-permute-done.23
  370.8 4.6 %collective-permute-done.18 = bf16[2,56,1152]{2,1,0:T(8,128)(2,1)S(1)} collective-permute-done((bf16[2,56,1152]{2,1,0:T(8,128)(2,1)S(1)}, bf16[2,56,1152]{2,1,0:T(8,128)(2,1)S(1)}, u32[]{:S(2)}, u32[]{:S(2)}) %collective-permute-start.18) | collective-permute-done | bytes 258080 | tf_op jit(solution)/shard_map/ppermute | solution.py:153
  375.8 1.9 fusion.55
  377.7 5.7 %collective-permute-done.19 = bf16[1,56,1152]{2,1,0:T(8,128)(2,1)S(1)} collective-permute-done((bf16[1,56,1152]{2,1,0:T(8,128)(2,1)S(1)}, bf16[1,56,1152]{2,1,0:T(8,128)(2,1)S(1)}, u32[]{:S(2)}, u32[]{:S(2)}) %collective-permute-start.19) | collective-permute-done | bytes 129056 | tf_op jit(solution)/shard_map/ppermute | solution.py:153
  (285 shorter events, 54.6 us)
Async XLA Ops:
  0.6 50.0 %copy-start = (bf16[896,576]{0,1:T(8,128)(2,1)S(1)}, bf16[896,576]{0,1:T(8,128)(2,1)}, u32[]{:S(2)}) copy-start(bf16[896,576]{0,1:T(8,128)(2,1)} %param.29) | copy-start | bytes 3096580
  0.7 47.9 %copy-start.3 = (bf16[512,896]{1,0:T(8,128)(2,1)S(1)}, bf16[512,896]{1,0:T(8,128)(2,1)}, u32[]{:S(2)}) copy-start(bf16[512,896]{1,0:T(8,128)(2,1)} %param.24) | copy-start | bytes 2752516
  0.7 47.9 %copy-start.49 = (f32[896]{0:T(1024)S(1)}, f32[896]{0:T(1024)}, u32[]{:S(2)}) copy-start(f32[896]{0:T(1024)} %param.28) | copy-start | bytes 10756
  0.7 7.6 %copy-start.18 = (bf16[512,896]{1,0:T(8,128)(2,1)S(1)}, bf16[512,896]{1,0:T(8,128)(2,1)}, u32[]{:S(2)}) copy-start(bf16[512,896]{1,0:T(8,128)(2,1)} %param.25) | copy-start | bytes 2752516
  0.7 7.6 %copy-start.59 = (s32[64]{0:T(128)S(1)}, s32[64]{0:T(128)}, u32[]{:S(2)}) copy-start(s32[64]{0:T(128)} %param.27) | copy-start | bytes 772
  0.7 7.6 %copy-start.58 = (s32[64]{0:T(128)S(1)}, s32[64]{0:T(128)}, u32[]{:S(2)}) copy-start(s32[64]{0:T(128)} %param.26) | copy-start | bytes 772
  2.9 47.8 %copy-start.52 = (f32[512]{0:T(512)}, f32[512]{0:T(512)S(1)}, u32[]{:S(2)}) copy-start(f32[512]{0:T(512)S(1)} %get-tuple-element.174) | copy-start | bytes 6148
  5.3 24.5 %collective-permute-start = (bf16[512,896]{1,0:T(8,128)(2,1)}, bf16[512,896]{1,0:T(8,128)(2,1)}, u32[]{:S(2)}, u32[]{:S(2)}) collective-permute-start(bf16[512,896]{1,0:T(8,128)(2,1)} %fusion.52), channel_id=1, source_target_pairs={{0,1},{1,0},{2,3},{3,2},{4,5},{5,4},{6,7},{7,6},{8,9},{9,8},{10,11... | collective-permute-start | bytes 2752520 | tf_op jit(solution)/shard_map/ppermute | solution.py:103
  8.3 40.3 %collective-permute-start.1 = (bf16[512,896]{1,0:T(8,128)(2,1)S(1)}, bf16[512,896]{1,0:T(8,128)(2,1)}, u32[]{:S(2)}, u32[]{:S(2)}) collective-permute-start(bf16[512,896]{1,0:T(8,128)(2,1)S(1)} %copy-done.18), channel_id=1, source_target_pairs={{0,1},{1,0},{2,3},{3,2},{4,5},{5,4},{6,7},{7,6},{8,9},{9,8},{10,11... | collective-permute-start | bytes 2752520 | tf_op jit(solution)/shard_map/ppermute | solution.py:103
  8.3 44.1 %copy-start.56 = (f32[32]{0:T(128)}, f32[32]{0:T(128)S(1)}, u32[]{:S(2)}) copy-start(f32[32]{0:T(128)S(1)} %multiply_power_fusion) | copy-start | bytes 388
  8.9 43.5 %copy-start.46 = (f32[1024]{0:T(1024)}, f32[1024]{0:T(1024)S(1)}, u32[]{:S(2)}) copy-start(f32[1024]{0:T(1024)S(1)} %get-tuple-element.194) | copy-start | bytes 12292
  9.8 43.2 %copy-start.28 = (f32[1024,32]{0,1:T(8,128)}, f32[1024,32]{0,1:T(8,128)S(1)}, u32[]{:S(2)}) copy-start(f32[1024,32]{0,1:T(8,128)S(1)} %get-tuple-element.167) | copy-start | bytes 393220
  9.8 43.2 %copy-start.30 = (f32[1024,32]{0,1:T(8,128)}, f32[1024,32]{0,1:T(8,128)S(1)}, u32[]{:S(2)}) copy-start(f32[1024,32]{0,1:T(8,128)S(1)} %get-tuple-element.168) | copy-start | bytes 393220
  10.5 40.2 %copy-start.60 = (f32[576]{0:T(1024)S(1)}, f32[576]{0:T(1024)}, u32[]{:S(2)}) copy-start(f32[576]{0:T(1024)} %param.30) | copy-start | bytes 6916
  52.1 21.1 %copy-start.51 = (bf16[1024,576]{0,1:T(8,128)(2,1)}, bf16[1024,576]{0,1:T(8,128)(2,1)S(1)}, u32[]{:S(2)}) copy-start(bf16[1024,576]{0,1:T(8,128)(2,1)S(1)} %get-tuple-element.181) | copy-start | bytes 3538948
  53.0 197.5 %copy-start.32 = (bf16[1024,1,32]{0,2,1:T(8,128)(2,1)}, bf16[1024,1,32]{0,2,1:T(8,128)(2,1)S(1)}, u32[]{:S(2)}) copy-start(bf16[1024,1,32]{0,2,1:T(8,128)(2,1)S(1)} %get-tuple-element.163) | copy-start | bytes 196612
  53.0 197.5 %copy-start.34 = (bf16[1024,1,32]{0,2,1:T(8,128)(2,1)}, bf16[1024,1,32]{0,2,1:T(8,128)(2,1)S(1)}, u32[]{:S(2)}) copy-start(bf16[1024,1,32]{0,2,1:T(8,128)(2,1)S(1)} %get-tuple-element.164) | copy-start | bytes 196612
  83.0 21.7 %collective-permute-start.2 = (bf16[512,896]{1,0:T(8,128)(2,1)S(1)}, bf16[512,896]{1,0:T(8,128)(2,1)}, u32[]{:S(2)}, u32[]{:S(2)}) collective-permute-start(bf16[512,896]{1,0:T(8,128)(2,1)S(1)} %convolution_convert_fusion.5), channel_id=1, source_target_pairs={{0,1},{1,0},{2,3},{3,2},{4,5},{5,4},{6,7},{7,6},{8,9},{9,8},{10,11... | collective-permute-start | bytes 2752520 | tf_op jit(solution)/shard_map/ppermute | solution.py:103
  84.9 22.6 %copy-start.48 = (f32[896]{0:T(1024)S(1)}, f32[896]{0:T(1024)}, u32[]{:S(2)}) copy-start(f32[896]{0:T(1024)} %param.32) | copy-start | bytes 10756
  107.5 21.6 %slice-start.6 = ((s8[4358144]{0:T(1024)(128)(4,1)}), s8[4194304]{0:T(1024)(128)(4,1)S(1)}, s32[]{:S(2)}) async-start(s8[4358144]{0:T(1024)(128)(4,1)} %bitcast.367), calls=%async_computation.6 | async-start | bytes 8388608
  107.8 21.3 %slice-start.7 = ((s8[4358144]{0:T(1024)(128)(4,1)}), s8[163840]{0:T(1024)(128)(4,1)S(1)}, s32[]{:S(2)}) async-start(s8[4358144]{0:T(1024)(128)(4,1)} %bitcast.367), calls=%async_computation.7 | async-start | bytes 327680
  107.8 20.7 %collective-permute-start.3 = (bf16[512,896]{1,0:T(8,128)(2,1)S(1)}, bf16[512,896]{1,0:T(8,128)(2,1)S(1)}, u32[]{:S(2)}, u32[]{:S(2)}) collective-permute-start(bf16[512,896]{1,0:T(8,128)(2,1)S(1)} %multiply_convert_fusion.3), channel_id=1, source_target_pairs={{0,1},{1,0},{2,3},{3,2},{4,5},{5,4},{6,7},{7,6},{8,9},{9,8},{10,11... | collective-permute-start | bytes 2752520 | tf_op jit(solution)/shard_map/ppermute | solution.py:103
  156.0 12.4 %slice-start.8 = ((s8[4358144]{0:T(1024)(128)(4,1)}), s8[4194304]{0:T(1024)(128)(4,1)S(1)}, s32[]{:S(2)}) async-start(s8[4358144]{0:T(1024)(128)(4,1)} %bitcast.369), calls=%async_computation.8 | async-start | bytes 8388608
  156.0 12.4 %slice-start.14 = ((s8[4980736]{0:T(1024)(128)(4,1)}), s8[4194304]{0:T(1024)(128)(4,1)S(1)}, s32[]{:S(2)}) async-start(s8[4980736]{0:T(1024)(128)(4,1)} %bitcast.375), calls=%async_computation.14 | async-start | bytes 8388608
  167.2 19.8 %collective-permute-start.4 = (bf16[512,896]{1,0:T(8,128)(2,1)S(1)}, bf16[512,896]{1,0:T(8,128)(2,1)S(1)}, u32[]{:S(2)}, u32[]{:S(2)}) collective-permute-start(bf16[512,896]{1,0:T(8,128)(2,1)S(1)} %add_convert_fusion.1), channel_id=1, source_target_pairs={{0,1},{1,0},{2,3},{3,2},{4,5},{5,4},{6,7},{7,6},{8,9},{9,8},{10,11... | collective-permute-start | bytes 2752520 | tf_op jit(solution)/shard_map/ppermute | solution.py:103
  168.4 8.2 %slice-start.10 = ((s8[4358144]{0:T(1024)(128)(4,1)}), s8[4194304]{0:T(1024)(128)(4,1)S(1)}, s32[]{:S(2)}) async-start(s8[4358144]{0:T(1024)(128)(4,1)} %bitcast.371), calls=%async_computation.10 | async-start | bytes 8388608
  171.3 8.2 %slice-start.16 = ((s8[4980736]{0:T(1024)(128)(4,1)}), s8[4194304]{0:T(1024)(128)(4,1)S(1)}, s32[]{:S(2)}) async-start(s8[4980736]{0:T(1024)(128)(4,1)} %bitcast.377), calls=%async_computation.16 | async-start | bytes 8388608
  188.2 7.4 %slice-start.18 = ((s8[4980736]{0:T(1024)(128)(4,1)}), s8[786432]{0:T(1024)(128)(4,1)S(1)}, s32[]{:S(2)}) async-start(s8[4980736]{0:T(1024)(128)(4,1)} %bitcast.379), calls=%async_computation.18 | async-start | bytes 1572864
  193.9 18.8 %collective-permute-start.5 = (bf16[512,896]{1,0:T(8,128)(2,1)S(1)}, bf16[512,896]{1,0:T(8,128)(2,1)S(1)}, u32[]{:S(2)}, u32[]{:S(2)}) collective-permute-start(bf16[512,896]{1,0:T(8,128)(2,1)S(1)} %get-tuple-element.115), channel_id=1, source_target_pairs={{0,1},{1,0},{2,3},{3,2},{4,5},{5,4},{6,7},{7,6},{8,9},{9,8},{10,11... | collective-permute-start | bytes 2752520 | tf_op jit(solution)/shard_map/ppermute | solution.py:103
  194.8 18.2 %collective-permute-start.6 = (bf16[8,56,2432]{2,1,0:T(8,128)(2,1)S(1)}, bf16[8,56,2432]{2,1,0:T(8,128)(2,1)S(1)}, u32[]{:S(2)}, u32[]{:S(2)}) collective-permute-start(bf16[8,56,2432]{2,1,0:T(8,128)(2,1)S(1)} %dynamic-slice_bitcast_fusion.2), channel_id=1, source_target_pairs={{0,2},{2,0},{4,6},{6,4},{8,10},{10,8},{12,14},{14,12},{16,18},{18,... | collective-permute-start | bytes 6537224 | tf_op jit(solution)/shard_map/ppermute | solution.py:153
  195.1 19.8 %collective-permute-start.7 = (bf16[8,56,2432]{2,1,0:T(8,128)(2,1)S(1)}, bf16[8,56,2432]{2,1,0:T(8,128)(2,1)S(1)}, u32[]{:S(2)}, u32[]{:S(2)}) collective-permute-start(bf16[8,56,2432]{2,1,0:T(8,128)(2,1)S(1)} %dynamic-slice_bitcast_fusion.1), channel_id=1, source_target_pairs={{0,2},{2,0},{4,6},{6,4},{8,10},{10,8},{12,14},{14,12},{16,18},{18,... | collective-permute-start | bytes 6537224 | tf_op jit(solution)/shard_map/ppermute | solution.py:153
  230.4 23.9 %collective-permute-start.11 = (bf16[512,896]{1,0:T(8,128)(2,1)}, bf16[512,896]{1,0:T(8,128)(2,1)S(1)}, u32[]{:S(2)}, u32[]{:S(2)}) collective-permute-start(bf16[512,896]{1,0:T(8,128)(2,1)} %fusion.64), channel_id=1, source_target_pairs={{0,1},{1,0},{2,3},{3,2},{4,5},{5,4},{6,7},{7,6},{8,9},{9,8},{10,11... | collective-permute-start | bytes 2752520 | tf_op jit(solution)/shard_map/ppermute | solution.py:103
  233.2 24.0 %collective-permute-start.9 = (bf16[4,56,2432]{2,1,0:T(8,128)(2,1)}, bf16[4,56,2432]{2,1,0:T(8,128)(2,1)}, u32[]{:S(2)}, u32[]{:S(2)}) collective-permute-start(bf16[4,56,2432]{2,1,0:T(8,128)(2,1)} %dynamic-slice_bitcast_fusion.4), channel_id=1, source_target_pairs={{0,4},{2,6},{4,0},{6,2},{8,12},{10,14},{12,8},{14,10},{16,20},{18,... | collective-permute-start | bytes 3268616 | tf_op jit(solution)/shard_map/ppermute | solution.py:153
  239.5 22.8 %collective-permute-start.10 = (bf16[4,56,2432]{2,1,0:T(8,128)(2,1)}, bf16[4,56,2432]{2,1,0:T(8,128)(2,1)}, u32[]{:S(2)}, u32[]{:S(2)}) collective-permute-start(bf16[4,56,2432]{2,1,0:T(8,128)(2,1)} %bitcast.43), channel_id=1, source_target_pairs={{0,8},{2,10},{4,12},{6,14},{8,0},{10,2},{12,4},{14,6},{16,24},{18,... | collective-permute-start | bytes 3268616 | tf_op jit(solution)/shard_map/ppermute | solution.py:153
  241.1 22.7 %collective-permute-start.8 = (bf16[8,56,2432]{2,1,0:T(8,128)(2,1)}, bf16[8,56,2432]{2,1,0:T(8,128)(2,1)}, u32[]{:S(2)}, u32[]{:S(2)}) collective-permute-start(bf16[8,56,2432]{2,1,0:T(8,128)(2,1)} %dynamic-slice_bitcast_fusion), channel_id=1, source_target_pairs={{0,2},{2,0},{4,6},{6,4},{8,10},{10,8},{12,14},{14,12},{16,18},{18,... | collective-permute-start | bytes 6537224 | tf_op jit(solution)/shard_map/ppermute | solution.py:153
  241.1 25.6 %slice-start = ((s8[14680064]{0:T(1024)(128)(4,1)}), s8[4194304]{0:T(1024)(128)(4,1)S(1)}, s32[]{:S(2)}) async-start(s8[14680064]{0:T(1024)(128)(4,1)} %bitcast.324), calls=%async_computation | async-start | bytes 8388608
  241.1 25.6 %slice-start.1 = ((s8[14680064]{0:T(1024)(128)(4,1)}), s8[2097152]{0:T(1024)(128)(4,1)S(1)}, s32[]{:S(2)}) async-start(s8[14680064]{0:T(1024)(128)(4,1)} %bitcast.324), calls=%async_computation.1 | async-start | bytes 4194304
  250.5 16.2 %slice-start.2 = ((s8[14680064]{0:T(1024)(128)(4,1)}), s8[4194304]{0:T(1024)(128)(4,1)S(1)}, s32[]{:S(2)}) async-start(s8[14680064]{0:T(1024)(128)(4,1)} %bitcast.324), calls=%async_computation.2 | async-start | bytes 8388608
  254.4 7.9 %copy-start.13 = (bf16[2,1,2,56,2432]{4,3,2,1,0:T(8,128)(2,1)S(1)}, bf16[2,1,2,56,2432]{4,3,2,1,0:T(8,128)(2,1)}, u32[]{:S(2)}) copy-start(bf16[2,1,2,56,2432]{4,3,2,1,0:T(8,128)(2,1)} %get-tuple-element.147) | copy-start | bytes 3268612
  257.2 9.5 %slice-start.3 = ((s8[14680064]{0:T(1024)(128)(4,1)}), s8[4194304]{0:T(1024)(128)(4,1)S(1)}, s32[]{:S(2)}) async-start(s8[14680064]{0:T(1024)(128)(4,1)} %bitcast.324), calls=%async_computation.3 | async-start | bytes 8388608
  258.8 19.9 %copy-start.15 = (bf16[4,56,2432]{2,1,0:T(8,128)(2,1)}, bf16[4,56,2432]{2,1,0:T(8,128)(2,1)S(1)}, u32[]{:S(2)}) copy-start(bf16[4,56,2432]{2,1,0:T(8,128)(2,1)S(1)} %fusion.45) | copy-start | bytes 3268612
  266.7 7.8 %copy-start.44 = (f32[512,1,64]{0,2,1:T(8,128)S(1)}, f32[512,1,64]{0,2,1:T(8,128)}, u32[]{:S(2)}) copy-start(f32[512,1,64]{0,2,1:T(8,128)} %fusion.104) | copy-start | bytes 393220
  280.4 26.8 %collective-permute-start.14 = (bf16[2,56,2432]{2,1,0:T(8,128)(2,1)}, bf16[2,56,2432]{2,1,0:T(8,128)(2,1)}, u32[]{:S(2)}, u32[]{:S(2)}) collective-permute-start(bf16[2,56,2432]{2,1,0:T(8,128)(2,1)} %dynamic-slice_bitcast_fusion.7), channel_id=1, source_target_pairs={{0,16},{2,18},{4,20},{6,22},{8,24},{10,26},{12,28},{14,30},{16,0},... | collective-permute-start | bytes 1634312 | tf_op jit(solution)/shard_map/ppermute | solution.py:153
  283.1 23.2 %collective-permute-start.13 = (bf16[2,56,2432]{2,1,0:T(8,128)(2,1)}, bf16[2,56,2432]{2,1,0:T(8,128)(2,1)S(1)}, u32[]{:S(2)}, u32[]{:S(2)}) collective-permute-start(bf16[2,56,2432]{2,1,0:T(8,128)(2,1)} %dynamic-slice_bitcast_fusion.8), channel_id=1, source_target_pairs={{0,8},{2,10},{4,12},{6,14},{8,0},{10,2},{12,4},{14,6},{16,24},{18,... | collective-permute-start | bytes 1634312 | tf_op jit(solution)/shard_map/ppermute | solution.py:153
  284.8 24.6 %collective-permute-start.12 = (bf16[4,56,2432]{2,1,0:T(8,128)(2,1)S(1)}, bf16[4,56,2432]{2,1,0:T(8,128)(2,1)}, u32[]{:S(2)}, u32[]{:S(2)}) collective-permute-start(bf16[4,56,2432]{2,1,0:T(8,128)(2,1)S(1)} %dynamic-slice_bitcast_fusion.3), channel_id=1, source_target_pairs={{0,4},{2,6},{4,0},{6,2},{8,12},{10,14},{12,8},{14,10},{16,20},{18,... | collective-permute-start | bytes 3268616 | tf_op jit(solution)/shard_map/ppermute | solution.py:153
  297.2 9.1 %copy-start.16 = (bf16[4,56,2432]{2,1,0:T(8,128)(2,1)S(1)}, bf16[4,56,2432]{2,1,0:T(8,128)(2,1)}, u32[]{:S(2)}) copy-start(bf16[4,56,2432]{2,1,0:T(8,128)(2,1)} %copy-done.15) | copy-start | bytes 3268612
  316.4 22.6 %copy-start.4 = (bf16[512,896]{1,0:T(8,128)(2,1)S(1)}, bf16[512,896]{1,0:T(8,128)(2,1)}, u32[]{:S(2)}) copy-start(bf16[512,896]{1,0:T(8,128)(2,1)} %param.24) | copy-start | bytes 2752516
  316.4 22.6 %copy-start.50 = (f32[896]{0:T(1024)S(1)}, f32[896]{0:T(1024)}, u32[]{:S(2)}) copy-start(f32[896]{0:T(1024)} %param.28) | copy-start | bytes 10756
  316.4 22.5 %copy-start.53 = (f32[512]{0:T(512)S(1)}, f32[512]{0:T(512)}, u32[]{:S(2)}) copy-start(f32[512]{0:T(512)} %copy-done.52) | copy-start | bytes 6148
  318.8 20.1 %collective-permute-start.15 = (bf16[512,896]{1,0:T(8,128)(2,1)}, bf16[512,896]{1,0:T(8,128)(2,1)S(1)}, u32[]{:S(2)}, u32[]{:S(2)}) collective-permute-start(bf16[512,896]{1,0:T(8,128)(2,1)} %convolution_convert_fusion.6), channel_id=1, source_target_pairs={{0,1},{1,0},{2,3},{3,2},{4,5},{5,4},{6,7},{7,6},{8,9},{9,8},{10,11... | collective-permute-start | bytes 2752520 | tf_op jit(solution)/shard_map/ppermute | solution.py:103
  320.5 27.5 %collective-permute-start.24 = (bf16[1,56,2432]{2,1,0:T(8,128)(2,1)}, bf16[1,56,2432]{2,1,0:T(8,128)(2,1)}, u32[]{:S(2)}, u32[]{:S(2)}) collective-permute-start(bf16[1,56,2432]{2,1,0:T(8,128)(2,1)} %constant_dynamic-slice_fusion), channel_id=1, source_target_pairs={{0,16},{2,18},{4,20},{6,22},{8,24},{10,26},{12,28},{14,30},{16,0},... | collective-permute-start | bytes 817160 | tf_op jit(solution)/shard_map/ppermute | solution.py:153
  322.6 27.3 %collective-permute-start.21 = (bf16[1,56,2432]{2,1,0:T(8,128)(2,1)S(1)}, bf16[1,56,2432]{2,1,0:T(8,128)(2,1)}, u32[]{:S(2)}, u32[]{:S(2)}) collective-permute-start(bf16[1,56,2432]{2,1,0:T(8,128)(2,1)S(1)} %constant_dynamic-slice_fusion.2), channel_id=1, source_target_pairs={{0,4},{2,6},{4,0},{6,2},{8,12},{10,14},{12,8},{14,10},{16,20},{18,... | collective-permute-start | bytes 817160 | tf_op jit(solution)/shard_map/ppermute | solution.py:153
  325.2 16.3 %copy-start.55 = (bf16[896]{0:T(1024)(128)(2,1)S(1)}, bf16[896]{0:T(1024)(128)(2,1)}, u32[]{:S(2)}) copy-start(bf16[896]{0:T(1024)(128)(2,1)} %get-tuple-element.136) | copy-start | bytes 5380
  325.2 27.5 %collective-permute-start.22 = (bf16[2,56,2432]{2,1,0:T(8,128)(2,1)}, bf16[2,56,2432]{2,1,0:T(8,128)(2,1)}, u32[]{:S(2)}, u32[]{:S(2)}) collective-permute-start(bf16[2,56,2432]{2,1,0:T(8,128)(2,1)} %dynamic-slice_bitcast_fusion.6), channel_id=1, source_target_pairs={{0,8},{2,10},{4,12},{6,14},{8,0},{10,2},{12,4},{14,6},{16,24},{18,... | collective-permute-start | bytes 1634312 | tf_op jit(solution)/shard_map/ppermute | solution.py:153
  348.0 3.7 collective-permute-start.16
  352.0 14.2 %collective-permute-start.17 = (bf16[4,56,1152]{2,1,0:T(8,128)(2,1)S(1)}, bf16[4,56,1152]{2,1,0:T(8,128)(2,1)S(1)}, u32[]{:S(2)}, u32[]{:S(2)}) collective-permute-start(bf16[4,56,1152]{2,1,0:T(8,128)(2,1)S(1)} %dynamic-slice_bitcast_fusion.9), channel_id=1, source_target_pairs={{0,4},{2,6},{4,0},{6,2},{8,12},{10,14},{12,8},{14,10},{16,20},{18,... | collective-permute-start | bytes 1548296 | tf_op jit(solution)/shard_map/ppermute | solution.py:153
  354.1 21.7 %copy-start.37 = (bf16[512,896]{1,0:T(8,128)(2,1)S(1)}, bf16[512,896]{1,0:T(8,128)(2,1)}, u32[]{:S(2)}) copy-start(bf16[512,896]{1,0:T(8,128)(2,1)} %copy-done.36) | copy-start | bytes 2752516
  354.2 21.7 %copy-start.12 = (f32[512,896]{1,0:T(8,128)S(1)}, f32[512,896]{1,0:T(8,128)}, u32[]{:S(2)}) copy-start(f32[512,896]{1,0:T(8,128)} %get-tuple-element.143) | copy-start | bytes 5505028
  354.2 21.6 %copy-start.27 = (f32[512,896]{1,0:T(8,128)S(1)}, f32[512,896]{1,0:T(8,128)}, u32[]{:S(2)}) copy-start(f32[512,896]{1,0:T(8,128)} %get-tuple-element.191) | copy-start | bytes 5505028
  354.2 21.6 %copy-start.54 = (f32[512]{0:T(512)S(1)}, f32[512]{0:T(512)}, u32[]{:S(2)}) copy-start(f32[512]{0:T(512)} %get-tuple-element.173) | copy-start | bytes 6148
  354.2 15.7 %collective-permute-start.23 = (bf16[1,56,2432]{2,1,0:T(8,128)(2,1)S(1)}, bf16[1,56,2432]{2,1,0:T(8,128)(2,1)S(1)}, u32[]{:S(2)}, u32[]{:S(2)}) collective-permute-start(bf16[1,56,2432]{2,1,0:T(8,128)(2,1)S(1)} %constant_dynamic-slice_fusion.1), channel_id=1, source_target_pairs={{0,16},{2,18},{4,20},{6,22},{8,24},{10,26},{12,28},{14,30},{16,0},... | collective-permute-start | bytes 817160 | tf_op jit(solution)/shard_map/ppermute | solution.py:153
  366.4 8.9 %collective-permute-start.18 = (bf16[2,56,1152]{2,1,0:T(8,128)(2,1)S(1)}, bf16[2,56,1152]{2,1,0:T(8,128)(2,1)S(1)}, u32[]{:S(2)}, u32[]{:S(2)}) collective-permute-start(bf16[2,56,1152]{2,1,0:T(8,128)(2,1)S(1)} %dynamic-slice_bitcast_fusion.10), channel_id=1, source_target_pairs={{0,8},{2,10},{4,12},{6,14},{8,0},{10,2},{12,4},{14,6},{16,24},{18,... | collective-permute-start | bytes 774152 | tf_op jit(solution)/shard_map/ppermute | solution.py:153
  375.5 8.0 %collective-permute-start.19 = (bf16[1,56,1152]{2,1,0:T(8,128)(2,1)S(1)}, bf16[1,56,1152]{2,1,0:T(8,128)(2,1)S(1)}, u32[]{:S(2)}, u32[]{:S(2)}) collective-permute-start(bf16[1,56,1152]{2,1,0:T(8,128)(2,1)S(1)} %constant_dynamic-slice_fusion.3), channel_id=1, source_target_pairs={{0,16},{2,18},{4,20},{6,22},{8,24},{10,26},{12,28},{14,30},{16,0},... | collective-permute-start | bytes 387080 | tf_op jit(solution)/shard_map/ppermute | solution.py:153
  383.6 3.5 collective-permute-start.20
  (43 other events, 149.5 us)

commit v3 on v2

--- a/solution.py
+++ b/solution.py
@@ -192,8 +192,6 @@
     token_vals = tokens.astype(jnp.float32)
     rms_one, normed_one = rms_forward(token_vals, norm1_gain)
     normed_one = gather_pair(normed_one.astype(jnp.bfloat16))
-    cot_sent, _ = lax.optimization_barrier((cotangent, normed_one))
-    cot_group = gather_pair(cot_sent)
     projected = jnp.dot(normed_one, qkv_weight, preferred_element_type=jnp.float32) + qkv_bias
     query_rows = projected[:, :query_columns].reshape(
         group_rows, kv_local, heads_per_group, HEAD_WIDTH
@@ -245,7 +243,8 @@
     context = (
         jnp.concatenate(contexts, axis=0).reshape(group_rows, query_columns).astype(jnp.bfloat16)
     )
-    context, cot_group = after(context, cot_group)
+    cot_sent, _ = after(cotangent, contexts[0])
+    cot_group = gather_pair(cot_sent)
     hidden_one = token_vals + sum_pair(
         lambda t: jnp.dot(half_rows(context, t), out_weight, preferred_element_type=jnp.float32)
     )

time: 395 us -> 405 us (1.025)
  waiting for transfers between devices: 123 us -> 129 us
    ppermute x9, waiting for transfers between devices: 85.2 us -> 91.5 us  [pair_swap(): return lax.ppermute(block, 'tensor', [(0, 1), (1, 0)])]
    dot_general x8, matrix products: 32.7 us -> 37.2 us  [times_transpose(): lax.dot_general(left, right, (((1,), (1,)), ((), ())), preferred_element_...]
  transfers between devices with their start and end apart: 25 -> 25, of which waited for: 14 -> 13; matrix products, arithmetic and copies ran while one was open for 28% -> 26% of each run, Pallas kernels for 0% -> 0%
where the time goes in v3:
time: 405 us; the launch traced here: 398 us
  matrix products  142 us (35%)
  waiting for transfers between devices  129 us (32%)
  other arithmetic  68.7 us (17%)
  local copies, waits for them, and re-layouts  33 us (8%)
  starting transfers between devices  23.3 us (6%)
    ppermute x9, waiting for transfers between devices, pair_swap(): return lax.ppermute(block, 'tensor', [(0, 1), (1, 0)])  91.5 us
    dot_general x8, matrix products, times_transpose(): lax.dot_general(left, right, (((1,), (1,)), ((), ())), preferred_element_...  37.2 us
    ppermute x16, waiting for transfers between devices, dp_stage(): got = lax.ppermute(sent, 'dp', [(i, i ^ step) for i in range(count)])  37.1 us
    dot_general x5, matrix products, contract_rows(): lax.dot_general(left, right, (((0,), (0,)), ((), ())), preferred_element_...  22.2 us
    dot_general x1, matrix products, shards(): jnp.dot(normed_two, gate_weight, preferred_element_type=jnp.float32)  18.9 us
    convert_element_type x12, other arithmetic, dp_stage(): return total if at == len(bits) - 1 else total.astype(jnp.bfloat16)  17 us
    dot_general x2, matrix products, shards(): jnp.einsum('qjgd,kjd->jgqk', d_block, value_matrix[:row_end], preferred_e...  13 us
    ppermute x9, starting transfers between devices, pair_swap(): return lax.ppermute(block, 'tensor', [(0, 1), (1, 0)])  12.8 us
  transfers between devices with their start and end apart: 25, of which 13 were waited for; matrix products, arithmetic and copies ran while one was open for 26% of the time, Pallas kernels for 0%

profile of v3, /device:TPU:0, one launch (start us, length us, event | category | flops | bytes accessed | tf_op | source)
XLA Modules:
  0.0 398.0 jit_solution(11957594314590833969)
XLA Ops:
  2.9 2.4 fusion.52
  5.3 3.0 collective-permute-start
  10.5 18.3 %collective-permute-done = bf16[512,896]{1,0:T(8,128)(2,1)S(1)} collective-permute-done((bf16[512,896]{1,0:T(8,128)(2,1)}, bf16[512,896]{1,0:T(8,128)(2,1)S(1)}, u32[]{:S(2)}, u32[]{:S(2)}) %collective-permute-start) | collective-permute-done | bytes 917536 | tf_op jit(solution)/shard_map/ppermute | solution.py:103
  34.4 2.0 copy-done.1
  37.7 7.1 %fusion.191 = (f32[7,512]{1,0:T(8,128)S(1)}, f32[1,7,512,1024]{2,3,1,0:T(8,128)}) fusion(bf16[1024,1,7,32]{0,3,2,1:T(8,128)(2,1)S(1)} %get-tuple-element.148, bf16[1024,1,7,32]{0,3,2,1:T(8,128)(2,1)S(1)} %get-tuple-element.147, bf16[1024,32]{0,1:T(8,128)(2,1)S(1)} %bitcast.358, bf16[1024,32]{0,1:T(8,128)(2,1)S(1)} %bitcast.356, ...), kind=kOutput, calls=%fused_computation.288 | convolution fusion | flops 481948160 | bytes 16267264 | tf_op jit(solution)/shard_map/qjgd,kjd->jgqk/dot_general | solution.py:220
  44.8 7.2 %fusion.3 = f32[7,512]{1,0:T(8,128)S(1)} fusion(f32[1,7,512,1024]{2,3,1,0:T(8,128)} %get-tuple-element.176, f32[7,512]{1,0:T(8,128)S(1)} %get-tuple-element.175), kind=kLoop, calls=%fused_computation.9 | loop fusion | flops 7336448 | bytes 14708736 | tf_op jit(solution)/shard_map/reduce_sum | solution.py:231
  51.9 6.7 %fusion.80 = bf16[512,1,7,64]{0,3,2,1:T(8,128)(2,1)S(1)} fusion(f32[7,512]{1,0:T(8,128)S(1)} %fusion.3, f32[1,7,512,1024]{2,3,1,0:T(8,128)} %get-tuple-element.176, f32[7,512]{1,0:T(8,128)S(1)} %get-tuple-element.175, bf16[1024,576]{0,1:T(8,128)(2,1)S(1)} %get-tuple-element.177), kind=kOutput, calls=%fused_computation.123 | convolution fusion | flops 481001472 | bytes 15302656 | tf_op jit(solution)/shard_map/jgqk,kjd->qjgd/dot_general | solution.py:236
  60.4 1.8 collective-permute-start.1
  62.5 21.4 %collective-permute-done.1 = bf16[512,896]{1,0:T(8,128)(2,1)} collective-permute-done((bf16[512,896]{1,0:T(8,128)(2,1)S(1)}, bf16[512,896]{1,0:T(8,128)(2,1)}, u32[]{:S(2)}, u32[]{:S(2)}) %collective-permute-start.1) | collective-permute-done | bytes 917536 | tf_op jit(solution)/shard_map/ppermute | solution.py:103
  83.9 2.7 multiply_reduce_fusion.2
  87.8 1.7 collective-permute-start.2
  89.6 14.0 %collective-permute-done.3 = bf16[512,896]{1,0:T(8,128)(2,1)} collective-permute-done((bf16[512,896]{1,0:T(8,128)(2,1)}, bf16[512,896]{1,0:T(8,128)(2,1)}, u32[]{:S(2)}, u32[]{:S(2)}) %collective-permute-start.3) | collective-permute-done | bytes 917536 | tf_op jit(solution)/shard_map/ppermute | solution.py:103
  103.6 17.9 %collective-permute-done.2 = bf16[512,896]{1,0:T(8,128)(2,1)} collective-permute-done((bf16[512,896]{1,0:T(8,128)(2,1)}, bf16[512,896]{1,0:T(8,128)(2,1)}, u32[]{:S(2)}, u32[]{:S(2)}) %collective-permute-start.2) | collective-permute-done | bytes 917536 | tf_op jit(solution)/shard_map/ppermute | solution.py:103
  121.5 2.3 broadcast_select_fusion.3
  123.9 11.2 %fusion.83 = f32[1024,2432]{1,0:T(8,128)} fusion(bf16[2432,896]{1,0:T(8,128)(2,1)} %param.35, bf16[512,896]{1,0:T(8,128)(2,1)S(1)} %get-tuple-element.152, bf16[512,896]{1,0:T(8,128)(2,1)S(1)} %get-tuple-element.151), kind=kOutput, calls=%fused_computation.124 | convolution fusion | flops 4466409472 | bytes 16154624 | tf_op jit(solution)/shard_map/dot_general | solution.py:97
  135.2 8.0 %fusion.194 = f32[1024,2432]{1,0:T(8,128)} fusion(bf16[1024,896]{1,0:T(8,128)(2,1)S(1)} %pad_maximum_fusion.1, bf16[896,2432]{1,0:T(8,128)(2,1)S(1)} %bitcast.364), kind=kOutput, calls=%fused_computation.291 | convolution fusion | flops 4462739456 | bytes 16154624 | tf_op jit(solution)/shard_map/dot_general | solution.py:255
  143.2 18.9 %multiply_convert_fusion = (bf16[1024,2432]{1,0:T(8,128)(2,1)}, bf16[1024,2432]{1,0:T(8,128)(2,1)}, bf16[1024,2432]{1,0:T(8,128)(2,1)}) fusion(f32[1024,2432]{1,0:T(8,128)} %fusion.83, f32[1024,2432]{1,0:T(8,128)} %fusion.194, bf16[1024,896]{1,0:T(8,128)(2,1)S(1)} %pad_maximum_fusion.1, bf16[896,2432]{1,0:T(8,128)(2,1)} %param.33), kind=kOutput, calls=%fused_computation.11 | convolution fusion | flops 4500094976 | bytes 41058304 | tf_op jit(solution)/shard_map/dot_general | solution.py:254
  162.1 6.0 %fusion.39 = f32[512,896]{1,0:T(8,128)S(1)} fusion(bf16[896,2432]{1,0:T(8,128)(2,1)} %param.34, bf16[1024,2432]{1,0:T(8,128)(2,1)} %get-tuple-element.112, s32[]{:T(128)S(6)} %select_n.219), kind=kOutput, calls=%fused_computation.65 | convolution fusion | flops 2231369728 | bytes 8683524 | tf_op jit(solution)/shard_map/dot_general | solution.py:97
  168.2 5.2 %add_convert_fusion.1 = bf16[512,896]{1,0:T(8,128)(2,1)S(1)} fusion(f32[512,896]{1,0:T(8,128)S(1)} %fusion.39, bf16[896,2432]{1,0:T(8,128)(2,1)} %param.33, bf16[1024,2432]{1,0:T(8,128)(2,1)S(1)} %copy-done.58, s32[]{:T(128)S(6)} %select_n.219), kind=kOutput, calls=%fused_computation.106 | convolution fusion | flops 2232287232 | bytes 9601028 | tf_op jit(solution)/shard_map/dot_general | solution.py:97
  174.9 4.1 %fusion.35 = f32[512,896]{1,0:T(8,128)} fusion(bf16[896,2432]{1,0:T(8,128)(2,1)S(1)} %bitcast.366, bf16[1024,2432]{1,0:T(8,128)(2,1)S(1)} %bitcast.372, s32[]{:T(128)S(6)} %select_n.218), kind=kOutput, calls=%fused_computation.61 | convolution fusion | flops 2231369728 | bytes 8683524 | tf_op jit(solution)/shard_map/dot_general | solution.py:97
  179.0 5.3 %convolution_convert_fusion.1 = bf16[896,2432]{1,0:T(8,128)(2,1)S(1)} fusion(bf16[1024,896]{1,0:T(8,128)(2,1)S(1)} %pad_maximum_fusion.1, bf16[1024,2432]{1,0:T(8,128)(2,1)S(1)} %copy-done.59), kind=kOutput, calls=%fused_computation.34 | convolution fusion | flops 4464918528 | bytes 11173888 | tf_op jit(solution)/shard_map/dot_general | solution.py:91
  184.3 5.2 %fusion.61 = f32[512,896]{1,0:T(8,128)S(1)} fusion(f32[512,896]{1,0:T(8,128)} %fusion.35, bf16[896,2432]{1,0:T(8,128)(2,1)S(1)} %bitcast.368, bf16[1024,2432]{1,0:T(8,128)(2,1)} %get-tuple-element.108, s32[]{:T(128)S(6)} %select_n.218), kind=kOutput, calls=%fused_computation.111 | convolution fusion | flops 2231828480 | bytes 10518532 | tf_op jit(solution)/shard_map/dot_general | solution.py:97
  189.5 5.5 %convolution_convert_fusion.2 = bf16[896,2432]{1,0:T(8,128)(2,1)S(1)} fusion(bf16[1024,2432]{1,0:T(8,128)(2,1)S(1)} %bitcast.374, bf16[512,896]{1,0:T(8,128)(2,1)S(1)} %get-tuple-element.152, bf16[512,896]{1,0:T(8,128)(2,1)S(1)} %get-tuple-element.151), kind=kOutput, calls=%fused_computation.35 | convolution fusion | flops 4468588544 | bytes 11173888 | tf_op jit(solution)/shard_map/dot_general | solution.py:91
  196.2 3.2 fusion.187
  199.4 3.8 fusion.64
  204.8 4.1 %fusion.31 = f32[512,896]{1,0:T(8,128)} fusion(bf16[2432,896]{1,0:T(8,128)(2,1)S(1)} %bitcast.370, bf16[1024,2432]{1,0:T(8,128)(2,1)S(1)} %bitcast.376, s32[]{:T(128)S(6)} %select_n.218), kind=kOutput, calls=%fused_computation.57 | convolution fusion | flops 2231369728 | bytes 8683524 | tf_op jit(solution)/shard_map/dot_general | solution.py:292
  208.8 7.0 %convolution_convert_fusion = bf16[896,2432]{1,0:T(8,128)(2,1)} fusion(bf16[1024,896]{1,0:T(8,128)(2,1)S(1)} %pad_maximum_fusion.1, bf16[1024,2432]{1,0:T(8,128)(2,1)S(1)} %bitcast.372), kind=kOutput, calls=%fused_computation.33 | convolution fusion | flops 4464918528 | bytes 11173888 | tf_op jit(solution)/shard_map/dot_general | solution.py:91
  215.9 7.3 %collective-permute-done.5 = bf16[512,896]{1,0:T(8,128)(2,1)S(1)} collective-permute-done((bf16[512,896]{1,0:T(8,128)(2,1)S(1)}, bf16[512,896]{1,0:T(8,128)(2,1)S(1)}, u32[]{:S(2)}, u32[]{:S(2)}) %collective-permute-start.5) | collective-permute-done | bytes 917536 | tf_op jit(solution)/shard_map/ppermute | solution.py:103
  223.6 1.8 fusion.20
  225.4 1.9 fusion.19
  227.4 2.0 convolution_convert_fusion.7
  231.5 1.9 fusion.102
  233.4 5.2 %fusion.10 = (f32[7,512]{1,0:T(8,128)S(1)}, f32[512,512,7]{1,0,2:T(8,128)}) fusion(f32[1,7,512,512]{2,3,1,0:T(8,128)S(1)} %bitcast.323, f32[7,512]{1,0:T(8,128)S(1)} %log_add_fusion.1, bf16[512,7,64]{0,2,1:T(8,128)(2,1)S(1)} %bitcast.346, bf16[1024,576]{0,1:T(8,128)(2,1)} %copy-done.48), kind=kOutput, calls=%fused_computation.22 | convolution fusion | flops 240382464 | bytes 15233024 | tf_op jit(solution)/shard_map/qjgd,kjd->jgqk/dot_general | solution.py:327
  238.7 2.2 copy.67
  241.8 2.3 dynamic-slice_bitcast_fusion.4
  245.3 3.2 dynamic-slice_bitcast_fusion
  251.7 9.4 %fusion.12 = bf16[1,7,512,512]{2,3,1,0:T(8,128)(2,1)} fusion(f32[512,512,7]{1,0,2:T(8,128)} %get-tuple-element.184, f32[1,7,512,512]{2,3,1,0:T(8,128)} %copy-done.1, f32[7,512]{1,0:T(8,128)S(1)} %get-tuple-element.183, f32[7,512]{1,0:T(8,128)S(1)} %log_add_fusion.1), kind=kLoop, calls=%fused_computation.24 | loop fusion | flops 7340032 | bytes 18378752 | tf_op jit(solution)/shard_map/convert_element_type | solution.py:331
  261.1 3.9 fusion.73
  265.0 2.8 add_convert_fusion
  269.4 3.2 collective-permute-done.10
  274.1 2.9 fusion.18
  277.1 7.8 %fusion = (f32[7,512]{1,0:T(8,128)S(1)}, f32[1024,512,7]{1,0,2:T(8,128)}) fusion(f32[1,7,512,1024]{2,3,1,0:T(8,128)S(1)} %bitcast.321, f32[7,512]{1,0:T(8,128)S(1)} %log_add_fusion, bf16[1024,1,7,64]{0,3,2,1:T(8,128)(2,1)S(1)} %bitcast.349, bf16[1024,576]{0,1:T(8,128)(2,1)} %copy-done.48), kind=kOutput, calls=%fused_computation.3 | convolution fusion | flops 480768512 | bytes 29980672 | tf_op jit(solution)/shard_map/qjgd,kjd->jgqk/dot_general | solution.py:327
  284.9 3.0 fusion.96
  290.8 2.6 collective-permute-start.14
  295.6 7.1 %fusion.9 = bf16[7,512,1024]{1,2,0:T(8,128)(2,1)S(1)} fusion(f32[1024,512,7]{1,0,2:T(8,128)} %get-tuple-element.186, f32[1,7,512,1024]{2,3,1,0:T(8,128)S(1)} %bitcast.321, f32[7,512]{1,0:T(8,128)S(1)} %get-tuple-element.185, f32[7,512]{1,0:T(8,128)S(1)} %log_add_fusion), kind=kLoop, calls=%fused_computation.18 | loop fusion | flops 14680064 | bytes 36728832 | tf_op jit(solution)/shard_map/reshape.221
  304.2 2.3 fusion.89
  308.2 8.7 %collective-permute-done.13 = bf16[2,56,2432]{2,1,0:T(8,128)(2,1)S(1)} collective-permute-done((bf16[2,56,2432]{2,1,0:T(8,128)(2,1)}, bf16[2,56,2432]{2,1,0:T(8,128)(2,1)S(1)}, u32[]{:S(2)}, u32[]{:S(2)}) %collective-permute-start.13) | collective-permute-done | bytes 544800 | tf_op jit(solution)/shard_map/ppermute | solution.py:153
  317.8 2.1 fusion.112
  319.9 2.5 fusion.43
  322.5 2.3 convolution_convert_fusion.3
  324.8 1.9 convolution_convert_fusion.6
  327.0 2.4 copy.66
  331.0 1.7 constant_dynamic-slice_fusion
  334.3 1.9 dynamic-slice_bitcast_fusion.6
  337.0 12.6 %collective-permute-done.15 = bf16[512,896]{1,0:T(8,128)(2,1)S(1)} collective-permute-done((bf16[512,896]{1,0:T(8,128)(2,1)}, bf16[512,896]{1,0:T(8,128)(2,1)S(1)}, u32[]{:S(2)}, u32[]{:S(2)}) %collective-permute-start.15) | collective-permute-done | bytes 917536 | tf_op jit(solution)/shard_map/ppermute | solution.py:103
  349.6 2.5 fusion.58
  352.2 4.9 %concatenate.104 = bf16[8,2,1,56,1152]{4,3,1,0,2:T(8,128)(2,1)} concatenate(bf16[8,2,1,56,576]{4,3,1,0,2:T(8,128)(2,1)} %bitcast.330, bf16[8,2,1,56,448]{4,3,1,0,2:T(8,128)(2,1)} %bitcast.347, bf16[8,2,1,56,128]{4,3,1,0,2:T(8,128)(2,1)S(1)} %broadcast_in_dim.83), dimensions={4} | concatenate | bytes 4128768 | tf_op jit(solution)/shard_map/concatenate | solution.py:388
  358.7 1.8 add_bitcast_fusion
  360.5 1.8 add_bitcast_fusion.2
  364.9 11.9 %collective-permute-done.17 = bf16[4,56,1152]{2,1,0:T(8,128)(2,1)S(1)} collective-permute-done((bf16[4,56,1152]{2,1,0:T(8,128)(2,1)S(1)}, bf16[4,56,1152]{2,1,0:T(8,128)(2,1)S(1)}, u32[]{:S(2)}, u32[]{:S(2)}) %collective-permute-start.17) | collective-permute-done | bytes 516128 | tf_op jit(solution)/shard_map/ppermute | solution.py:153
  377.1 2.6 collective-permute-done.23
  380.6 4.6 %collective-permute-done.18 = bf16[2,56,1152]{2,1,0:T(8,128)(2,1)S(1)} collective-permute-done((bf16[2,56,1152]{2,1,0:T(8,128)(2,1)S(1)}, bf16[2,56,1152]{2,1,0:T(8,128)(2,1)S(1)}, u32[]{:S(2)}, u32[]{:S(2)}) %collective-permute-start.18) | collective-permute-done | bytes 258080 | tf_op jit(solution)/shard_map/ppermute | solution.py:153
  385.5 1.9 fusion.55
  387.4 6.0 %collective-permute-done.19 = bf16[1,56,1152]{2,1,0:T(8,128)(2,1)S(1)} collective-permute-done((bf16[1,56,1152]{2,1,0:T(8,128)(2,1)S(1)}, bf16[1,56,1152]{2,1,0:T(8,128)(2,1)S(1)}, u32[]{:S(2)}, u32[]{:S(2)}) %collective-permute-start.19) | collective-permute-done | bytes 129056 | tf_op jit(solution)/shard_map/ppermute | solution.py:153
  (281 shorter events, 52.7 us)
Async XLA Ops:
  0.6 28.7 %copy-start = (bf16[896,576]{0,1:T(8,128)(2,1)S(1)}, bf16[896,576]{0,1:T(8,128)(2,1)}, u32[]{:S(2)}) copy-start(bf16[896,576]{0,1:T(8,128)(2,1)} %param.29) | copy-start | bytes 3096580
  0.7 28.1 %copy-start.3 = (bf16[512,896]{1,0:T(8,128)(2,1)S(1)}, bf16[512,896]{1,0:T(8,128)(2,1)}, u32[]{:S(2)}) copy-start(bf16[512,896]{1,0:T(8,128)(2,1)} %param.24) | copy-start | bytes 2752516
  0.7 28.1 %copy-start.46 = (f32[896]{0:T(1024)S(1)}, f32[896]{0:T(1024)}, u32[]{:S(2)}) copy-start(f32[896]{0:T(1024)} %param.28) | copy-start | bytes 10756
  0.7 7.6 %copy-start.56 = (s32[64]{0:T(128)S(1)}, s32[64]{0:T(128)}, u32[]{:S(2)}) copy-start(s32[64]{0:T(128)} %param.27) | copy-start | bytes 772
  0.7 7.6 %copy-start.55 = (s32[64]{0:T(128)S(1)}, s32[64]{0:T(128)}, u32[]{:S(2)}) copy-start(s32[64]{0:T(128)} %param.26) | copy-start | bytes 772
  2.9 26.4 %copy-start.49 = (f32[512]{0:T(512)}, f32[512]{0:T(512)S(1)}, u32[]{:S(2)}) copy-start(f32[512]{0:T(512)S(1)} %get-tuple-element.170) | copy-start | bytes 6148
  5.3 23.5 %collective-permute-start = (bf16[512,896]{1,0:T(8,128)(2,1)}, bf16[512,896]{1,0:T(8,128)(2,1)S(1)}, u32[]{:S(2)}, u32[]{:S(2)}) collective-permute-start(bf16[512,896]{1,0:T(8,128)(2,1)} %fusion.52), channel_id=1, source_target_pairs={{0,1},{1,0},{2,3},{3,2},{4,5},{5,4},{6,7},{7,6},{8,9},{9,8},{10,11... | collective-permute-start | bytes 2752520 | tf_op jit(solution)/shard_map/ppermute | solution.py:103
  8.2 22.8 %copy-start.53 = (f32[32]{0:T(128)}, f32[32]{0:T(128)S(1)}, u32[]{:S(2)}) copy-start(f32[32]{0:T(128)S(1)} %multiply_power_fusion) | copy-start | bytes 388
  8.9 22.2 %copy-start.43 = (f32[1024]{0:T(1024)}, f32[1024]{0:T(1024)S(1)}, u32[]{:S(2)}) copy-start(f32[1024]{0:T(1024)S(1)} %subtract_convert_fusion.2) | copy-start | bytes 12292
  9.2 20.2 %copy-start.57 = (f32[576]{0:T(1024)S(1)}, f32[576]{0:T(1024)}, u32[]{:S(2)}) copy-start(f32[576]{0:T(1024)} %param.30) | copy-start | bytes 6916
  9.7 21.9 %copy-start.25 = (f32[1024,32]{0,1:T(8,128)}, f32[1024,32]{0,1:T(8,128)S(1)}, u32[]{:S(2)}) copy-start(f32[1024,32]{0,1:T(8,128)S(1)} %get-tuple-element.163) | copy-start | bytes 393220
  9.7 21.9 %copy-start.27 = (f32[1024,32]{0,1:T(8,128)}, f32[1024,32]{0,1:T(8,128)S(1)}, u32[]{:S(2)}) copy-start(f32[1024,32]{0,1:T(8,128)S(1)} %get-tuple-element.164) | copy-start | bytes 393220
  30.8 21.1 %copy-start.48 = (bf16[1024,576]{0,1:T(8,128)(2,1)}, bf16[1024,576]{0,1:T(8,128)(2,1)S(1)}, u32[]{:S(2)}) copy-start(bf16[1024,576]{0,1:T(8,128)(2,1)S(1)} %get-tuple-element.177) | copy-start | bytes 3538948
  31.6 229.4 %copy-start.29 = (bf16[1024,1,32]{0,2,1:T(8,128)(2,1)}, bf16[1024,1,32]{0,2,1:T(8,128)(2,1)S(1)}, u32[]{:S(2)}) copy-start(bf16[1024,1,32]{0,2,1:T(8,128)(2,1)S(1)} %get-tuple-element.159) | copy-start | bytes 196612
  31.6 229.4 %copy-start.31 = (bf16[1024,1,32]{0,2,1:T(8,128)(2,1)}, bf16[1024,1,32]{0,2,1:T(8,128)(2,1)S(1)}, u32[]{:S(2)}) copy-start(bf16[1024,1,32]{0,2,1:T(8,128)(2,1)S(1)} %get-tuple-element.160) | copy-start | bytes 196612
  51.9 7.8 %copy-start.39 = (bf16[448,896]{1,0:T(8,128)(2,1)S(1)}, bf16[448,896]{1,0:T(8,128)(2,1)}, u32[]{:S(2)}) copy-start(bf16[448,896]{1,0:T(8,128)(2,1)} %param.31) | copy-start | bytes 2408452
  60.4 23.5 %collective-permute-start.1 = (bf16[512,896]{1,0:T(8,128)(2,1)S(1)}, bf16[512,896]{1,0:T(8,128)(2,1)}, u32[]{:S(2)}, u32[]{:S(2)}) collective-permute-start(bf16[512,896]{1,0:T(8,128)(2,1)S(1)} %convolution_convert_fusion.5), channel_id=1, source_target_pairs={{0,1},{1,0},{2,3},{3,2},{4,5},{5,4},{6,7},{7,6},{8,9},{9,8},{10,11... | collective-permute-start | bytes 2752520 | tf_op jit(solution)/shard_map/ppermute | solution.py:103
  62.2 24.4 %copy-start.45 = (f32[896]{0:T(1024)S(1)}, f32[896]{0:T(1024)}, u32[]{:S(2)}) copy-start(f32[896]{0:T(1024)} %param.32) | copy-start | bytes 10756
  62.2 41.3 %collective-permute-start.3 = (bf16[512,896]{1,0:T(8,128)(2,1)}, bf16[512,896]{1,0:T(8,128)(2,1)}, u32[]{:S(2)}, u32[]{:S(2)}) collective-permute-start(bf16[512,896]{1,0:T(8,128)(2,1)} %param.25), channel_id=1, source_target_pairs={{0,1},{1,0},{2,3},{3,2},{4,5},{5,4},{6,7},{7,6},{8,9},{9,8},{10,11... | collective-permute-start | bytes 2752520 | tf_op jit(solution)/shard_map/ppermute | solution.py:103
  87.8 33.7 %collective-permute-start.2 = (bf16[512,896]{1,0:T(8,128)(2,1)}, bf16[512,896]{1,0:T(8,128)(2,1)}, u32[]{:S(2)}, u32[]{:S(2)}) collective-permute-start(bf16[512,896]{1,0:T(8,128)(2,1)} %multiply_convert_fusion.3), channel_id=1, source_target_pairs={{0,1},{1,0},{2,3},{3,2},{4,5},{5,4},{6,7},{7,6},{8,9},{9,8},{10,11... | collective-permute-start | bytes 2752520 | tf_op jit(solution)/shard_map/ppermute | solution.py:103
  123.8 11.4 %slice-start.6 = ((s8[4358144]{0:T(1024)(128)(4,1)}), s8[4194304]{0:T(1024)(128)(4,1)S(1)}, s32[]{:S(2)}) async-start(s8[4358144]{0:T(1024)(128)(4,1)} %bitcast.363), calls=%async_computation.6 | async-start | bytes 8388608
  123.9 11.3 %slice-start.7 = ((s8[4358144]{0:T(1024)(128)(4,1)}), s8[163840]{0:T(1024)(128)(4,1)S(1)}, s32[]{:S(2)}) async-start(s8[4358144]{0:T(1024)(128)(4,1)} %bitcast.363), calls=%async_computation.7 | async-start | bytes 327680
  162.1 12.7 %slice-start.8 = ((s8[4358144]{0:T(1024)(128)(4,1)}), s8[4194304]{0:T(1024)(128)(4,1)S(1)}, s32[]{:S(2)}) async-start(s8[4358144]{0:T(1024)(128)(4,1)} %bitcast.365), calls=%async_computation.8 | async-start | bytes 8388608
  162.1 12.7 %slice-start.14 = ((s8[4980736]{0:T(1024)(128)(4,1)}), s8[4194304]{0:T(1024)(128)(4,1)S(1)}, s32[]{:S(2)}) async-start(s8[4980736]{0:T(1024)(128)(4,1)} %bitcast.371), calls=%async_computation.14 | async-start | bytes 8388608
  173.3 21.7 %collective-permute-start.4 = (bf16[512,896]{1,0:T(8,128)(2,1)S(1)}, bf16[512,896]{1,0:T(8,128)(2,1)S(1)}, u32[]{:S(2)}, u32[]{:S(2)}) collective-permute-start(bf16[512,896]{1,0:T(8,128)(2,1)S(1)} %add_convert_fusion.1), channel_id=1, source_target_pairs={{0,1},{1,0},{2,3},{3,2},{4,5},{5,4},{6,7},{7,6},{8,9},{9,8},{10,11... | collective-permute-start | bytes 2752520 | tf_op jit(solution)/shard_map/ppermute | solution.py:103
  174.9 9.4 %slice-start.10 = ((s8[4358144]{0:T(1024)(128)(4,1)}), s8[4194304]{0:T(1024)(128)(4,1)S(1)}, s32[]{:S(2)}) async-start(s8[4358144]{0:T(1024)(128)(4,1)} %bitcast.367), calls=%async_computation.10 | async-start | bytes 8388608
  179.0 10.5 %slice-start.16 = ((s8[4980736]{0:T(1024)(128)(4,1)}), s8[4194304]{0:T(1024)(128)(4,1)S(1)}, s32[]{:S(2)}) async-start(s8[4980736]{0:T(1024)(128)(4,1)} %bitcast.373), calls=%async_computation.16 | async-start | bytes 8388608
  196.2 8.5 %slice-start.18 = ((s8[4980736]{0:T(1024)(128)(4,1)}), s8[786432]{0:T(1024)(128)(4,1)S(1)}, s32[]{:S(2)}) async-start(s8[4980736]{0:T(1024)(128)(4,1)} %bitcast.375), calls=%async_computation.18 | async-start | bytes 1572864
  203.2 20.0 %collective-permute-start.5 = (bf16[512,896]{1,0:T(8,128)(2,1)S(1)}, bf16[512,896]{1,0:T(8,128)(2,1)S(1)}, u32[]{:S(2)}, u32[]{:S(2)}) collective-permute-start(bf16[512,896]{1,0:T(8,128)(2,1)S(1)} %get-tuple-element.111), channel_id=1, source_target_pairs={{0,1},{1,0},{2,3},{3,2},{4,5},{5,4},{6,7},{7,6},{8,9},{9,8},{10,11... | collective-permute-start | bytes 2752520 | tf_op jit(solution)/shard_map/ppermute | solution.py:103
  203.9 19.6 %collective-permute-start.6 = (bf16[8,56,2432]{2,1,0:T(8,128)(2,1)S(1)}, bf16[8,56,2432]{2,1,0:T(8,128)(2,1)S(1)}, u32[]{:S(2)}, u32[]{:S(2)}) collective-permute-start(bf16[8,56,2432]{2,1,0:T(8,128)(2,1)S(1)} %dynamic-slice_bitcast_fusion.2), channel_id=1, source_target_pairs={{0,2},{2,0},{4,6},{6,4},{8,10},{10,8},{12,14},{14,12},{16,18},{18,... | collective-permute-start | bytes 6537224 | tf_op jit(solution)/shard_map/ppermute | solution.py:153
  204.2 21.2 %collective-permute-start.7 = (bf16[8,56,2432]{2,1,0:T(8,128)(2,1)S(1)}, bf16[8,56,2432]{2,1,0:T(8,128)(2,1)S(1)}, u32[]{:S(2)}, u32[]{:S(2)}) collective-permute-start(bf16[8,56,2432]{2,1,0:T(8,128)(2,1)S(1)} %dynamic-slice_bitcast_fusion.1), channel_id=1, source_target_pairs={{0,2},{2,0},{4,6},{6,4},{8,10},{10,8},{12,14},{14,12},{16,18},{18,... | collective-permute-start | bytes 6537224 | tf_op jit(solution)/shard_map/ppermute | solution.py:153
  240.9 24.0 %collective-permute-start.11 = (bf16[512,896]{1,0:T(8,128)(2,1)}, bf16[512,896]{1,0:T(8,128)(2,1)S(1)}, u32[]{:S(2)}, u32[]{:S(2)}) collective-permute-start(bf16[512,896]{1,0:T(8,128)(2,1)} %fusion.64), channel_id=1, source_target_pairs={{0,1},{1,0},{2,3},{3,2},{4,5},{5,4},{6,7},{7,6},{8,9},{9,8},{10,11... | collective-permute-start | bytes 2752520 | tf_op jit(solution)/shard_map/ppermute | solution.py:103
  244.2 23.6 %collective-permute-start.9 = (bf16[4,56,2432]{2,1,0:T(8,128)(2,1)}, bf16[4,56,2432]{2,1,0:T(8,128)(2,1)}, u32[]{:S(2)}, u32[]{:S(2)}) collective-permute-start(bf16[4,56,2432]{2,1,0:T(8,128)(2,1)} %dynamic-slice_bitcast_fusion.4), channel_id=1, source_target_pairs={{0,4},{2,6},{4,0},{6,2},{8,12},{10,14},{12,8},{14,10},{16,20},{18,... | collective-permute-start | bytes 3268616 | tf_op jit(solution)/shard_map/ppermute | solution.py:153
  250.1 22.6 %collective-permute-start.10 = (bf16[4,56,2432]{2,1,0:T(8,128)(2,1)}, bf16[4,56,2432]{2,1,0:T(8,128)(2,1)}, u32[]{:S(2)}, u32[]{:S(2)}) collective-permute-start(bf16[4,56,2432]{2,1,0:T(8,128)(2,1)} %bitcast.44), channel_id=1, source_target_pairs={{0,8},{2,10},{4,12},{6,14},{8,0},{10,2},{12,4},{14,6},{16,24},{18,... | collective-permute-start | bytes 3268616 | tf_op jit(solution)/shard_map/ppermute | solution.py:153
  251.7 22.4 %collective-permute-start.8 = (bf16[8,56,2432]{2,1,0:T(8,128)(2,1)}, bf16[8,56,2432]{2,1,0:T(8,128)(2,1)}, u32[]{:S(2)}, u32[]{:S(2)}) collective-permute-start(bf16[8,56,2432]{2,1,0:T(8,128)(2,1)} %dynamic-slice_bitcast_fusion), channel_id=1, source_target_pairs={{0,2},{2,0},{4,6},{6,4},{8,10},{10,8},{12,14},{14,12},{16,18},{18,... | collective-permute-start | bytes 6537224 | tf_op jit(solution)/shard_map/ppermute | solution.py:153
  251.7 25.3 %slice-start = ((s8[14680064]{0:T(1024)(128)(4,1)}), s8[4194304]{0:T(1024)(128)(4,1)S(1)}, s32[]{:S(2)}) async-start(s8[14680064]{0:T(1024)(128)(4,1)} %bitcast.320), calls=%async_computation | async-start | bytes 8388608
  251.7 25.3 %slice-start.1 = ((s8[14680064]{0:T(1024)(128)(4,1)}), s8[2097152]{0:T(1024)(128)(4,1)S(1)}, s32[]{:S(2)}) async-start(s8[14680064]{0:T(1024)(128)(4,1)} %bitcast.320), calls=%async_computation.1 | async-start | bytes 4194304
  261.1 16.0 %slice-start.2 = ((s8[14680064]{0:T(1024)(128)(4,1)}), s8[4194304]{0:T(1024)(128)(4,1)S(1)}, s32[]{:S(2)}) async-start(s8[14680064]{0:T(1024)(128)(4,1)} %bitcast.320), calls=%async_computation.2 | async-start | bytes 8388608
  265.0 7.7 %copy-start.13 = (bf16[2,1,2,56,2432]{4,3,2,1,0:T(8,128)(2,1)S(1)}, bf16[2,1,2,56,2432]{4,3,2,1,0:T(8,128)(2,1)}, u32[]{:S(2)}) copy-start(bf16[2,1,2,56,2432]{4,3,2,1,0:T(8,128)(2,1)} %get-tuple-element.143) | copy-start | bytes 3268612
  267.8 9.3 %slice-start.3 = ((s8[14680064]{0:T(1024)(128)(4,1)}), s8[4194304]{0:T(1024)(128)(4,1)S(1)}, s32[]{:S(2)}) async-start(s8[14680064]{0:T(1024)(128)(4,1)} %bitcast.320), calls=%async_computation.3 | async-start | bytes 8388608
  269.4 19.7 %copy-start.15 = (bf16[4,56,2432]{2,1,0:T(8,128)(2,1)}, bf16[4,56,2432]{2,1,0:T(8,128)(2,1)S(1)}, u32[]{:S(2)}) copy-start(bf16[4,56,2432]{2,1,0:T(8,128)(2,1)S(1)} %fusion.45) | copy-start | bytes 3268612
  277.1 7.8 %copy-start.41 = (f32[512,1,64]{0,2,1:T(8,128)S(1)}, f32[512,1,64]{0,2,1:T(8,128)}, u32[]{:S(2)}) copy-start(f32[512,1,64]{0,2,1:T(8,128)} %fusion.102) | copy-start | bytes 393220
  290.8 27.0 %collective-permute-start.14 = (bf16[2,56,2432]{2,1,0:T(8,128)(2,1)}, bf16[2,56,2432]{2,1,0:T(8,128)(2,1)}, u32[]{:S(2)}, u32[]{:S(2)}) collective-permute-start(bf16[2,56,2432]{2,1,0:T(8,128)(2,1)} %dynamic-slice_bitcast_fusion.7), channel_id=1, source_target_pairs={{0,16},{2,18},{4,20},{6,22},{8,24},{10,26},{12,28},{14,30},{16,0},... | collective-permute-start | bytes 1634312 | tf_op jit(solution)/shard_map/ppermute | solution.py:153
  293.4 23.5 %collective-permute-start.13 = (bf16[2,56,2432]{2,1,0:T(8,128)(2,1)}, bf16[2,56,2432]{2,1,0:T(8,128)(2,1)S(1)}, u32[]{:S(2)}, u32[]{:S(2)}) collective-permute-start(bf16[2,56,2432]{2,1,0:T(8,128)(2,1)} %dynamic-slice_bitcast_fusion.8), channel_id=1, source_target_pairs={{0,8},{2,10},{4,12},{6,14},{8,0},{10,2},{12,4},{14,6},{16,24},{18,... | collective-permute-start | bytes 1634312 | tf_op jit(solution)/shard_map/ppermute | solution.py:153
  295.0 24.9 %collective-permute-start.12 = (bf16[4,56,2432]{2,1,0:T(8,128)(2,1)S(1)}, bf16[4,56,2432]{2,1,0:T(8,128)(2,1)}, u32[]{:S(2)}, u32[]{:S(2)}) collective-permute-start(bf16[4,56,2432]{2,1,0:T(8,128)(2,1)S(1)} %dynamic-slice_bitcast_fusion.3), channel_id=1, source_target_pairs={{0,4},{2,6},{4,0},{6,2},{8,12},{10,14},{12,8},{14,10},{16,20},{18,... | collective-permute-start | bytes 3268616 | tf_op jit(solution)/shard_map/ppermute | solution.py:153
  307.5 9.4 %copy-start.16 = (bf16[4,56,2432]{2,1,0:T(8,128)(2,1)S(1)}, bf16[4,56,2432]{2,1,0:T(8,128)(2,1)}, u32[]{:S(2)}) copy-start(bf16[4,56,2432]{2,1,0:T(8,128)(2,1)} %copy-done.15) | copy-start | bytes 3268612
  327.0 22.6 %copy-start.4 = (bf16[512,896]{1,0:T(8,128)(2,1)S(1)}, bf16[512,896]{1,0:T(8,128)(2,1)}, u32[]{:S(2)}) copy-start(bf16[512,896]{1,0:T(8,128)(2,1)} %param.24) | copy-start | bytes 2752516
  327.0 22.6 %copy-start.47 = (f32[896]{0:T(1024)S(1)}, f32[896]{0:T(1024)}, u32[]{:S(2)}) copy-start(f32[896]{0:T(1024)} %param.28) | copy-start | bytes 10756
  327.0 22.6 %copy-start.50 = (f32[512]{0:T(512)S(1)}, f32[512]{0:T(512)}, u32[]{:S(2)}) copy-start(f32[512]{0:T(512)} %copy-done.49) | copy-start | bytes 6148
  329.4 20.1 %collective-permute-start.15 = (bf16[512,896]{1,0:T(8,128)(2,1)}, bf16[512,896]{1,0:T(8,128)(2,1)S(1)}, u32[]{:S(2)}, u32[]{:S(2)}) collective-permute-start(bf16[512,896]{1,0:T(8,128)(2,1)} %convolution_convert_fusion.6), channel_id=1, source_target_pairs={{0,1},{1,0},{2,3},{3,2},{4,5},{5,4},{6,7},{7,6},{8,9},{9,8},{10,11... | collective-permute-start | bytes 2752520 | tf_op jit(solution)/shard_map/ppermute | solution.py:103
  332.6 26.0 %collective-permute-start.24 = (bf16[1,56,2432]{2,1,0:T(8,128)(2,1)}, bf16[1,56,2432]{2,1,0:T(8,128)(2,1)}, u32[]{:S(2)}, u32[]{:S(2)}) collective-permute-start(bf16[1,56,2432]{2,1,0:T(8,128)(2,1)} %constant_dynamic-slice_fusion), channel_id=1, source_target_pairs={{0,16},{2,18},{4,20},{6,22},{8,24},{10,26},{12,28},{14,30},{16,0},... | collective-permute-start | bytes 817160 | tf_op jit(solution)/shard_map/ppermute | solution.py:153
  333.6 26.9 %collective-permute-start.21 = (bf16[1,56,2432]{2,1,0:T(8,128)(2,1)S(1)}, bf16[1,56,2432]{2,1,0:T(8,128)(2,1)}, u32[]{:S(2)}, u32[]{:S(2)}) collective-permute-start(bf16[1,56,2432]{2,1,0:T(8,128)(2,1)S(1)} %constant_dynamic-slice_fusion.2), channel_id=1, source_target_pairs={{0,4},{2,6},{4,0},{6,2},{8,12},{10,14},{12,8},{14,10},{16,20},{18,... | collective-permute-start | bytes 817160 | tf_op jit(solution)/shard_map/ppermute | solution.py:153
  336.2 15.9 %copy-start.52 = (bf16[896]{0:T(1024)(128)(2,1)S(1)}, bf16[896]{0:T(1024)(128)(2,1)}, u32[]{:S(2)}) copy-start(bf16[896]{0:T(1024)(128)(2,1)} %get-tuple-element.132) | copy-start | bytes 5380
  336.2 26.9 %collective-permute-start.22 = (bf16[2,56,2432]{2,1,0:T(8,128)(2,1)}, bf16[2,56,2432]{2,1,0:T(8,128)(2,1)}, u32[]{:S(2)}, u32[]{:S(2)}) collective-permute-start(bf16[2,56,2432]{2,1,0:T(8,128)(2,1)} %dynamic-slice_bitcast_fusion.6), channel_id=1, source_target_pairs={{0,8},{2,10},{4,12},{6,14},{8,0},{10,2},{12,4},{14,6},{16,24},{18,... | collective-permute-start | bytes 1634312 | tf_op jit(solution)/shard_map/ppermute | solution.py:153
  358.6 3.7 collective-permute-start.16
  362.6 14.2 %collective-permute-start.17 = (bf16[4,56,1152]{2,1,0:T(8,128)(2,1)S(1)}, bf16[4,56,1152]{2,1,0:T(8,128)(2,1)S(1)}, u32[]{:S(2)}, u32[]{:S(2)}) collective-permute-start(bf16[4,56,1152]{2,1,0:T(8,128)(2,1)S(1)} %dynamic-slice_bitcast_fusion.9), channel_id=1, source_target_pairs={{0,4},{2,6},{4,0},{6,2},{8,12},{10,14},{12,8},{14,10},{16,20},{18,... | collective-permute-start | bytes 1548296 | tf_op jit(solution)/shard_map/ppermute | solution.py:153
  364.7 20.8 %copy-start.34 = (bf16[512,896]{1,0:T(8,128)(2,1)S(1)}, bf16[512,896]{1,0:T(8,128)(2,1)}, u32[]{:S(2)}) copy-start(bf16[512,896]{1,0:T(8,128)(2,1)} %copy-done.33) | copy-start | bytes 2752516
  364.8 20.7 %copy-start.12 = (f32[512,896]{1,0:T(8,128)S(1)}, f32[512,896]{1,0:T(8,128)}, u32[]{:S(2)}) copy-start(f32[512,896]{1,0:T(8,128)} %get-tuple-element.139) | copy-start | bytes 5505028
  364.8 20.7 %copy-start.24 = (f32[512,896]{1,0:T(8,128)S(1)}, f32[512,896]{1,0:T(8,128)}, u32[]{:S(2)}) copy-start(f32[512,896]{1,0:T(8,128)} %get-tuple-element.187) | copy-start | bytes 5505028
  364.8 20.7 %copy-start.51 = (f32[512]{0:T(512)S(1)}, f32[512]{0:T(512)}, u32[]{:S(2)}) copy-start(f32[512]{0:T(512)} %get-tuple-element.169) | copy-start | bytes 6148
  364.8 14.9 %collective-permute-start.23 = (bf16[1,56,2432]{2,1,0:T(8,128)(2,1)S(1)}, bf16[1,56,2432]{2,1,0:T(8,128)(2,1)S(1)}, u32[]{:S(2)}, u32[]{:S(2)}) collective-permute-start(bf16[1,56,2432]{2,1,0:T(8,128)(2,1)S(1)} %constant_dynamic-slice_fusion.1), channel_id=1, source_target_pairs={{0,16},{2,18},{4,20},{6,22},{8,24},{10,26},{12,28},{14,30},{16,0},... | collective-permute-start | bytes 817160 | tf_op jit(solution)/shard_map/ppermute | solution.py:153
  377.0 8.2 %collective-permute-start.18 = (bf16[2,56,1152]{2,1,0:T(8,128)(2,1)S(1)}, bf16[2,56,1152]{2,1,0:T(8,128)(2,1)S(1)}, u32[]{:S(2)}, u32[]{:S(2)}) collective-permute-start(bf16[2,56,1152]{2,1,0:T(8,128)(2,1)S(1)} %dynamic-slice_bitcast_fusion.10), channel_id=1, source_target_pairs={{0,8},{2,10},{4,12},{6,14},{8,0},{10,2},{12,4},{14,6},{16,24},{18,... | collective-permute-start | bytes 774152 | tf_op jit(solution)/shard_map/ppermute | solution.py:153
  385.3 8.1 %collective-permute-start.19 = (bf16[1,56,1152]{2,1,0:T(8,128)(2,1)S(1)}, bf16[1,56,1152]{2,1,0:T(8,128)(2,1)S(1)}, u32[]{:S(2)}, u32[]{:S(2)}) collective-permute-start(bf16[1,56,1152]{2,1,0:T(8,128)(2,1)S(1)} %constant_dynamic-slice_fusion.3), channel_id=1, source_target_pairs={{0,16},{2,18},{4,20},{6,22},{8,24},{10,26},{12,28},{14,30},{16,0},... | collective-permute-start | bytes 387080 | tf_op jit(solution)/shard_map/ppermute | solution.py:153
  393.6 3.5 collective-permute-start.20
  (41 other events, 151.4 us)
